TPU v7x, 512 devices: a whole 4x4x16 slice. The times are simulated.
512 devices in a mesh: ctx: 16 (over x, z_hi, core), head: 32 (over y, z_lo).
Axes of the slice: x: 4, y: 4, z: 16 (z_hi: 2, z_lo: 8; z = z_hi * 8 + z_lo), core: 2. Of those that a mesh axis runs over, the one named last changes fastest.
Arguments:
- queries: bfloat16 [128, 24576], P('ctx', 'head'), may hold values from -8 to 8
- w_uk: bfloat16 [128, 128, 512], P('head'), may hold values from -0.5 to 0.5
- value_up_weight: bfloat16 [128, 512, 128], P('head'), may hold values from -1 to 1
- w_out: bfloat16 [16384, 7168], P('head', 'ctx'), may hold values from -0.046875 to 0.046875
- kv_cache: bfloat16 [1024, 36864], P('ctx'), may hold values from -8 to 8
- blocks: int32 [128, 32], replicated, may hold values from 0 to 1023, as said below
Outputs:
- attended: bfloat16 [128, 7168], P('head', 'ctx')
Inputs may be any that keep to these rules, and one draw needn't show every extreme that they name: Each row names 32 different blocks; at most 4 of a row's blocks lie in one shard of 64 blocks, and every row has exactly 4 in some shard.
All inputs are finite; a program needn't handle non-finite values.
Results may differ from a plain program's by a relative error of at most 0.011.
Values may be sent and summed in bfloat16 or wider, within the bound.
No kernel may reach another device: no remote copies, remote signals or barrier semaphores. Data moves between devices by JAX's collectives and lax.ppermute only.
A program may use at most 64 MiB of HBM per device.

v0:
```python
import jax
import jax.numpy as jnp
from jax import lax
from jax.sharding import PartitionSpec as P

NEG_FILL = -1e30


def shifted(block, axis, distance):
    devices = range(lax.axis_size(axis))
    route = [((i - distance) % len(devices), i) for i in devices]
    return lax.ppermute(block, axis, route)


def weigh_keys(scores, allowed, project):
    masked = jnp.where(allowed, scores, NEG_FILL)
    row_top = jnp.max(masked, axis=-1)
    weights = jnp.where(allowed, jnp.exp(scores - row_top[..., None]), 0.0).astype(jnp.bfloat16)
    row_total = jnp.sum(weights.astype(jnp.float32), axis=-1)
    return (row_top, row_total, project(weights))


def combine_parts(earlier, later):
    top_one, total_one, accum_one = earlier
    top_two, total_two, accum_two = later
    joined = jnp.maximum(top_one, top_two)
    factor_one = jnp.exp(top_one - joined)
    factor_two = jnp.exp(top_two - joined)
    return (
        joined,
        total_one * factor_one + total_two * factor_two,
        accum_one * factor_one[..., None] + accum_two * factor_two[..., None],
    )


def body(queries, w_uk, value_up_weight, w_out, kv_cache, blocks):
    head_count = w_uk.shape[0]
    nope_width = w_uk.shape[1]
    latent_width = w_uk.shape[2]
    value_width = value_up_weight.shape[2]
    row_count = queries.shape[0]
    qk_width = queries.shape[1] // head_count
    key_width = latent_width + qk_width - nope_width
    local_blocks = kv_cache.shape[0]
    block_span = kv_cache.shape[1] // key_width
    shard_count = lax.axis_size("ctx")
    shard_here = lax.axis_index("ctx")
    scaling = qk_width ** (-0.5)
    value_up_broad = value_up_weight.astype(jnp.float32)
    grouped = queries.reshape(row_count, head_count, qk_width)
    latent_q = jnp.einsum(
        "rhn,hnk->rhk", grouped[:, :, :nope_width], w_uk, preferred_element_type=jnp.float32
    ).astype(jnp.bfloat16)
    absorbed = jnp.concatenate([latent_q, grouped[:, :, nope_width:]], axis=-1)
    flat_keys = kv_cache.reshape(local_blocks * block_span, key_width)
    block_iota = jnp.arange(local_blocks, dtype=jnp.int32)

    def local_part(held_rows, anchor):
        chosen = lax.dynamic_slice_in_dim(blocks, anchor * row_count, row_count, 0)
        offsets = chosen - shard_here * local_blocks
        present = jnp.any(offsets[:, :, None] == block_iota[None, None, :], axis=1)
        allowed = jnp.repeat(present, block_span, axis=1)[:, None, :]
        scores = (
            jnp.einsum("rhc,kc->rhk", held_rows, flat_keys, preferred_element_type=jnp.float32)
            * scaling
        )
        return weigh_keys(
            scores,
            allowed,
            lambda weights: jnp.einsum(
                "rhk,kc->rhc",
                weights,
                flat_keys[:, :latent_width],
                preferred_element_type=jnp.float32,
            ),
        )

    def shard_part(held_rows, anchor):
        parts = local_part(held_rows, anchor)
        return parts

    def pass_queries(held_rows):
        return shifted(held_rows, "ctx", 1)

    last_anchor = (shard_here + 1) % shard_count

    def carry_on(partials):
        return shifted((partials[0], partials[1], partials[2]), "ctx", 1)

    def cycle_turn(cycle_step, carried):
        held_rows, partials = carried
        anchor = (shard_here - cycle_step) % shard_count
        partials = combine_parts(partials, shard_part(held_rows, anchor))
        moved = carry_on(partials)
        return (pass_queries(held_rows), (moved[0], moved[1], moved[2]))

    start_parts = (
        jnp.full((row_count, head_count), NEG_FILL, jnp.float32),
        jnp.zeros((row_count, head_count), jnp.float32),
        jnp.zeros((row_count, head_count, latent_width), jnp.float32),
    )
    held_rows, partials = lax.fori_loop(0, shard_count - 1, cycle_turn, (absorbed, start_parts))
    final_top, final_total, final_accum = carry_on(
        combine_parts(partials, shard_part(held_rows, last_anchor))
    )
    normalized_weights = final_accum / final_total[..., None]
    value_output_rows = jnp.einsum(
        "dng,ngm->dnm", normalized_weights, value_up_broad, precision=lax.Precision.HIGHEST
    ).astype(jnp.bfloat16)
    value_output_rows = value_output_rows.reshape(row_count, head_count * value_width)
    partial_out = jnp.dot(
        lax.all_gather(value_output_rows, "ctx", axis=0, tiled=True),
        w_out,
        preferred_element_type=jnp.float32,
    )
    return lax.psum_scatter(partial_out, "head", scatter_dimension=0, tiled=True).astype(
        jnp.bfloat16
    )


def solution(mesh):
    return jax.shard_map(
        body,
        mesh=mesh,
        in_specs=(
            P("ctx", "head"),
            P("head", None, None),
            P("head", None, None),
            P("head", "ctx"),
            P("ctx", None),
            P(),
        ),
        out_specs=P("head", "ctx"),
        check_vma=False,
    )
```

profile of v0, /device:TPU:2, one launch (start us, length us, event | category | flops | bytes accessed | tf_op | source)
XLA Modules:
  0.0 790.3 jit_solution(11050590960603674276)
XLA Ops:
  0.9 9.9 %reshape.25 = bf16[4096,576]{1,0:T(8,128)(2,1)} reshape(bf16[64,36864]{1,0:T(8,128)(2,1)} %param.12) | data formatting | bytes 9437184 | tf_op jit(solution)/shard_map/reshape | solution.py:55
  11.6 484.8 %while.22 = (s32[]{:T(128)}, bf16[8,4,576]{2,0,1:T(8,128)(2,1)S(1)}, f32[8,4]{0,1:T(4,128)S(1)}, f32[8,4]{0,1:T(4,128)S(1)}, f32[8,4,512]{2,0,1:T(8,128)S(1)}, /...) while((s32[]{:T(128)}, ...), condition=%wide.region_4.5_spmd.clone, body=%wide.region_0.4_spmd.clone.sunk | while | flops 286736256 | bytes 30221176 | solution.py:102
  12.2 4.3 select_reduce_fusion.3
  19.6 15.8 %collective-permute-start = (bf16[8,4,576]{2,0,1:T(8,128)(2,1)S(1)}, bf16[8,4,576]{2,0,1:T(8,128)(2,1)S(1)}, u32[]{:S(2)}, u32[]{:S(2)}) collective-permute-start(bf16[8,4,576]{2,0,1:T(8,128)(2,1)S(1)} %copy.49), channel_id=1, source_target_pairs={{480,0},{0,32},{32,64},{64,96},{96,128},{128,160},{160,192},{192,2... | collective-permute-start | bytes 110600 | tf_op jit(solution)/shard_map/while/body/eval_jaxpr/ppermute | solution.py:12
  39.3 10.7 %collective-permute-done.1 = f32[8,4]{0,1:T(4,128)S(1)} collective-permute-done((f32[8,4]{0,1:T(4,128)S(1)}, f32[8,4]{0,1:T(4,128)S(1)}, u32[]{:S(2)}, u32[]{:S(2)}) %collective-permute-start.1) | collective-permute-done | bytes 160 | tf_op jit(solution)/shard_map/while/body/eval_jaxpr/ppermute | solution.py:12
  52.4 4.3 select_reduce_fusion.3
  64.0 13.4 %collective-permute-start.2 = (f32[8,4]{0,1:T(4,128)S(1)}, f32[8,4]{0,1:T(4,128)S(1)}, u32[]{:S(2)}, u32[]{:S(2)}) collective-permute-start(f32[8,4]{0,1:T(4,128)S(1)} %get-tuple-element.370), channel_id=1, source_target_pairs={{480,0},{0,32},{32,64},{64,96},{96,128},{128,160},{160,192},{192,2... | collective-permute-start | bytes 392 | tf_op jit(solution)/shard_map/while/body/eval_jaxpr/ppermute | solution.py:12
  79.0 4.3 select_reduce_fusion.3
  86.5 12.5 %collective-permute-start = (bf16[8,4,576]{2,0,1:T(8,128)(2,1)S(1)}, bf16[8,4,576]{2,0,1:T(8,128)(2,1)S(1)}, u32[]{:S(2)}, u32[]{:S(2)}) collective-permute-start(bf16[8,4,576]{2,0,1:T(8,128)(2,1)S(1)} %copy.49), channel_id=1, source_target_pairs={{480,0},{0,32},{32,64},{64,96},{96,128},{128,160},{160,192},{192,2... | collective-permute-start | bytes 110600 | tf_op jit(solution)/shard_map/while/body/eval_jaxpr/ppermute | solution.py:12
  103.8 9.7 %collective-permute-done.1 = f32[8,4]{0,1:T(4,128)S(1)} collective-permute-done((f32[8,4]{0,1:T(4,128)S(1)}, f32[8,4]{0,1:T(4,128)S(1)}, u32[]{:S(2)}, u32[]{:S(2)}) %collective-permute-start.1) | collective-permute-done | bytes 160 | tf_op jit(solution)/shard_map/while/body/eval_jaxpr/ppermute | solution.py:12
  115.9 4.3 select_reduce_fusion.3
  127.3 13.4 %collective-permute-start.2 = (f32[8,4]{0,1:T(4,128)S(1)}, f32[8,4]{0,1:T(4,128)S(1)}, u32[]{:S(2)}, u32[]{:S(2)}) collective-permute-start(f32[8,4]{0,1:T(4,128)S(1)} %get-tuple-element.370), channel_id=1, source_target_pairs={{480,0},{0,32},{32,64},{64,96},{96,128},{128,160},{160,192},{192,2... | collective-permute-start | bytes 392 | tf_op jit(solution)/shard_map/while/body/eval_jaxpr/ppermute | solution.py:12
  142.3 4.3 select_reduce_fusion.3
  149.7 12.5 %collective-permute-start = (bf16[8,4,576]{2,0,1:T(8,128)(2,1)S(1)}, bf16[8,4,576]{2,0,1:T(8,128)(2,1)S(1)}, u32[]{:S(2)}, u32[]{:S(2)}) collective-permute-start(bf16[8,4,576]{2,0,1:T(8,128)(2,1)S(1)} %copy.49), channel_id=1, source_target_pairs={{480,0},{0,32},{32,64},{64,96},{96,128},{128,160},{160,192},{192,2... | collective-permute-start | bytes 110600 | tf_op jit(solution)/shard_map/while/body/eval_jaxpr/ppermute | solution.py:12
  164.1 4.2 collective-permute-start.2
  168.4 8.4 %collective-permute-done.1 = f32[8,4]{0,1:T(4,128)S(1)} collective-permute-done((f32[8,4]{0,1:T(4,128)S(1)}, f32[8,4]{0,1:T(4,128)S(1)}, u32[]{:S(2)}, u32[]{:S(2)}) %collective-permute-start.1) | collective-permute-done | bytes 160 | tf_op jit(solution)/shard_map/while/body/eval_jaxpr/ppermute | solution.py:12
  179.2 4.3 select_reduce_fusion.3
  191.8 12.6 %collective-permute-start.2 = (f32[8,4]{0,1:T(4,128)S(1)}, f32[8,4]{0,1:T(4,128)S(1)}, u32[]{:S(2)}, u32[]{:S(2)}) collective-permute-start(f32[8,4]{0,1:T(4,128)S(1)} %get-tuple-element.370), channel_id=1, source_target_pairs={{480,0},{0,32},{32,64},{64,96},{96,128},{128,160},{160,192},{192,2... | collective-permute-start | bytes 392 | tf_op jit(solution)/shard_map/while/body/eval_jaxpr/ppermute | solution.py:12
  206.9 4.3 select_reduce_fusion.3
  214.3 11.7 %collective-permute-start = (bf16[8,4,576]{2,0,1:T(8,128)(2,1)S(1)}, bf16[8,4,576]{2,0,1:T(8,128)(2,1)S(1)}, u32[]{:S(2)}, u32[]{:S(2)}) collective-permute-start(bf16[8,4,576]{2,0,1:T(8,128)(2,1)S(1)} %copy.49), channel_id=1, source_target_pairs={{480,0},{0,32},{32,64},{64,96},{96,128},{128,160},{160,192},{192,2... | collective-permute-start | bytes 110600 | tf_op jit(solution)/shard_map/while/body/eval_jaxpr/ppermute | solution.py:12
  231.9 8.5 %collective-permute-done.1 = f32[8,4]{0,1:T(4,128)S(1)} collective-permute-done((f32[8,4]{0,1:T(4,128)S(1)}, f32[8,4]{0,1:T(4,128)S(1)}, u32[]{:S(2)}, u32[]{:S(2)}) %collective-permute-start.1) | collective-permute-done | bytes 160 | tf_op jit(solution)/shard_map/while/body/eval_jaxpr/ppermute | solution.py:12
  242.9 4.3 select_reduce_fusion.3
  255.4 12.6 %collective-permute-start.2 = (f32[8,4]{0,1:T(4,128)S(1)}, f32[8,4]{0,1:T(4,128)S(1)}, u32[]{:S(2)}, u32[]{:S(2)}) collective-permute-start(f32[8,4]{0,1:T(4,128)S(1)} %get-tuple-element.370), channel_id=1, source_target_pairs={{480,0},{0,32},{32,64},{64,96},{96,128},{128,160},{160,192},{192,2... | collective-permute-start | bytes 392 | tf_op jit(solution)/shard_map/while/body/eval_jaxpr/ppermute | solution.py:12
  270.4 4.3 select_reduce_fusion.3
  277.8 11.7 %collective-permute-start = (bf16[8,4,576]{2,0,1:T(8,128)(2,1)S(1)}, bf16[8,4,576]{2,0,1:T(8,128)(2,1)S(1)}, u32[]{:S(2)}, u32[]{:S(2)}) collective-permute-start(bf16[8,4,576]{2,0,1:T(8,128)(2,1)S(1)} %copy.49), channel_id=1, source_target_pairs={{480,0},{0,32},{32,64},{64,96},{96,128},{128,160},{160,192},{192,2... | collective-permute-start | bytes 110600 | tf_op jit(solution)/shard_map/while/body/eval_jaxpr/ppermute | solution.py:12
  291.4 4.0 collective-permute-start.2
  295.5 8.5 %collective-permute-done.1 = f32[8,4]{0,1:T(4,128)S(1)} collective-permute-done((f32[8,4]{0,1:T(4,128)S(1)}, f32[8,4]{0,1:T(4,128)S(1)}, u32[]{:S(2)}, u32[]{:S(2)}) %collective-permute-start.1) | collective-permute-done | bytes 160 | tf_op jit(solution)/shard_map/while/body/eval_jaxpr/ppermute | solution.py:12
  306.4 4.3 select_reduce_fusion.3
  318.9 12.6 %collective-permute-start.2 = (f32[8,4]{0,1:T(4,128)S(1)}, f32[8,4]{0,1:T(4,128)S(1)}, u32[]{:S(2)}, u32[]{:S(2)}) collective-permute-start(f32[8,4]{0,1:T(4,128)S(1)} %get-tuple-element.370), channel_id=1, source_target_pairs={{480,0},{0,32},{32,64},{64,96},{96,128},{128,160},{160,192},{192,2... | collective-permute-start | bytes 392 | tf_op jit(solution)/shard_map/while/body/eval_jaxpr/ppermute | solution.py:12
  333.9 4.3 select_reduce_fusion.3
  341.4 11.7 %collective-permute-start = (bf16[8,4,576]{2,0,1:T(8,128)(2,1)S(1)}, bf16[8,4,576]{2,0,1:T(8,128)(2,1)S(1)}, u32[]{:S(2)}, u32[]{:S(2)}) collective-permute-start(bf16[8,4,576]{2,0,1:T(8,128)(2,1)S(1)} %copy.49), channel_id=1, source_target_pairs={{480,0},{0,32},{32,64},{64,96},{96,128},{128,160},{160,192},{192,2... | collective-permute-start | bytes 110600 | tf_op jit(solution)/shard_map/while/body/eval_jaxpr/ppermute | solution.py:12
  359.0 8.5 %collective-permute-done.1 = f32[8,4]{0,1:T(4,128)S(1)} collective-permute-done((f32[8,4]{0,1:T(4,128)S(1)}, f32[8,4]{0,1:T(4,128)S(1)}, u32[]{:S(2)}, u32[]{:S(2)}) %collective-permute-start.1) | collective-permute-done | bytes 160 | tf_op jit(solution)/shard_map/while/body/eval_jaxpr/ppermute | solution.py:12
  370.0 4.3 select_reduce_fusion.3
  382.5 12.3 %collective-permute-start.2 = (f32[8,4]{0,1:T(4,128)S(1)}, f32[8,4]{0,1:T(4,128)S(1)}, u32[]{:S(2)}, u32[]{:S(2)}) collective-permute-start(f32[8,4]{0,1:T(4,128)S(1)} %get-tuple-element.370), channel_id=1, source_target_pairs={{480,0},{0,32},{32,64},{64,96},{96,128},{128,160},{160,192},{192,2... | collective-permute-start | bytes 392 | tf_op jit(solution)/shard_map/while/body/eval_jaxpr/ppermute | solution.py:12
  397.5 4.3 select_reduce_fusion.3
  404.9 11.4 %collective-permute-start = (bf16[8,4,576]{2,0,1:T(8,128)(2,1)S(1)}, bf16[8,4,576]{2,0,1:T(8,128)(2,1)S(1)}, u32[]{:S(2)}, u32[]{:S(2)}) collective-permute-start(bf16[8,4,576]{2,0,1:T(8,128)(2,1)S(1)} %copy.49), channel_id=1, source_target_pairs={{480,0},{0,32},{32,64},{64,96},{96,128},{128,160},{160,192},{192,2... | collective-permute-start | bytes 110600 | tf_op jit(solution)/shard_map/while/body/eval_jaxpr/ppermute | solution.py:12
  418.2 4.2 collective-permute-start.2
  422.4 8.4 %collective-permute-done.1 = f32[8,4]{0,1:T(4,128)S(1)} collective-permute-done((f32[8,4]{0,1:T(4,128)S(1)}, f32[8,4]{0,1:T(4,128)S(1)}, u32[]{:S(2)}, u32[]{:S(2)}) %collective-permute-start.1) | collective-permute-done | bytes 160 | tf_op jit(solution)/shard_map/while/body/eval_jaxpr/ppermute | solution.py:12
  433.2 4.3 select_reduce_fusion.3
  445.9 12.6 %collective-permute-start.2 = (f32[8,4]{0,1:T(4,128)S(1)}, f32[8,4]{0,1:T(4,128)S(1)}, u32[]{:S(2)}, u32[]{:S(2)}) collective-permute-start(f32[8,4]{0,1:T(4,128)S(1)} %get-tuple-element.370), channel_id=1, source_target_pairs={{480,0},{0,32},{32,64},{64,96},{96,128},{128,160},{160,192},{192,2... | collective-permute-start | bytes 392 | tf_op jit(solution)/shard_map/while/body/eval_jaxpr/ppermute | solution.py:12
  460.9 4.3 select_reduce_fusion.3
  468.4 11.7 %collective-permute-start = (bf16[8,4,576]{2,0,1:T(8,128)(2,1)S(1)}, bf16[8,4,576]{2,0,1:T(8,128)(2,1)S(1)}, u32[]{:S(2)}, u32[]{:S(2)}) collective-permute-start(bf16[8,4,576]{2,0,1:T(8,128)(2,1)S(1)} %copy.49), channel_id=1, source_target_pairs={{480,0},{0,32},{32,64},{64,96},{96,128},{128,160},{160,192},{192,2... | collective-permute-start | bytes 110600 | tf_op jit(solution)/shard_map/while/body/eval_jaxpr/ppermute | solution.py:12
  482.0 4.0 collective-permute-start.2
  486.0 8.5 %collective-permute-done.1 = f32[8,4]{0,1:T(4,128)S(1)} collective-permute-done((f32[8,4]{0,1:T(4,128)S(1)}, f32[8,4]{0,1:T(4,128)S(1)}, u32[]{:S(2)}, u32[]{:S(2)}) %collective-permute-start.1) | collective-permute-done | bytes 160 | tf_op jit(solution)/shard_map/while/body/eval_jaxpr/ppermute | solution.py:12
  496.5 4.4 select_reduce_fusion.1
  509.0 9.4 %collective-permute-done.5 = f32[8,4]{0,1:T(4,128)S(1)} collective-permute-done((f32[8,4]{0,1:T(4,128)S(1)}, f32[8,4]{0,1:T(4,128)S(1)}, u32[]{:S(2)}, u32[]{:S(2)}) %collective-permute-start.5) | collective-permute-done | bytes 160 | tf_op jit(solution)/shard_map/ppermute | solution.py:12
  518.8 35.0 %all_gather.3 = bf16[128,512]{1,0:T(8,128)(2,1)S(1)} all-gather(bf16[8,512]{1,0:T(8,128)(2,1)S(1)} %fusion.27), channel_id=1, replica_groups=mesh['ctx'=16,'head'=32] {'ctx'}, dimensions={0}, use_global_device_ids=true | all-gather | bytes 139264 | tf_op jit(solution)/shard_map/all_gather | solution.py:112
  554.1 235.6 %all-reduce.2 = bf16[128,448]{1,0:T(8,128)(2,1)S(1)} all-reduce(f32[128,448]{1,0:T(8,128)S(1)} %fusion.37), channel_id=2, replica_groups=mesh['ctx'=16,'head'=32] {'head'}, use_global_device_ids=true, to_apply=%region_8.9.clone | all-reduce | flops 57344 | bytes 344064
  (277 shorter events, 152.6 us)
Async XLA Ops:
  17.7 34.2 %collective-permute-start.3 = (f32[8,4,512]{2,0,1:T(8,128)S(1)}, f32[8,4,512]{2,0,1:T(8,128)S(1)}, u32[]{:S(2)}, u32[]{:S(2)}) collective-permute-start(f32[8,4,512]{2,0,1:T(8,128)S(1)} %fusion.51), channel_id=1, source_target_pairs={{480,0},{0,32},{32,64},{64,96},{96,128},{128,160},{160,192},{192,2... | collective-permute-start | bytes 196616 | tf_op jit(solution)/shard_map/while/body/eval_jaxpr/ppermute | solution.py:12
  19.6 32.3 %collective-permute-start = (bf16[8,4,576]{2,0,1:T(8,128)(2,1)S(1)}, bf16[8,4,576]{2,0,1:T(8,128)(2,1)S(1)}, u32[]{:S(2)}, u32[]{:S(2)}) collective-permute-start(bf16[8,4,576]{2,0,1:T(8,128)(2,1)S(1)} %copy.49), channel_id=1, source_target_pairs={{480,0},{0,32},{32,64},{64,96},{96,128},{128,160},{160,192},{192,2... | collective-permute-start | bytes 110600 | tf_op jit(solution)/shard_map/while/body/eval_jaxpr/ppermute | solution.py:12
  35.4 14.5 %collective-permute-start.1 = (f32[8,4]{0,1:T(4,128)S(1)}, f32[8,4]{0,1:T(4,128)S(1)}, u32[]{:S(2)}, u32[]{:S(2)}) collective-permute-start(f32[8,4]{0,1:T(4,128)S(1)} %get-tuple-element.369), channel_id=1, source_target_pairs={{480,0},{0,32},{32,64},{64,96},{96,128},{128,160},{160,192},{192,2... | collective-permute-start | bytes 392 | tf_op jit(solution)/shard_map/while/body/eval_jaxpr/ppermute | solution.py:12
  37.3 14.5 %collective-permute-start.2 = (f32[8,4]{0,1:T(4,128)S(1)}, f32[8,4]{0,1:T(4,128)S(1)}, u32[]{:S(2)}, u32[]{:S(2)}) collective-permute-start(f32[8,4]{0,1:T(4,128)S(1)} %get-tuple-element.370), channel_id=1, source_target_pairs={{480,0},{0,32},{32,64},{64,96},{96,128},{128,160},{160,192},{192,2... | collective-permute-start | bytes 392 | tf_op jit(solution)/shard_map/while/body/eval_jaxpr/ppermute | solution.py:12
  57.9 20.7 %collective-permute-start.3 = (f32[8,4,512]{2,0,1:T(8,128)S(1)}, f32[8,4,512]{2,0,1:T(8,128)S(1)}, u32[]{:S(2)}, u32[]{:S(2)}) collective-permute-start(f32[8,4,512]{2,0,1:T(8,128)S(1)} %fusion.51), channel_id=1, source_target_pairs={{480,0},{0,32},{32,64},{64,96},{96,128},{128,160},{160,192},{192,2... | collective-permute-start | bytes 196616 | tf_op jit(solution)/shard_map/while/body/eval_jaxpr/ppermute | solution.py:12
  59.8 18.8 %collective-permute-start = (bf16[8,4,576]{2,0,1:T(8,128)(2,1)S(1)}, bf16[8,4,576]{2,0,1:T(8,128)(2,1)S(1)}, u32[]{:S(2)}, u32[]{:S(2)}) collective-permute-start(bf16[8,4,576]{2,0,1:T(8,128)(2,1)S(1)} %copy.49), channel_id=1, source_target_pairs={{480,0},{0,32},{32,64},{64,96},{96,128},{128,160},{160,192},{192,2... | collective-permute-start | bytes 110600 | tf_op jit(solution)/shard_map/while/body/eval_jaxpr/ppermute | solution.py:12
  61.8 15.7 %collective-permute-start.1 = (f32[8,4]{0,1:T(4,128)S(1)}, f32[8,4]{0,1:T(4,128)S(1)}, u32[]{:S(2)}, u32[]{:S(2)}) collective-permute-start(f32[8,4]{0,1:T(4,128)S(1)} %get-tuple-element.369), channel_id=1, source_target_pairs={{480,0},{0,32},{32,64},{64,96},{96,128},{128,160},{160,192},{192,2... | collective-permute-start | bytes 392 | tf_op jit(solution)/shard_map/while/body/eval_jaxpr/ppermute | solution.py:12
  64.0 14.5 %collective-permute-start.2 = (f32[8,4]{0,1:T(4,128)S(1)}, f32[8,4]{0,1:T(4,128)S(1)}, u32[]{:S(2)}, u32[]{:S(2)}) collective-permute-start(f32[8,4]{0,1:T(4,128)S(1)} %get-tuple-element.370), channel_id=1, source_target_pairs={{480,0},{0,32},{32,64},{64,96},{96,128},{128,160},{160,192},{192,2... | collective-permute-start | bytes 392 | tf_op jit(solution)/shard_map/while/body/eval_jaxpr/ppermute | solution.py:12
  84.5 30.9 %collective-permute-start.3 = (f32[8,4,512]{2,0,1:T(8,128)S(1)}, f32[8,4,512]{2,0,1:T(8,128)S(1)}, u32[]{:S(2)}, u32[]{:S(2)}) collective-permute-start(f32[8,4,512]{2,0,1:T(8,128)S(1)} %fusion.51), channel_id=1, source_target_pairs={{480,0},{0,32},{32,64},{64,96},{96,128},{128,160},{160,192},{192,2... | collective-permute-start | bytes 196616 | tf_op jit(solution)/shard_map/while/body/eval_jaxpr/ppermute | solution.py:12
  86.5 28.9 %collective-permute-start = (bf16[8,4,576]{2,0,1:T(8,128)(2,1)S(1)}, bf16[8,4,576]{2,0,1:T(8,128)(2,1)S(1)}, u32[]{:S(2)}, u32[]{:S(2)}) collective-permute-start(bf16[8,4,576]{2,0,1:T(8,128)(2,1)S(1)} %copy.49), channel_id=1, source_target_pairs={{480,0},{0,32},{32,64},{64,96},{96,128},{128,160},{160,192},{192,2... | collective-permute-start | bytes 110600 | tf_op jit(solution)/shard_map/while/body/eval_jaxpr/ppermute | solution.py:12
  99.0 14.5 %collective-permute-start.1 = (f32[8,4]{0,1:T(4,128)S(1)}, f32[8,4]{0,1:T(4,128)S(1)}, u32[]{:S(2)}, u32[]{:S(2)}) collective-permute-start(f32[8,4]{0,1:T(4,128)S(1)} %get-tuple-element.369), channel_id=1, source_target_pairs={{480,0},{0,32},{32,64},{64,96},{96,128},{128,160},{160,192},{192,2... | collective-permute-start | bytes 392 | tf_op jit(solution)/shard_map/while/body/eval_jaxpr/ppermute | solution.py:12
  100.9 14.5 %collective-permute-start.2 = (f32[8,4]{0,1:T(4,128)S(1)}, f32[8,4]{0,1:T(4,128)S(1)}, u32[]{:S(2)}, u32[]{:S(2)}) collective-permute-start(f32[8,4]{0,1:T(4,128)S(1)} %get-tuple-element.370), channel_id=1, source_target_pairs={{480,0},{0,32},{32,64},{64,96},{96,128},{128,160},{160,192},{192,2... | collective-permute-start | bytes 392 | tf_op jit(solution)/shard_map/while/body/eval_jaxpr/ppermute | solution.py:12
  121.4 20.4 %collective-permute-start.3 = (f32[8,4,512]{2,0,1:T(8,128)S(1)}, f32[8,4,512]{2,0,1:T(8,128)S(1)}, u32[]{:S(2)}, u32[]{:S(2)}) collective-permute-start(f32[8,4,512]{2,0,1:T(8,128)S(1)} %fusion.51), channel_id=1, source_target_pairs={{480,0},{0,32},{32,64},{64,96},{96,128},{128,160},{160,192},{192,2... | collective-permute-start | bytes 196616 | tf_op jit(solution)/shard_map/while/body/eval_jaxpr/ppermute | solution.py:12
  123.3 18.5 %collective-permute-start = (bf16[8,4,576]{2,0,1:T(8,128)(2,1)S(1)}, bf16[8,4,576]{2,0,1:T(8,128)(2,1)S(1)}, u32[]{:S(2)}, u32[]{:S(2)}) collective-permute-start(bf16[8,4,576]{2,0,1:T(8,128)(2,1)S(1)} %copy.49), channel_id=1, source_target_pairs={{480,0},{0,32},{32,64},{64,96},{96,128},{128,160},{160,192},{192,2... | collective-permute-start | bytes 110600 | tf_op jit(solution)/shard_map/while/body/eval_jaxpr/ppermute | solution.py:12
  125.4 15.3 %collective-permute-start.1 = (f32[8,4]{0,1:T(4,128)S(1)}, f32[8,4]{0,1:T(4,128)S(1)}, u32[]{:S(2)}, u32[]{:S(2)}) collective-permute-start(f32[8,4]{0,1:T(4,128)S(1)} %get-tuple-element.369), channel_id=1, source_target_pairs={{480,0},{0,32},{32,64},{64,96},{96,128},{128,160},{160,192},{192,2... | collective-permute-start | bytes 392 | tf_op jit(solution)/shard_map/while/body/eval_jaxpr/ppermute | solution.py:12
  127.3 14.5 %collective-permute-start.2 = (f32[8,4]{0,1:T(4,128)S(1)}, f32[8,4]{0,1:T(4,128)S(1)}, u32[]{:S(2)}, u32[]{:S(2)}) collective-permute-start(f32[8,4]{0,1:T(4,128)S(1)} %get-tuple-element.370), channel_id=1, source_target_pairs={{480,0},{0,32},{32,64},{64,96},{96,128},{128,160},{160,192},{192,2... | collective-permute-start | bytes 392 | tf_op jit(solution)/shard_map/while/body/eval_jaxpr/ppermute | solution.py:12
  147.8 30.9 %collective-permute-start.3 = (f32[8,4,512]{2,0,1:T(8,128)S(1)}, f32[8,4,512]{2,0,1:T(8,128)S(1)}, u32[]{:S(2)}, u32[]{:S(2)}) collective-permute-start(f32[8,4,512]{2,0,1:T(8,128)S(1)} %fusion.51), channel_id=1, source_target_pairs={{480,0},{0,32},{32,64},{64,96},{96,128},{128,160},{160,192},{192,2... | collective-permute-start | bytes 196616 | tf_op jit(solution)/shard_map/while/body/eval_jaxpr/ppermute | solution.py:12
  149.7 28.9 %collective-permute-start = (bf16[8,4,576]{2,0,1:T(8,128)(2,1)S(1)}, bf16[8,4,576]{2,0,1:T(8,128)(2,1)S(1)}, u32[]{:S(2)}, u32[]{:S(2)}) collective-permute-start(bf16[8,4,576]{2,0,1:T(8,128)(2,1)S(1)} %copy.49), channel_id=1, source_target_pairs={{480,0},{0,32},{32,64},{64,96},{96,128},{128,160},{160,192},{192,2... | collective-permute-start | bytes 110600 | tf_op jit(solution)/shard_map/while/body/eval_jaxpr/ppermute | solution.py:12
  162.2 14.5 %collective-permute-start.1 = (f32[8,4]{0,1:T(4,128)S(1)}, f32[8,4]{0,1:T(4,128)S(1)}, u32[]{:S(2)}, u32[]{:S(2)}) collective-permute-start(f32[8,4]{0,1:T(4,128)S(1)} %get-tuple-element.369), channel_id=1, source_target_pairs={{480,0},{0,32},{32,64},{64,96},{96,128},{128,160},{160,192},{192,2... | collective-permute-start | bytes 392 | tf_op jit(solution)/shard_map/while/body/eval_jaxpr/ppermute | solution.py:12
  164.1 14.5 %collective-permute-start.2 = (f32[8,4]{0,1:T(4,128)S(1)}, f32[8,4]{0,1:T(4,128)S(1)}, u32[]{:S(2)}, u32[]{:S(2)}) collective-permute-start(f32[8,4]{0,1:T(4,128)S(1)} %get-tuple-element.370), channel_id=1, source_target_pairs={{480,0},{0,32},{32,64},{64,96},{96,128},{128,160},{160,192},{192,2... | collective-permute-start | bytes 392 | tf_op jit(solution)/shard_map/while/body/eval_jaxpr/ppermute | solution.py:12
  184.6 21.7 %collective-permute-start.3 = (f32[8,4,512]{2,0,1:T(8,128)S(1)}, f32[8,4,512]{2,0,1:T(8,128)S(1)}, u32[]{:S(2)}, u32[]{:S(2)}) collective-permute-start(f32[8,4,512]{2,0,1:T(8,128)S(1)} %fusion.51), channel_id=1, source_target_pairs={{480,0},{0,32},{32,64},{64,96},{96,128},{128,160},{160,192},{192,2... | collective-permute-start | bytes 196616 | tf_op jit(solution)/shard_map/while/body/eval_jaxpr/ppermute | solution.py:12
  186.6 19.8 %collective-permute-start = (bf16[8,4,576]{2,0,1:T(8,128)(2,1)S(1)}, bf16[8,4,576]{2,0,1:T(8,128)(2,1)S(1)}, u32[]{:S(2)}, u32[]{:S(2)}) collective-permute-start(bf16[8,4,576]{2,0,1:T(8,128)(2,1)S(1)} %copy.49), channel_id=1, source_target_pairs={{480,0},{0,32},{32,64},{64,96},{96,128},{128,160},{160,192},{192,2... | collective-permute-start | bytes 110600 | tf_op jit(solution)/shard_map/while/body/eval_jaxpr/ppermute | solution.py:12
  189.9 14.5 %collective-permute-start.1 = (f32[8,4]{0,1:T(4,128)S(1)}, f32[8,4]{0,1:T(4,128)S(1)}, u32[]{:S(2)}, u32[]{:S(2)}) collective-permute-start(f32[8,4]{0,1:T(4,128)S(1)} %get-tuple-element.369), channel_id=1, source_target_pairs={{480,0},{0,32},{32,64},{64,96},{96,128},{128,160},{160,192},{192,2... | collective-permute-start | bytes 392 | tf_op jit(solution)/shard_map/while/body/eval_jaxpr/ppermute | solution.py:12
  191.8 14.5 %collective-permute-start.2 = (f32[8,4]{0,1:T(4,128)S(1)}, f32[8,4]{0,1:T(4,128)S(1)}, u32[]{:S(2)}, u32[]{:S(2)}) collective-permute-start(f32[8,4]{0,1:T(4,128)S(1)} %get-tuple-element.370), channel_id=1, source_target_pairs={{480,0},{0,32},{32,64},{64,96},{96,128},{128,160},{160,192},{192,2... | collective-permute-start | bytes 392 | tf_op jit(solution)/shard_map/while/body/eval_jaxpr/ppermute | solution.py:12
  212.4 30.1 %collective-permute-start.3 = (f32[8,4,512]{2,0,1:T(8,128)S(1)}, f32[8,4,512]{2,0,1:T(8,128)S(1)}, u32[]{:S(2)}, u32[]{:S(2)}) collective-permute-start(f32[8,4,512]{2,0,1:T(8,128)S(1)} %fusion.51), channel_id=1, source_target_pairs={{480,0},{0,32},{32,64},{64,96},{96,128},{128,160},{160,192},{192,2... | collective-permute-start | bytes 196616 | tf_op jit(solution)/shard_map/while/body/eval_jaxpr/ppermute | solution.py:12
  214.3 28.1 %collective-permute-start = (bf16[8,4,576]{2,0,1:T(8,128)(2,1)S(1)}, bf16[8,4,576]{2,0,1:T(8,128)(2,1)S(1)}, u32[]{:S(2)}, u32[]{:S(2)}) collective-permute-start(bf16[8,4,576]{2,0,1:T(8,128)(2,1)S(1)} %copy.49), channel_id=1, source_target_pairs={{480,0},{0,32},{32,64},{64,96},{96,128},{128,160},{160,192},{192,2... | collective-permute-start | bytes 110600 | tf_op jit(solution)/shard_map/while/body/eval_jaxpr/ppermute | solution.py:12
  226.0 14.5 %collective-permute-start.1 = (f32[8,4]{0,1:T(4,128)S(1)}, f32[8,4]{0,1:T(4,128)S(1)}, u32[]{:S(2)}, u32[]{:S(2)}) collective-permute-start(f32[8,4]{0,1:T(4,128)S(1)} %get-tuple-element.369), channel_id=1, source_target_pairs={{480,0},{0,32},{32,64},{64,96},{96,128},{128,160},{160,192},{192,2... | collective-permute-start | bytes 392 | tf_op jit(solution)/shard_map/while/body/eval_jaxpr/ppermute | solution.py:12
  227.9 14.5 %collective-permute-start.2 = (f32[8,4]{0,1:T(4,128)S(1)}, f32[8,4]{0,1:T(4,128)S(1)}, u32[]{:S(2)}, u32[]{:S(2)}) collective-permute-start(f32[8,4]{0,1:T(4,128)S(1)} %get-tuple-element.370), channel_id=1, source_target_pairs={{480,0},{0,32},{32,64},{64,96},{96,128},{128,160},{160,192},{192,2... | collective-permute-start | bytes 392 | tf_op jit(solution)/shard_map/while/body/eval_jaxpr/ppermute | solution.py:12
  248.4 21.5 %collective-permute-start.3 = (f32[8,4,512]{2,0,1:T(8,128)S(1)}, f32[8,4,512]{2,0,1:T(8,128)S(1)}, u32[]{:S(2)}, u32[]{:S(2)}) collective-permute-start(f32[8,4,512]{2,0,1:T(8,128)S(1)} %fusion.51), channel_id=1, source_target_pairs={{480,0},{0,32},{32,64},{64,96},{96,128},{128,160},{160,192},{192,2... | collective-permute-start | bytes 196616 | tf_op jit(solution)/shard_map/while/body/eval_jaxpr/ppermute | solution.py:12
  250.3 19.6 %collective-permute-start = (bf16[8,4,576]{2,0,1:T(8,128)(2,1)S(1)}, bf16[8,4,576]{2,0,1:T(8,128)(2,1)S(1)}, u32[]{:S(2)}, u32[]{:S(2)}) collective-permute-start(bf16[8,4,576]{2,0,1:T(8,128)(2,1)S(1)} %copy.49), channel_id=1, source_target_pairs={{480,0},{0,32},{32,64},{64,96},{96,128},{128,160},{160,192},{192,2... | collective-permute-start | bytes 110600 | tf_op jit(solution)/shard_map/while/body/eval_jaxpr/ppermute | solution.py:12
  275.9 30.0 %collective-permute-start.3 = (f32[8,4,512]{2,0,1:T(8,128)S(1)}, f32[8,4,512]{2,0,1:T(8,128)S(1)}, u32[]{:S(2)}, u32[]{:S(2)}) collective-permute-start(f32[8,4,512]{2,0,1:T(8,128)S(1)} %fusion.51), channel_id=1, source_target_pairs={{480,0},{0,32},{32,64},{64,96},{96,128},{128,160},{160,192},{192,2... | collective-permute-start | bytes 196616 | tf_op jit(solution)/shard_map/while/body/eval_jaxpr/ppermute | solution.py:12
  277.8 28.1 %collective-permute-start = (bf16[8,4,576]{2,0,1:T(8,128)(2,1)S(1)}, bf16[8,4,576]{2,0,1:T(8,128)(2,1)S(1)}, u32[]{:S(2)}, u32[]{:S(2)}) collective-permute-start(bf16[8,4,576]{2,0,1:T(8,128)(2,1)S(1)} %copy.49), channel_id=1, source_target_pairs={{480,0},{0,32},{32,64},{64,96},{96,128},{128,160},{160,192},{192,2... | collective-permute-start | bytes 110600 | tf_op jit(solution)/shard_map/while/body/eval_jaxpr/ppermute | solution.py:12
  289.5 14.5 %collective-permute-start.1 = (f32[8,4]{0,1:T(4,128)S(1)}, f32[8,4]{0,1:T(4,128)S(1)}, u32[]{:S(2)}, u32[]{:S(2)}) collective-permute-start(f32[8,4]{0,1:T(4,128)S(1)} %get-tuple-element.369), channel_id=1, source_target_pairs={{480,0},{0,32},{32,64},{64,96},{96,128},{128,160},{160,192},{192,2... | collective-permute-start | bytes 392 | tf_op jit(solution)/shard_map/while/body/eval_jaxpr/ppermute | solution.py:12
  291.4 14.5 %collective-permute-start.2 = (f32[8,4]{0,1:T(4,128)S(1)}, f32[8,4]{0,1:T(4,128)S(1)}, u32[]{:S(2)}, u32[]{:S(2)}) collective-permute-start(f32[8,4]{0,1:T(4,128)S(1)} %get-tuple-element.370), channel_id=1, source_target_pairs={{480,0},{0,32},{32,64},{64,96},{96,128},{128,160},{160,192},{192,2... | collective-permute-start | bytes 392 | tf_op jit(solution)/shard_map/while/body/eval_jaxpr/ppermute | solution.py:12
  311.9 21.5 %collective-permute-start.3 = (f32[8,4,512]{2,0,1:T(8,128)S(1)}, f32[8,4,512]{2,0,1:T(8,128)S(1)}, u32[]{:S(2)}, u32[]{:S(2)}) collective-permute-start(f32[8,4,512]{2,0,1:T(8,128)S(1)} %fusion.51), channel_id=1, source_target_pairs={{480,0},{0,32},{32,64},{64,96},{96,128},{128,160},{160,192},{192,2... | collective-permute-start | bytes 196616 | tf_op jit(solution)/shard_map/while/body/eval_jaxpr/ppermute | solution.py:12
  313.9 19.6 %collective-permute-start = (bf16[8,4,576]{2,0,1:T(8,128)(2,1)S(1)}, bf16[8,4,576]{2,0,1:T(8,128)(2,1)S(1)}, u32[]{:S(2)}, u32[]{:S(2)}) collective-permute-start(bf16[8,4,576]{2,0,1:T(8,128)(2,1)S(1)} %copy.49), channel_id=1, source_target_pairs={{480,0},{0,32},{32,64},{64,96},{96,128},{128,160},{160,192},{192,2... | collective-permute-start | bytes 110600 | tf_op jit(solution)/shard_map/while/body/eval_jaxpr/ppermute | solution.py:12
  318.9 14.5 %collective-permute-start.2 = (f32[8,4]{0,1:T(4,128)S(1)}, f32[8,4]{0,1:T(4,128)S(1)}, u32[]{:S(2)}, u32[]{:S(2)}) collective-permute-start(f32[8,4]{0,1:T(4,128)S(1)} %get-tuple-element.370), channel_id=1, source_target_pairs={{480,0},{0,32},{32,64},{64,96},{96,128},{128,160},{160,192},{192,2... | collective-permute-start | bytes 392 | tf_op jit(solution)/shard_map/while/body/eval_jaxpr/ppermute | solution.py:12
  339.4 30.0 %collective-permute-start.3 = (f32[8,4,512]{2,0,1:T(8,128)S(1)}, f32[8,4,512]{2,0,1:T(8,128)S(1)}, u32[]{:S(2)}, u32[]{:S(2)}) collective-permute-start(f32[8,4,512]{2,0,1:T(8,128)S(1)} %fusion.51), channel_id=1, source_target_pairs={{480,0},{0,32},{32,64},{64,96},{96,128},{128,160},{160,192},{192,2... | collective-permute-start | bytes 196616 | tf_op jit(solution)/shard_map/while/body/eval_jaxpr/ppermute | solution.py:12
  341.4 28.1 %collective-permute-start = (bf16[8,4,576]{2,0,1:T(8,128)(2,1)S(1)}, bf16[8,4,576]{2,0,1:T(8,128)(2,1)S(1)}, u32[]{:S(2)}, u32[]{:S(2)}) collective-permute-start(bf16[8,4,576]{2,0,1:T(8,128)(2,1)S(1)} %copy.49), channel_id=1, source_target_pairs={{480,0},{0,32},{32,64},{64,96},{96,128},{128,160},{160,192},{192,2... | collective-permute-start | bytes 110600 | tf_op jit(solution)/shard_map/while/body/eval_jaxpr/ppermute | solution.py:12
  375.5 21.5 %collective-permute-start.3 = (f32[8,4,512]{2,0,1:T(8,128)S(1)}, f32[8,4,512]{2,0,1:T(8,128)S(1)}, u32[]{:S(2)}, u32[]{:S(2)}) collective-permute-start(f32[8,4,512]{2,0,1:T(8,128)S(1)} %fusion.51), channel_id=1, source_target_pairs={{480,0},{0,32},{32,64},{64,96},{96,128},{128,160},{160,192},{192,2... | collective-permute-start | bytes 196616 | tf_op jit(solution)/shard_map/while/body/eval_jaxpr/ppermute | solution.py:12
  377.4 19.6 %collective-permute-start = (bf16[8,4,576]{2,0,1:T(8,128)(2,1)S(1)}, bf16[8,4,576]{2,0,1:T(8,128)(2,1)S(1)}, u32[]{:S(2)}, u32[]{:S(2)}) collective-permute-start(bf16[8,4,576]{2,0,1:T(8,128)(2,1)S(1)} %copy.49), channel_id=1, source_target_pairs={{480,0},{0,32},{32,64},{64,96},{96,128},{128,160},{160,192},{192,2... | collective-permute-start | bytes 110600 | tf_op jit(solution)/shard_map/while/body/eval_jaxpr/ppermute | solution.py:12
  403.0 29.8 %collective-permute-start.3 = (f32[8,4,512]{2,0,1:T(8,128)S(1)}, f32[8,4,512]{2,0,1:T(8,128)S(1)}, u32[]{:S(2)}, u32[]{:S(2)}) collective-permute-start(f32[8,4,512]{2,0,1:T(8,128)S(1)} %fusion.51), channel_id=1, source_target_pairs={{480,0},{0,32},{32,64},{64,96},{96,128},{128,160},{160,192},{192,2... | collective-permute-start | bytes 196616 | tf_op jit(solution)/shard_map/while/body/eval_jaxpr/ppermute | solution.py:12
  404.9 27.8 %collective-permute-start = (bf16[8,4,576]{2,0,1:T(8,128)(2,1)S(1)}, bf16[8,4,576]{2,0,1:T(8,128)(2,1)S(1)}, u32[]{:S(2)}, u32[]{:S(2)}) collective-permute-start(bf16[8,4,576]{2,0,1:T(8,128)(2,1)S(1)} %copy.49), channel_id=1, source_target_pairs={{480,0},{0,32},{32,64},{64,96},{96,128},{128,160},{160,192},{192,2... | collective-permute-start | bytes 110600 | tf_op jit(solution)/shard_map/while/body/eval_jaxpr/ppermute | solution.py:12
  438.7 21.7 %collective-permute-start.3 = (f32[8,4,512]{2,0,1:T(8,128)S(1)}, f32[8,4,512]{2,0,1:T(8,128)S(1)}, u32[]{:S(2)}, u32[]{:S(2)}) collective-permute-start(f32[8,4,512]{2,0,1:T(8,128)S(1)} %fusion.51), channel_id=1, source_target_pairs={{480,0},{0,32},{32,64},{64,96},{96,128},{128,160},{160,192},{192,2... | collective-permute-start | bytes 196616 | tf_op jit(solution)/shard_map/while/body/eval_jaxpr/ppermute | solution.py:12
  440.7 19.8 %collective-permute-start = (bf16[8,4,576]{2,0,1:T(8,128)(2,1)S(1)}, bf16[8,4,576]{2,0,1:T(8,128)(2,1)S(1)}, u32[]{:S(2)}, u32[]{:S(2)}) collective-permute-start(bf16[8,4,576]{2,0,1:T(8,128)(2,1)S(1)} %copy.49), channel_id=1, source_target_pairs={{480,0},{0,32},{32,64},{64,96},{96,128},{128,160},{160,192},{192,2... | collective-permute-start | bytes 110600 | tf_op jit(solution)/shard_map/while/body/eval_jaxpr/ppermute | solution.py:12
  466.4 30.1 %collective-permute-start.3 = (f32[8,4,512]{2,0,1:T(8,128)S(1)}, f32[8,4,512]{2,0,1:T(8,128)S(1)}, u32[]{:S(2)}, u32[]{:S(2)}) collective-permute-start(f32[8,4,512]{2,0,1:T(8,128)S(1)} %fusion.51), channel_id=1, source_target_pairs={{480,0},{0,32},{32,64},{64,96},{96,128},{128,160},{160,192},{192,2... | collective-permute-start | bytes 196616 | tf_op jit(solution)/shard_map/while/body/eval_jaxpr/ppermute | solution.py:12
  468.4 28.1 %collective-permute-start = (bf16[8,4,576]{2,0,1:T(8,128)(2,1)S(1)}, bf16[8,4,576]{2,0,1:T(8,128)(2,1)S(1)}, u32[]{:S(2)}, u32[]{:S(2)}) collective-permute-start(bf16[8,4,576]{2,0,1:T(8,128)(2,1)S(1)} %copy.49), channel_id=1, source_target_pairs={{480,0},{0,32},{32,64},{64,96},{96,128},{128,160},{160,192},{192,2... | collective-permute-start | bytes 110600 | tf_op jit(solution)/shard_map/while/body/eval_jaxpr/ppermute | solution.py:12
  502.0 16.4 %collective-permute-start.4 = (f32[8,4,512]{2,0,1:T(8,128)S(1)}, f32[8,4,512]{2,0,1:T(8,128)S(1)}, u32[]{:S(2)}, u32[]{:S(2)}) collective-permute-start(f32[8,4,512]{2,0,1:T(8,128)S(1)} %fusion.25), channel_id=1, source_target_pairs={{480,0},{0,32},{32,64},{64,96},{96,128},{128,160},{160,192},{192,2... | collective-permute-start | bytes 196616 | tf_op jit(solution)/shard_map/ppermute | solution.py:12
  (34 other events, 370.3 us)
where the time goes:
time: 792 us; the launch traced here: 790 us
  starting transfers between devices  301 us (38%)
  blocking collectives  271 us (34%)
  waiting for transfers between devices  108 us (14%)
  matrix products  84 us (11%)
  local copies, waits for them, and re-layouts  17.9 us (2%)
    ppermute x62, starting transfers between devices, shifted(): return lax.ppermute(block, axis, route)  301 us
    unnamed x1, blocking collectives  236 us
    ppermute x62, waiting for transfers between devices, shifted(): return lax.ppermute(block, axis, route)  108 us
    dot_general x16, matrix products, local_part(): jnp.einsum('rhc,kc->rhk', held_rows, flat_keys, preferred_element_type=jn...  69.6 us
    all_gather x1, blocking collectives, body(): lax.all_gather(value_output_rows, 'ctx', axis=0, tiled=True)  35 us
  transfers between devices with their start and end apart: 62, of which 25 were waited for; matrix products, arithmetic and copies ran while one was open for 0% of the time, Pallas kernels for 0%

commit v1 on v0

v1 whole, which is shorter than its diff:
```python
import numpy as np
import jax
import jax.numpy as jnp
from jax import lax
from jax.experimental import pallas as pl
from jax.experimental.pallas import tpu as pltpu
from jax.sharding import PartitionSpec as P

BF = jnp.bfloat16
F32 = jnp.float32
NEG = -1e30
H_DEV = 4
ROWS = 128
NOPE = 128
ROPE = 64
KVR = 512
VD = 128
BLOCK = 64
WIDE = 640
PAIR = 1152
QUAD = 4
COEF = float((NOPE + ROPE) ** -0.5 * np.log2(np.e))
INTERPRET = False

SAME_CORE = [[x * 4 + z * 2 + c for x in range(4) for z in range(2)] for c in range(2)]
SAME_CHIP = [[x * 4 + z * 2 + c for c in range(2)] for x in range(4) for z in range(2)]
SAME_HALF = [[x * 4 + z * 2 + c for c in range(2) for x in range(4)] for z in range(2)]


def nt_dot(a, b):
    return lax.dot_general(a, b, (((1,), (1,)), ((), ())), preferred_element_type=F32)


def dot(a, b):
    return jnp.dot(a, b, preferred_element_type=F32)


def pieces(x, n):
    out = []
    for _ in range(n):
        part = x.astype(BF).astype(F32)
        out.append(part)
        x = x - part
    return out


def with_stats(tops, totals, rows):
    lane = lax.broadcasted_iota(jnp.int32, (rows, 128), 1)
    tail = jnp.zeros((rows, 128), F32)
    for h in range(H_DEV):
        cols = pieces(tops[h], 3) + pieces(totals[h], 2)
        for k, col in enumerate(cols):
            tail = jnp.where(lane == 8 * h + k, col, tail)
    return tail


def stats_of(tail, h):
    t = tail[:, 8 * h : 8 * h + 8]
    top = t[:, 0:1] + (t[:, 1:2] + t[:, 2:3])
    return top, t[:, 3:4] + t[:, 4:5]


def attend(q_ref, we_ref, wo_ref, vue_ref, vuo_ref, bias_ref, kv_ref, out_ref, qe, qo, s_ref, p_ref):
    n_pairs = kv_ref.shape[1] // PAIR
    n_groups = n_pairs // QUAD
    for h in range(H_DEV):
        start = (h // 2) * 384 + (h % 2) * 128
        qs = q_ref[:, start : start + 256]
        qe[h * ROWS : (h + 1) * ROWS, :] = dot(qs, we_ref[h]).astype(BF)
        qo[h * ROWS : (h + 1) * ROWS, :] = dot(qs, wo_ref[h]).astype(BF)
    bias = jnp.concatenate([bias_ref[...]] * H_DEV, axis=0)

    top = jnp.full((H_DEV * ROWS, 128), NEG, F32)
    chunk = QUAD * BLOCK
    for i in range(n_groups):
        for odd in range(2):
            s = nt_dot((qe, qo)[odd][...], kv_slice(kv_ref, i, odd, WIDE))
            for part in range(chunk // 128):
                piece = s[:, part * 128 : (part + 1) * 128] + bias
                top = jnp.maximum(top, piece)
                at = (odd * n_groups + i) * chunk + part * 128
                s_ref[:, at : at + 128] = piece
    top = jnp.max(top, axis=1, keepdims=True)
    total = jnp.zeros((H_DEV * ROWS, 128), F32)
    for at in range(0, s_ref.shape[1], 128):
        w = jnp.exp2((s_ref[:, at : at + 128] - top) * COEF)
        total = total + w
        p_ref[:, at : at + 128] = w.astype(BF)
    total = jnp.sum(total, axis=1, keepdims=True)
    acc = [jnp.zeros((H_DEV * ROWS, KVR), F32), jnp.zeros((H_DEV * ROWS, WIDE), F32)]
    for odd in range(2):
        values = jnp.concatenate(
            [kv_slice(kv_ref, i, odd, (KVR, WIDE)[odd]) for i in range(n_groups)], axis=0
        )
        half = n_groups * chunk
        acc[odd] = dot(p_ref[:, odd * half : (odd + 1) * half], values).astype(BF)
    tops, totals = [], []
    for h in range(H_DEV):
        rows = slice(h * ROWS, (h + 1) * ROWS)
        z = dot(acc[0][rows], vue_ref[h]) + dot(acc[1][rows], vuo_ref[h])
        out_ref[:, h * VD : (h + 1) * VD] = z.astype(BF)
        tops.append(top[rows])
        totals.append(total[rows])
    out_ref[:, H_DEV * VD :] = with_stats(tops, totals, ROWS).astype(BF)


def kv_slice(kv_ref, i, odd, width):
    starts = [(i * QUAD + t) * PAIR + odd * KVR for t in range(QUAD)]
    return jnp.concatenate([kv_ref[:, s : s + width] for s in starts], axis=0)


def merge(parts, tails):
    nums, tops, totals = [], [], []
    for h in range(H_DEV):
        stats = [stats_of(t, h) for t in tails]
        top = stats[0][0]
        for m, _ in stats[1:]:
            top = jnp.maximum(top, m)
        num, total = 0.0, 0.0
        for part, (m, l) in zip(parts, stats):
            f = jnp.exp2((m - top) * COEF)
            num = num + part[:, h * VD : (h + 1) * VD] * f
            total = total + l * f
        nums.append(num)
        tops.append(top)
        totals.append(total)
    return nums, tops, totals


def merge_half(in_ref, out_ref):
    n, rows, _ = in_ref.shape
    data = [in_ref[s].astype(F32) for s in range(n)]
    nums, tops, totals = merge([d[:, : H_DEV * VD] for d in data], [d[:, H_DEV * VD :] for d in data])
    whole = jnp.concatenate(nums + [with_stats(tops, totals, rows)], axis=1).astype(BF)
    for k in range(out_ref.shape[0]):
        out_ref[k] = whole


def project(in_ref, w_ref, out_ref):
    groups = in_ref.shape[0] // 2
    data = [
        jnp.concatenate([in_ref[2 * g + z].astype(F32) for g in range(groups)], axis=0)
        for z in range(2)
    ]
    nums, _, totals = merge([d[:, : H_DEV * VD] for d in data], [d[:, H_DEV * VD :] for d in data])
    value = jnp.concatenate([n / t for n, t in zip(nums, totals)], axis=1).astype(BF)
    res = dot(value, w_ref[...])
    order = [res[(c * 8 + xz) * 8 : (c * 8 + xz) * 8 + 8] for xz in range(8) for c in range(2)]
    out_ref[...] = jnp.concatenate(order, axis=0).astype(BF)


def call(kernel, out_shape, *args, scratch=(), limit=16):
    return pl.pallas_call(
        kernel,
        out_shape=out_shape,
        in_specs=[pl.BlockSpec(memory_space=pltpu.VMEM)] * len(args),
        out_specs=pl.BlockSpec(memory_space=pltpu.VMEM),
        scratch_shapes=list(scratch),
        compiler_params=pltpu.CompilerParams(vmem_limit_bytes=limit * 2**20),
        interpret=INTERPRET,
    )(*args)


def spread(chunks, axis, groups):
    return lax.all_to_all(chunks, axis, 0, 0, axis_index_groups=groups)


def body(queries, w_uk, value_up_weight, w_out, kv_cache, blocks):
    own_rows = queries.shape[0]
    n_blocks = kv_cache.shape[0]
    q = spread(jnp.broadcast_to(queries[None], (8,) + queries.shape), "ctx", SAME_CORE)
    q = lax.all_gather(q.reshape(8 * own_rows, -1), "ctx", axis=0, tiled=True, axis_index_groups=SAME_CHIP)

    eye = jnp.broadcast_to(jnp.eye(ROPE, dtype=BF)[None], (H_DEV, ROPE, ROPE))

    def extended(lead):
        nope = jnp.pad(w_uk, ((0, 0), (0, 0), (lead, WIDE - KVR - lead)))
        rope = jnp.pad(eye, ((0, 0), (0, 0), (lead + KVR, WIDE - KVR - ROPE - lead)))
        both = jnp.concatenate([nope, rope], axis=1).reshape(H_DEV // 2, 2, NOPE + ROPE, WIDE)
        zero = jnp.zeros_like(both[:, 0, :ROPE])
        first = jnp.concatenate([both[:, 0], zero], axis=1)
        second = jnp.concatenate([zero, both[:, 1]], axis=1)
        return jnp.stack([first, second], axis=1).reshape(H_DEV, 256, WIDE)

    vu_odd = jnp.pad(value_up_weight, ((0, 0), (ROPE, ROPE), (0, 0)))
    picked = blocks.reshape(4, 2, 2, own_rows, -1).transpose(2, 0, 1, 3, 4).reshape(ROWS, -1)
    offsets = picked - lax.axis_index("ctx") * n_blocks
    lane = jnp.arange(2 * n_blocks, dtype=jnp.int32) % n_blocks
    present = jnp.any(offsets[:, :, None] == lane[None, None, :], axis=1)
    bias = jnp.where(present, 0.0, NEG).astype(F32)

    n_keys = n_blocks * BLOCK
    parts = call(
        attend,
        jax.ShapeDtypeStruct((ROWS, WIDE), BF),
        q, extended(0), extended(ROPE), value_up_weight, vu_odd, bias, kv_cache,
        scratch=[
            pltpu.VMEM((H_DEV * ROWS, WIDE), BF),
            pltpu.VMEM((H_DEV * ROWS, WIDE), BF),
            pltpu.VMEM((H_DEV * ROWS, n_keys), F32),
            pltpu.VMEM((H_DEV * ROWS, n_keys), BF),
        ],
        limit=40,
    )
    parts = spread(parts.reshape(8, 2 * own_rows, WIDE), "ctx", SAME_HALF)
    halves = call(merge_half, jax.ShapeDtypeStruct((8, 2 * own_rows, WIDE), BF), parts)
    halves = spread(halves, "ctx", SAME_CORE)
    halves = lax.all_gather(halves, "ctx", axis=0, tiled=True, axis_index_groups=SAME_CHIP)
    partial = call(project, jax.ShapeDtypeStruct((ROWS, w_out.shape[1]), BF), halves, w_out)
    n_head = lax.axis_size("head")
    pieces_in = lax.all_to_all(partial.reshape(n_head, ROWS // n_head, -1), "head", 0, 0)
    return jnp.sum(pieces_in.astype(F32), axis=0).astype(BF)


def solution(mesh):
    return jax.shard_map(
        body,
        mesh=mesh,
        in_specs=(
            P("ctx", "head"),
            P("head", None, None),
            P("head", None, None),
            P("head", "ctx"),
            P("ctx", None),
            P(),
        ),
        out_specs=P("head", "ctx"),
        check_vma=False,
    )
```

time: 792 us -> 108 us (0.14)
  the two profiles are of different devices: /device:TPU:2 before, /device:TPU:8 now
where the time goes in v1:
time: 108 us; the launch traced here: 107 us
  blocking collectives  37.1 us (34%)
  waiting for transfers between devices  25 us (23%)
  starting transfers between devices  22.1 us (20%)
  Pallas kernels  11.3 us (10%)
  local copies, waits for them, and re-layouts  7.85 us (7%)
  other arithmetic  3.55 us (3%)
    all_to_all x2, waiting for transfers between devices, spread(): return lax.all_to_all(chunks, axis, 0, 0, axis_index_groups=groups)  25 us
    all_to_all x1, blocking collectives, body(): lax.all_to_all(partial.reshape(n_head, ROWS // n_head, -1), 'head', 0, 0)  24.9 us
    all_to_all x2, starting transfers between devices, spread(): return lax.all_to_all(chunks, axis, 0, 0, axis_index_groups=groups)  22.1 us
    pallas_call x3, Pallas kernels, call(): pl.pallas_call(kernel, out_shape=out_shape, in_specs=[pl.BlockSpec(memory...  11.3 us
    all_to_all x1, blocking collectives, spread(): return lax.all_to_all(chunks, axis, 0, 0, axis_index_groups=groups)  8.25 us
    unnamed x10, local copies, waits for them, and re-layouts  6 us
  transfers between devices with their start and end apart: 2, of which 2 were waited for; matrix products, arithmetic and copies ran while one was open for 4% of the time, Pallas kernels for 0%

profile of v1, /device:TPU:8, one launch (start us, length us, event | category | flops | bytes accessed | tf_op | source)
XLA Modules:
  0.0 107.0 jit_solution(6546036039483284251)
XLA Ops:
  0.0 1.3 %broadcast_in_dim.24 = bf16[8,8,768]{2,1,0:T(8,128)(2,1)} broadcast(bf16[8,768]{1,0:T(8,128)(2,1)} %param.6), dimensions={1,2} | broadcast | bytes 110592 | tf_op jit(solution)/shard_map/broadcast_in_dim | solution.py:171
  1.3 17.6 %all-to-all-start = ((bf16[8,8,768]{2,1,0:T(8,128)(2,1)}), bf16[8,8,768]{2,1,0:T(8,128)(2,1)S(1)}, u32[]{:S(2)}, u32[]{:S(2)}) async-start(bf16[8,8,768]{2,1,0:T(8,128)(2,1)} %broadcast_in_dim.24), calls=%async_computation | async-start | bytes 196608 | tf_op jit(solution)/shard_map/all_to_all | solution.py:165
  18.9 1.7 %fusion.5 = (bf16[4,192,640]{2,1,0:T(8,128)(2,1)S(1)}, bf16[4,192,640]{2,1,0:T(8,128)(2,1)S(1)}) fusion(bf16[4,64,64]{2,1,0:T(8,128)(2,1)S(1)} %broadcast_in_dim.25, bf16[4,128,512]{2,1,0:T(8,128)(2,1)} %param.7), kind=kLoop, calls=%fused_computation.10 | loop fusion | flops 6881280 | bytes 2523136 | tf_op jit(solution)/shard_map/concatenate | solution.py:179
  20.6 0.0 copy-start.3
  20.6 0.1 slice_bitcast_fusion.1
  20.7 0.1 slice_bitcast_fusion.3
  20.8 0.5 copy-done.3
  21.3 0.1 copy.30
  21.5 0.1 pad_bitcast_fusion
  21.6 0.1 pad_maximum_fusion.1
  21.7 0.0 copy-start.1
  21.7 0.1 pad_bitcast_fusion.2
  21.9 0.1 pad_maximum_fusion
  22.0 0.8 copy-done.1
  22.8 0.1 pad.28.vuo_ref
  22.8 0.9 compare_reduce_fusion
  23.7 10.4 %all-to-all-done = bf16[8,8,768]{2,1,0:T(8,128)(2,1)S(1)} async-done(((bf16[8,8,768]{2,1,0:T(8,128)(2,1)}), bf16[8,8,768]{2,1,0:T(8,128)(2,1)S(1)}, u32[]{:S(2)}, u32[]{:S(2)}) %all-to-all-start) | async-done | bytes 98336 | tf_op jit(solution)/shard_map/all_to_all | solution.py:165
  34.1 1.9 %all_gather.6.q_ref = bf16[128,768]{1,0:T(8,128)(2,1)S(1)} all-gather(bf16[64,768]{1,0:T(8,128)(2,1)S(1)} %bitcast.39), channel_id=1, replica_groups={{0,32},{64,96},{128,160},{192,224},{256,288},{320,352},{384,416},{448,4..., dimensions={0}, use_global_device_ids=true | all-gather | bytes 294912 | tf_op jit(solution)/shard_map/all_gather | solution.py:172
  36.1 0.0 copy-start
  36.1 2.3 %copy-done = bf16[64,36864]{1,0:T(8,128)(2,1)S(1)} copy-done((bf16[64,36864]{1,0:T(8,128)(2,1)S(1)}, bf16[64,36864]{1,0:T(8,128)(2,1)}, u32[]{:S(2)}) %copy-start) | copy-done | bytes 4718616
  38.4 0.0 copy-start.2
  38.4 1.0 copy-done.2
  39.5 9.6 %shard_map.64 = bf16[128,640]{1,0:T(8,128)(2,1)S(1)} custom-call(bf16[128,768]{1,0:T(8,128)(2,1)S(1)} %all_gather.6.q_ref, bf16[4,256,640]{2,1,0:T(8,128)(2,1)S(1)} %bitcast.35, bf16[4,256,640]{2,1,0:T(8,128)(2,1)S(1)} %bitcast.34, bf16[4,512,128]{2,1,0:T(8,128)(2,1)S(1)} %copy-done.2, bf16[4,640,128]{2,1,0:T(8,128)(2,1)S(1)} %pad.28.vuo_ref, ...), custom_call_target="tpu_custom_call" | custom-call | tf_op jit(solution)/shard_map/pallas_call | solution.py:153
  49.1 8.3 %all_to_all.20.in_ref = bf16[8,16,640]{2,1,0:T(8,128)(2,1)S(1)} all-to-all(bf16[8,16,640]{2,1,0:T(8,128)(2,1)S(1)} %bitcast.36), channel_id=1, replica_groups={{0,128,256,384,32,160,288,416},{64,192,320,448,96,224,352,480},{1,129,2..., dimensions={0} | all-to-all | bytes 327680 | tf_op jit(solution)/shard_map/all_to_all | solution.py:165
  57.3 1.0 shard_map.65
  58.3 4.5 %all-to-all-start.2 = ((bf16[8,16,640]{2,1,0:T(8,128)(2,1)}), bf16[8,16,640]{2,1,0:T(8,128)(2,1)S(1)}, u32[]{:S(2)}, u32[]{:S(2)}) async-start(bf16[8,16,640]{2,1,0:T(8,128)(2,1)} %shard_map.65), calls=%async_computation.2 | async-start | bytes 327680 | tf_op jit(solution)/shard_map/all_to_all | solution.py:165
  62.8 1.2 %copy.32.w_ref = bf16[512,448]{1,0:T(8,128)(2,1)S(1)} copy(bf16[512,448]{0,1:T(8,128)(2,1)} %param.9) | data formatting | bytes 917504 | tf_op args[3]
  64.1 14.6 %all-to-all-done.2 = bf16[8,16,640]{2,1,0:T(8,128)(2,1)S(1)} async-done(((bf16[8,16,640]{2,1,0:T(8,128)(2,1)}), bf16[8,16,640]{2,1,0:T(8,128)(2,1)S(1)}, u32[]{:S(2)}, u32[]{:S(2)}) %all-to-all-start.2) | async-done | bytes 163872 | tf_op jit(solution)/shard_map/all_to_all | solution.py:165
  78.7 2.0 %all_gather.7.in_ref = bf16[16,16,640]{2,1,0:T(8,128)(2,1)S(1)} all-gather(bf16[8,16,640]{2,1,0:T(8,128)(2,1)S(1)} %all-to-all-done.2), channel_id=1, replica_groups={{0,32},{64,96},{128,160},{192,224},{256,288},{320,352},{384,416},{448,4..., dimensions={0}, use_global_device_ids=true | all-gather | bytes 491520 | tf_op jit(solution)/shard_map/all_gather | solution.py:208
  80.7 0.7 shard_map.66
  81.4 0.1 reshape.56
  81.4 24.9 %all_to_all.21 = bf16[32,4,448]{2,1,0:T(4,128)(2,1)S(1)} all-to-all(bf16[32,4,448]{2,1,0:T(4,128)(2,1)S(1)} %reshape.56), channel_id=1, replica_groups=mesh['ctx'=16,'head'=32] {'head'}, dimensions={0} | all-to-all | bytes 229376 | tf_op jit(solution)/shard_map/all_to_all | solution.py:211
  106.3 0.7 reduce_sum.12
  (6 shorter events, 0.0 us)
Async XLA Ops:
  1.3 32.8 %all-to-all-start = ((bf16[8,8,768]{2,1,0:T(8,128)(2,1)}), bf16[8,8,768]{2,1,0:T(8,128)(2,1)S(1)}, u32[]{:S(2)}, u32[]{:S(2)}) async-start(bf16[8,8,768]{2,1,0:T(8,128)(2,1)} %broadcast_in_dim.24), calls=%async_computation | async-start | bytes 196608 | tf_op jit(solution)/shard_map/all_to_all | solution.py:165
  20.6 0.7 copy-start.3
  21.7 1.0 copy-start.1
  36.1 2.3 %copy-start = (bf16[64,36864]{1,0:T(8,128)(2,1)S(1)}, bf16[64,36864]{1,0:T(8,128)(2,1)}, u32[]{:S(2)}) copy-start(bf16[64,36864]{1,0:T(8,128)(2,1)} %kv_ref.1) | copy-start | bytes 14155780
  38.4 1.0 copy-start.2
  58.3 20.4 %all-to-all-start.2 = ((bf16[8,16,640]{2,1,0:T(8,128)(2,1)}), bf16[8,16,640]{2,1,0:T(8,128)(2,1)S(1)}, u32[]{:S(2)}, u32[]{:S(2)}) async-start(bf16[8,16,640]{2,1,0:T(8,128)(2,1)} %shard_map.65), calls=%async_computation.2 | async-start | bytes 327680 | tf_op jit(solution)/shard_map/all_to_all | solution.py:165

commit v2 on v1

v2 whole, which is shorter than its diff:
```python
import numpy as np
import jax
import jax.numpy as jnp
from jax import lax
from jax.experimental import pallas as pl
from jax.experimental.pallas import tpu as pltpu
from jax.sharding import PartitionSpec as P

BF = jnp.bfloat16
F32 = jnp.float32
NEG = -1e30
H_DEV = 4
ROWS = 128
NOPE = 128
ROPE = 64
KVR = 512
VD = 128
BLOCK = 64
WIDE = 640
PAIR = 1152
PARTS = 2
CHUNK = 512
QUAD = 4
COEF = float((NOPE + ROPE) ** -0.5 * np.log2(np.e))
INTERPRET = False
KEY = KVR + ROPE

SAME_HALF = [[x * 4 + z * 2 + c for x in range(4) for c in range(2)] for z in range(2)]


def nt_dot(a, b):
    return lax.dot_general(a, b, (((1,), (1,)), ((), ())), preferred_element_type=F32)


def dot(a, b):
    return jnp.dot(a, b, preferred_element_type=F32)


def pieces(x, n):
    out = []
    for _ in range(n):
        part = x.astype(BF).astype(F32)
        out.append(part)
        x = x - part
    return out


def with_stats(tops, totals, rows):
    lane = lax.broadcasted_iota(jnp.int32, (rows, 128), 1)
    tail = jnp.zeros((rows, 128), F32)
    for h in range(H_DEV):
        cols = pieces(tops[h], 3) + pieces(totals[h], 2)
        for k, col in enumerate(cols):
            tail = jnp.where(lane == 8 * h + k, col, tail)
    return tail


def stats_of(tail, h):
    t = tail[:, 8 * h : 8 * h + 8]
    top = t[:, 0:1] + (t[:, 1:2] + t[:, 2:3])
    return top, t[:, 3:4] + t[:, 4:5]


def stage(kv_ref, out_ref):
    rows = kv_ref.shape[0]
    keys = [kv_ref[:, t * PAIR : (t + 1) * PAIR][:, o : o + KEY] for t in range(QUAD) for o in (0, KEY)]
    pad = jnp.zeros((rows, WIDE - KEY), BF)
    out_ref[...] = jnp.concatenate([jnp.concatenate([k, pad], axis=1) for k in keys], axis=0)


def staged(kv):
    steps = kv.shape[1] // (PAIR * QUAD)
    chunk = kv.shape[0] * 2 * QUAD
    return pl.pallas_call(
        stage,
        grid=(steps,),
        out_shape=jax.ShapeDtypeStruct((steps * chunk, WIDE), BF),
        in_specs=[pl.BlockSpec((kv.shape[0], PAIR * QUAD), lambda i: (0, i))],
        out_specs=pl.BlockSpec((chunk, WIDE), lambda i: (i, 0)),
        compiler_params=pltpu.CompilerParams(vmem_limit_bytes=16 * 2**20),
        interpret=INTERPRET,
    )(kv)


def attend(q_ref, we_ref, vue_ref, bias_ref, k_hbm, out_ref, qe, s_ref, p_ref, k_ref, sems):
    copies = {}
    for n, first in enumerate(range(0, k_ref.shape[0], CHUNK)):
        rows = pl.ds(first, CHUNK)
        copies[first] = pltpu.make_async_copy(k_hbm.at[rows], k_ref.at[rows], sems.at[n])
        copies[first].start()
    n_part = k_ref.shape[0] // PARTS
    for h in range(H_DEV):
        start = (h // 2) * 384 + (h % 2) * 128
        qs = q_ref[:, start : start + 256]
        qe[h * ROWS : (h + 1) * ROWS, :] = dot(qs, we_ref[h]).astype(BF)
    bias = jnp.concatenate([bias_ref[...]] * H_DEV, axis=0)

    def score(first, top):
        copies[first].wait()
        s = nt_dot(qe[...], k_ref[first : first + CHUNK, :])
        for at in range(0, CHUNK, 128):
            piece = s[:, at : at + 128] + bias
            top = jnp.maximum(top, piece)
            s_ref[:, first + at : first + at + 128] = piece
        return top

    def weigh(first, top, total):
        for at in range(first, first + CHUNK, 128):
            w = jnp.exp2((s_ref[:, at : at + 128] - top) * COEF)
            total = total + w
            p_ref[:, at : at + 128] = w.astype(BF)
        return total

    lowest = jnp.full((H_DEV * ROWS, 128), NEG, F32)
    tops, totals, accs = [], [], []
    top = lowest
    for first in range(0, n_part, CHUNK):
        top = score(first, top)
    tops.append(jnp.max(top, axis=1, keepdims=True))
    for part in range(PARTS):
        begin = part * n_part
        total = jnp.zeros((H_DEV * ROWS, 128), F32)
        top = lowest
        for first in range(begin, begin + n_part, CHUNK):
            if part + 1 < PARTS:
                top = score(first + n_part, top)
            total = weigh(first, tops[part], total)
        if part + 1 < PARTS:
            tops.append(jnp.max(top, axis=1, keepdims=True))
        totals.append(jnp.sum(total, axis=1, keepdims=True))
        accs.append(dot(p_ref[:, begin : begin + n_part], k_ref[begin : begin + n_part, :KVR]))
    top = tops[0]
    for t in tops[1:]:
        top = jnp.maximum(top, t)
    acc, total = 0.0, 0.0
    for a, t, l in zip(accs, tops, totals):
        f = jnp.exp2((t - top) * COEF)
        acc = acc + f * a
        total = total + f * l
    acc = acc.astype(BF)
    heads = [slice(h * ROWS, (h + 1) * ROWS) for h in range(H_DEV)]
    for h, rows in enumerate(heads):
        out_ref[:, h * VD : (h + 1) * VD] = dot(acc[rows], vue_ref[h]).astype(BF)
    tail = with_stats([top[rows] for rows in heads], [total[rows] for rows in heads], ROWS)
    out_ref[:, H_DEV * VD :] = tail.astype(BF)


def merge(parts, tails):
    nums, tops, totals = [], [], []
    for h in range(H_DEV):
        stats = [stats_of(t, h) for t in tails]
        top = stats[0][0]
        for m, _ in stats[1:]:
            top = jnp.maximum(top, m)
        num, total = 0.0, 0.0
        for part, (m, l) in zip(parts, stats):
            f = jnp.exp2((m - top) * COEF)
            num = num + part[:, h * VD : (h + 1) * VD] * f
            total = total + l * f
        nums.append(num)
        tops.append(top)
        totals.append(total)
    return nums, tops, totals


def merge_half(in_ref, out_ref):
    n, rows, _ = in_ref.shape
    data = [in_ref[s].astype(F32) for s in range(n)]
    nums, tops, totals = merge([d[:, : H_DEV * VD] for d in data], [d[:, H_DEV * VD :] for d in data])
    whole = jnp.concatenate(nums + [with_stats(tops, totals, rows)], axis=1).astype(BF)
    for k in range(out_ref.shape[0]):
        out_ref[k] = whole


def project(in_ref, w_ref, out_ref):
    data = [
        jnp.concatenate(
            [in_ref[x * 4 + z * 2 + c].astype(F32) for x in range(4) for c in range(2)], axis=0
        )
        for z in range(2)
    ]
    nums, _, totals = merge([d[:, : H_DEV * VD] for d in data], [d[:, H_DEV * VD :] for d in data])
    value = jnp.concatenate([n / t for n, t in zip(nums, totals)], axis=1).astype(BF)
    out_ref[...] = nt_dot(value, w_ref[...]).astype(BF)


def call(kernel, out_shape, *args, scratch=(), spaces=None, limit=16):
    return pl.pallas_call(
        kernel,
        out_shape=out_shape,
        in_specs=[pl.BlockSpec(memory_space=m) for m in spaces or [pltpu.VMEM] * len(args)],
        out_specs=pl.BlockSpec(memory_space=pltpu.VMEM),
        scratch_shapes=list(scratch),
        compiler_params=pltpu.CompilerParams(vmem_limit_bytes=limit * 2**20),
        interpret=INTERPRET,
    )(*args)


def body(queries, w_uk, value_up_weight, w_out, kv_cache, blocks):
    n_ctx = lax.axis_size("ctx")
    n_blocks = kv_cache.shape[0]
    q = lax.all_to_all(jnp.broadcast_to(queries[None], (n_ctx,) + queries.shape), "ctx", 0, 0)
    q = q.reshape(ROWS, -1)

    eye = jnp.broadcast_to(jnp.eye(ROPE, dtype=BF)[None], (H_DEV, ROPE, ROPE))
    nope = jnp.pad(w_uk, ((0, 0), (0, 0), (0, WIDE - KVR)))
    rope = jnp.pad(eye, ((0, 0), (0, 0), (KVR, WIDE - KVR - ROPE)))
    both = jnp.concatenate([nope, rope], axis=1).reshape(H_DEV // 2, 2, NOPE + ROPE, WIDE)
    zero = jnp.zeros_like(both[:, 0, :ROPE])
    first = jnp.concatenate([both[:, 0], zero], axis=1)
    second = jnp.concatenate([zero, both[:, 1]], axis=1)
    absorb = jnp.stack([first, second], axis=1).reshape(H_DEV, 256, WIDE)

    offsets = blocks - lax.axis_index("ctx") * n_blocks
    lane = jnp.arange(2 * n_blocks, dtype=jnp.int32) % n_blocks
    present = jnp.any(offsets[:, :, None] == lane[None, None, :], axis=1)
    bias = jnp.where(present, 0.0, NEG).astype(F32)

    keys = pltpu.with_memory_space_constraint(staged(kv_cache), pltpu.HBM)
    parts = call(
        attend,
        jax.ShapeDtypeStruct((ROWS, WIDE), BF),
        q, absorb, value_up_weight, bias, keys,
        scratch=[
            pltpu.VMEM((H_DEV * ROWS, WIDE), BF),
            pltpu.VMEM((H_DEV * ROWS, keys.shape[0]), F32),
            pltpu.VMEM((H_DEV * ROWS, keys.shape[0]), BF),
            pltpu.VMEM(keys.shape, BF),
            pltpu.SemaphoreType.DMA((keys.shape[0] // CHUNK,)),
        ],
        spaces=[pltpu.VMEM] * 4 + [pltpu.HBM],
        limit=40,
    )
    own = ROWS // (n_ctx // 2)
    parts = lax.all_to_all(
        parts.reshape(n_ctx // 2, own, WIDE), "ctx", 0, 0, axis_index_groups=SAME_HALF
    )
    halves = call(merge_half, jax.ShapeDtypeStruct((n_ctx, own, WIDE), BF), parts)
    halves = lax.all_to_all(halves, "ctx", 0, 0)
    partial = call(project, jax.ShapeDtypeStruct((ROWS, w_out.shape[1]), BF), halves, w_out.T)
    n_head = lax.axis_size("head")
    shares = lax.all_to_all(partial.reshape(n_head, ROWS // n_head, -1), "head", 0, 0)
    return jnp.sum(shares.astype(F32), axis=0).astype(BF)


def solution(mesh):
    return jax.shard_map(
        body,
        mesh=mesh,
        in_specs=(
            P("ctx", "head"),
            P("head", None, None),
            P("head", None, None),
            P("head", "ctx"),
            P("ctx", None),
            P(),
        ),
        out_specs=P("head", "ctx"),
        check_vma=False,
    )
```

time: 108 us -> 111 us (1.028)
  blocking collectives: 37.1 us -> 63.5 us
  waiting for transfers between devices: 25 us -> 9.1 us
  starting transfers between devices: 22.1 us -> 17.7 us
  local copies, waits for them, and re-layouts: 7.85 us -> 5.15 us
  Pallas kernels: 11.3 us -> 12.5 us
    all_to_all x1 -> x2, blocking collectives: 8.25 us -> 31.7 us  [the longest x1 22.8 us: body(): halves = lax.all_to_all(halves, 'ctx', 0, 0)]
    all_to_all x2 -> x1, waiting for transfers between devices: 25 us -> 9.1 us  [body(): lax.all_to_all(jnp.broadcast_to(queries[None], (n_ctx,) + queries.shape),...]
    all_to_all x1, blocking collectives: 24.9 us -> 31.8 us  [body(): lax.all_to_all(partial.reshape(n_head, ROWS // n_head, -1), 'head', 0, 0)]
    all_to_all x2 -> x1, starting transfers between devices: 22.1 us -> 17.7 us  [body(): lax.all_to_all(jnp.broadcast_to(queries[None], (n_ctx,) + queries.shape),...]
    all_gather x2 -> x0, blocking collectives: 3.96 us -> none  [the longest x1 2.03 us: body(): lax.all_gather(halves, 'ctx', axis=0, tiled=True, axis_index_groups=SAME_...]
    unnamed x10, local copies, waits for them, and re-layouts: 6 us -> 3.4 us
    pallas_call x0 -> x1, Pallas kernels: none -> 1.61 us  [staged(): pl.pallas_call(stage, grid=(steps,), out_shape=jax.ShapeDtypeStruct((step...]
    concatenate x1, other arithmetic: 1.68 us -> 0.08 us  [body(): jnp.concatenate([nope, rope], axis=1)]
  transfers between devices with their start and end apart: 2 -> 1, of which waited for: 2 -> 1; matrix products, arithmetic and copies ran while one was open for 4% -> 2% of each run, Pallas kernels for 0% -> 1%
where the time goes in v2:
time: 111 us
  blocking collectives  63.5 us (57%)
  starting transfers between devices  17.7 us (16%)
  Pallas kernels  12.5 us (11%)
  waiting for transfers between devices  9.1 us (8%)
  local copies, waits for them, and re-layouts  5.15 us (5%)
  other arithmetic  2.53 us (2%)
    all_to_all x1, blocking collectives, body(): lax.all_to_all(partial.reshape(n_head, ROWS // n_head, -1), 'head', 0, 0)  31.8 us
    all_to_all x1, blocking collectives, body(): halves = lax.all_to_all(halves, 'ctx', 0, 0)  22.8 us
    all_to_all x1, starting transfers between devices, body(): lax.all_to_all(jnp.broadcast_to(queries[None], (n_ctx,) + queries.shape),...  17.7 us
    pallas_call x3, Pallas kernels, call(): pl.pallas_call(kernel, out_shape=out_shape, in_specs=[pl.BlockSpec(memory...  10.8 us
    all_to_all x1, waiting for transfers between devices, body(): lax.all_to_all(jnp.broadcast_to(queries[None], (n_ctx,) + queries.shape),...  9.1 us
    all_to_all x1, blocking collectives, body(): lax.all_to_all(parts.reshape(n_ctx // 2, own, WIDE), 'ctx', 0, 0, axis_in...  8.88 us
    unnamed x10, local copies, waits for them, and re-layouts  3.4 us
  transfers between devices with their start and end apart: 1, of which 1 were waited for; matrix products, arithmetic and copies ran while one was open for 2% of the time, Pallas kernels for 1%

profile of v2, /device:TPU:8, one launch (start us, length us, event | category | flops | bytes accessed | tf_op | source)
XLA Modules:
  0.0 110.5 jit_solution(8644376981454236247)
XLA Ops:
  0.0 1.4 %broadcast_in_dim.10 = bf16[16,8,768]{2,1,0:T(8,128)(2,1)} broadcast(bf16[8,768]{1,0:T(8,128)(2,1)} %param.6), dimensions={1,2} | broadcast | bytes 208896 | tf_op jit(solution)/shard_map/broadcast_in_dim | solution.py:202
  1.4 17.7 %all-to-all-start = ((bf16[16,8,768]{2,1,0:T(8,128)(2,1)}), bf16[16,8,768]{2,1,0:T(8,128)(2,1)S(1)}, u32[]{:S(2)}, u32[]{:S(2)}) async-start(bf16[16,8,768]{2,1,0:T(8,128)(2,1)} %broadcast_in_dim.10), calls=%async_computation | async-start | bytes 393216 | tf_op jit(solution)/shard_map/all_to_all | solution.py:202
  19.1 0.7 broadcast_subtract_fusion
  19.8 0.1 copy.15
  19.9 0.0 copy-start.1
  19.9 2.3 %copy-done.1 = bf16[64,36864]{1,0:T(8,128)(2,1)S(1)} copy-done((bf16[64,36864]{1,0:T(8,128)(2,1)S(1)}, bf16[64,36864]{1,0:T(8,128)(2,1)}, u32[]{:S(2)}) %copy-start.1) | copy-done | bytes 4718616
  22.3 0.0 copy-start.4
  22.3 1.6 %shard_map.64.k_hbm = bf16[4096,640]{1,0:T(8,128)(2,1)S(1)} custom-call(bf16[64,36864]{1,0:T(8,128)(2,1)S(1)} %copy-done.1), custom_call_target="tpu_custom_call" | custom-call | tf_op jit(solution)/shard_map/pallas_call | solution.py:74
  23.9 0.0 copy-start
  23.9 0.9 compare_reduce_fusion
  24.8 0.0 copy-done.4
  24.8 0.1 fusion.2
  24.9 0.1 slice_bitcast_fusion.1
  25.0 0.0 copy-start.2
  25.0 0.1 pad_bitcast_fusion
  25.1 1.1 copy-done
  26.2 0.1 pad_maximum_fusion
  26.3 9.1 %all-to-all-done = bf16[16,8,768]{2,1,0:T(8,128)(2,1)S(1)} async-done(((bf16[16,8,768]{2,1,0:T(8,128)(2,1)}), bf16[16,8,768]{2,1,0:T(8,128)(2,1)S(1)}, u32[]{:S(2)}, u32[]{:S(2)}) %all-to-all-start) | async-done | bytes 196640 | tf_op jit(solution)/shard_map/all_to_all | solution.py:202
  35.4 0.0 copy-done.2
  35.4 0.0 copy-start.3
  35.4 9.8 %shard_map.65 = bf16[128,640]{1,0:T(8,128)(2,1)S(1)} custom-call(bf16[128,768]{1,0:T(8,128)(2,1)S(1)} %bitcast.18, bf16[4,256,640]{2,1,0:T(8,128)(2,1)S(1)} %bitcast.17, bf16[4,512,128]{2,1,0:T(8,128)(2,1)S(1)} %copy-done.2, f32[128,128]{1,0:T(8,128)S(1)} %broadcast_select_fusion.bias_ref, bf16[4096,640]{1,0:T(8,128)(2,1)} %copy-done), custom_call_target="tpu_custom_call" | custom-call | tf_op jit(solution)/shard_map/pallas_call | solution.py:188
  45.3 8.9 %all_to_all.20.in_ref = bf16[8,16,640]{2,1,0:T(8,128)(2,1)S(1)} all-to-all(bf16[8,16,640]{2,1,0:T(8,128)(2,1)S(1)} %bitcast.19), channel_id=1, replica_groups={{0,32,128,160,256,288,384,416},{64,96,192,224,320,352,448,480},{1,33,12..., dimensions={0} | all-to-all | bytes 327680 | tf_op jit(solution)/shard_map/all_to_all | solution.py:235
  54.1 0.4 shard_map.66
  54.5 22.8 %all_to_all.21.in_ref = bf16[16,16,640]{2,1,0:T(8,128)(2,1)S(1)} all-to-all(bf16[16,16,640]{2,1,0:T(8,128)(2,1)S(1)} %shard_map.66), channel_id=1, replica_groups=mesh['ctx'=16,'head'=32] {'ctx'}, dimensions={0} | all-to-all | bytes 655360 | tf_op jit(solution)/shard_map/all_to_all | solution.py:239
  77.3 0.0 copy-done.3
  77.3 0.6 shard_map.67
  78.0 0.1 reshape.38
  78.1 31.8 %all_to_all.22 = bf16[32,4,448]{2,1,0:T(4,128)(2,1)S(1)} all-to-all(bf16[32,4,448]{2,1,0:T(4,128)(2,1)S(1)} %reshape.38), channel_id=1, replica_groups=mesh['ctx'=16,'head'=32] {'head'}, dimensions={0} | all-to-all | bytes 229376 | tf_op jit(solution)/shard_map/all_to_all | solution.py:242
  109.9 0.7 reduce_sum.12
  (4 shorter events, 0.0 us)
Async XLA Ops:
  1.4 34.0 %all-to-all-start = ((bf16[16,8,768]{2,1,0:T(8,128)(2,1)}), bf16[16,8,768]{2,1,0:T(8,128)(2,1)S(1)}, u32[]{:S(2)}, u32[]{:S(2)}) async-start(bf16[16,8,768]{2,1,0:T(8,128)(2,1)} %broadcast_in_dim.10), calls=%async_computation | async-start | bytes 393216 | tf_op jit(solution)/shard_map/all_to_all | solution.py:202
  19.9 2.3 %copy-start.1 = (bf16[64,36864]{1,0:T(8,128)(2,1)S(1)}, bf16[64,36864]{1,0:T(8,128)(2,1)}, u32[]{:S(2)}) copy-start(bf16[64,36864]{1,0:T(8,128)(2,1)} %kv_ref.1) | copy-start | bytes 14155780
  22.3 2.5 %copy-start.4 = (bf16[4,128,512]{2,1,0:T(8,128)(2,1)S(1)}, bf16[4,128,512]{2,1,0:T(8,128)(2,1)}, u32[]{:S(2)}) copy-start(bf16[4,128,512]{2,1,0:T(8,128)(2,1)} %param.7) | copy-start | bytes 1572868
  23.9 2.3 %copy-start = (bf16[4096,640]{1,0:T(8,128)(2,1)}, bf16[4096,640]{1,0:T(8,128)(2,1)S(1)}, u32[]{:S(2)}) copy-start(bf16[4096,640]{1,0:T(8,128)(2,1)S(1)} %shard_map.64.k_hbm) | copy-start | bytes 15728644
  25.0 10.4 %copy-start.2 = (bf16[4,512,128]{2,1,0:T(8,128)(2,1)S(1)}, bf16[4,512,128]{2,1,0:T(8,128)(2,1)}, u32[]{:S(2)}) copy-start(bf16[4,512,128]{2,1,0:T(8,128)(2,1)} %vue_ref.1) | copy-start | bytes 1572868
  35.4 41.9 %copy-start.3 = (bf16[512,448]{0,1:T(8,128)(2,1)S(1)}, bf16[512,448]{0,1:T(8,128)(2,1)}, u32[]{:S(2)}) copy-start(bf16[512,448]{0,1:T(8,128)(2,1)} %param.9) | copy-start | bytes 1376260

commit v3 on v2

--- a/solution.py
+++ b/solution.py
@@ -18,14 +18,16 @@
 BLOCK = 64
 WIDE = 640
 PAIR = 1152
-PARTS = 2
+PARTS = (0.25, 0.375, 0.375)
 CHUNK = 512
 QUAD = 4
 COEF = float((NOPE + ROPE) ** -0.5 * np.log2(np.e))
 INTERPRET = False
 KEY = KVR + ROPE
 
-SAME_HALF = [[x * 4 + z * 2 + c for x in range(4) for c in range(2)] for z in range(2)]
+SAME_CORE = [[x * 4 + z * 2 + c for x in range(4) for z in range(2)] for c in range(2)]
+SAME_CHIP = [[x * 4 + z * 2 + c for c in range(2)] for x in range(4) for z in range(2)]
+SAME_HALF = [[x * 4 + z * 2 + c for c in range(2) for x in range(4)] for z in range(2)]
 
 
 def nt_dot(a, b):
@@ -34,6 +36,10 @@
 
 def dot(a, b):
     return jnp.dot(a, b, preferred_element_type=F32)
+
+
+def tn_dot(a, b):
+    return lax.dot_general(a, b, (((0,), (0,)), ((), ())), preferred_element_type=F32)
 
 
 def pieces(x, n):
@@ -82,67 +88,79 @@
     )(kv)
 
 
-def attend(q_ref, we_ref, vue_ref, bias_ref, k_hbm, out_ref, qe, s_ref, p_ref, k_ref, sems):
-    copies = {}
-    for n, first in enumerate(range(0, k_ref.shape[0], CHUNK)):
-        rows = pl.ds(first, CHUNK)
-        copies[first] = pltpu.make_async_copy(k_hbm.at[rows], k_ref.at[rows], sems.at[n])
-        copies[first].start()
-    n_part = k_ref.shape[0] // PARTS
+def attend(q_ref, wt_ref, vue_ref, bias_ref, k_hbm, out_ref, qt, s_ref, p_ref, k_ref, sems):
+    width = qt.shape[1]
+    rows = width // H_DEV
+    bounds = [0]
+    for share in PARTS:
+        bounds.append(bounds[-1] + int(share * k_ref.shape[0]))
+    spans = list(zip(bounds, bounds[1:]))
+    copies = []
+    for n, (a, b) in enumerate(spans):
+        span = pl.ds(a, b - a)
+        copies.append(pltpu.make_async_copy(k_hbm.at[span], k_ref.at[span], sems.at[n]))
+        copies[-1].start()
     for h in range(H_DEV):
         start = (h // 2) * 384 + (h % 2) * 128
-        qs = q_ref[:, start : start + 256]
-        qe[h * ROWS : (h + 1) * ROWS, :] = dot(qs, we_ref[h]).astype(BF)
-    bias = jnp.concatenate([bias_ref[...]] * H_DEV, axis=0)
+        q = q_ref[:, start : start + 256]
+        qt[:, h * rows : (h + 1) * rows] = nt_dot(wt_ref[h], q).astype(BF)
 
     def score(first, top):
-        copies[first].wait()
-        s = nt_dot(qe[...], k_ref[first : first + CHUNK, :])
+        s = dot(k_ref[first : first + CHUNK, :], qt[...])
         for at in range(0, CHUNK, 128):
-            piece = s[:, at : at + 128] + bias
-            top = jnp.maximum(top, piece)
-            s_ref[:, first + at : first + at + 128] = piece
+            piece = s[at : at + 128, :] + jnp.concatenate([bias_ref[...]] * H_DEV, axis=1)
+            top = jnp.maximum(top, jnp.max(piece.reshape(16, 8, width), axis=0))
+            s_ref[first + at : first + at + 128, :] = piece
         return top
 
     def weigh(first, top, total):
         for at in range(first, first + CHUNK, 128):
-            w = jnp.exp2((s_ref[:, at : at + 128] - top) * COEF)
-            total = total + w
-            p_ref[:, at : at + 128] = w.astype(BF)
+            w = jnp.exp2((s_ref[at : at + 128, :] - top) * COEF)
+            total = total + jnp.sum(w.reshape(16, 8, width), axis=0)
+            p_ref[at : at + 128, :] = w.astype(BF)
         return total
 
-    lowest = jnp.full((H_DEV * ROWS, 128), NEG, F32)
+    lowest = jnp.full((8, width), NEG, F32)
     tops, totals, accs = [], [], []
+    copies[0].wait()
     top = lowest
-    for first in range(0, n_part, CHUNK):
+    for first in range(spans[0][0], spans[0][1], CHUNK):
         top = score(first, top)
-    tops.append(jnp.max(top, axis=1, keepdims=True))
-    for part in range(PARTS):
-        begin = part * n_part
-        total = jnp.zeros((H_DEV * ROWS, 128), F32)
+    tops.append(jnp.max(top, axis=0, keepdims=True))
+    for n, (a, b) in enumerate(spans):
+        total = jnp.zeros((8, width), F32)
         top = lowest
-        for first in range(begin, begin + n_part, CHUNK):
-            if part + 1 < PARTS:
-                top = score(first + n_part, top)
-            total = weigh(first, tops[part], total)
-        if part + 1 < PARTS:
-            tops.append(jnp.max(top, axis=1, keepdims=True))
-        totals.append(jnp.sum(total, axis=1, keepdims=True))
-        accs.append(dot(p_ref[:, begin : begin + n_part], k_ref[begin : begin + n_part, :KVR]))
+        now = list(range(a, b, CHUNK))
+        later = []
+        if n + 1 < len(spans):
+            copies[n + 1].wait()
+            later = list(range(spans[n + 1][0], spans[n + 1][1], CHUNK))
+        while now or later:
+            if later:
+                top = score(later.pop(0), top)
+            if now:
+                total = weigh(now.pop(0), tops[n], total)
+        if n + 1 < len(spans):
+            tops.append(jnp.max(top, axis=0, keepdims=True))
+        totals.append(jnp.sum(total, axis=0, keepdims=True))
+        accs.append(tn_dot(p_ref[a:b, :], k_ref[a:b, :KVR]))
     top = tops[0]
     for t in tops[1:]:
         top = jnp.maximum(top, t)
     acc, total = 0.0, 0.0
     for a, t, l in zip(accs, tops, totals):
         f = jnp.exp2((t - top) * COEF)
-        acc = acc + f * a
+        acc = acc + a * f.reshape(width, 1)
         total = total + f * l
     acc = acc.astype(BF)
-    heads = [slice(h * ROWS, (h + 1) * ROWS) for h in range(H_DEV)]
-    for h, rows in enumerate(heads):
-        out_ref[:, h * VD : (h + 1) * VD] = dot(acc[rows], vue_ref[h]).astype(BF)
-    tail = with_stats([top[rows] for rows in heads], [total[rows] for rows in heads], ROWS)
-    out_ref[:, H_DEV * VD :] = tail.astype(BF)
+    line = lax.broadcasted_iota(jnp.int32, (128, rows), 0)
+    tail = jnp.zeros((128, rows), F32)
+    for h in range(H_DEV):
+        own = slice(h * rows, (h + 1) * rows)
+        out_ref[:, h * VD : (h + 1) * VD] = dot(acc[own], vue_ref[h]).astype(BF)
+        for k, row in enumerate(pieces(top[:, own], 3) + pieces(total[:, own], 2)):
+            tail = jnp.where(line == 8 * h + k, row, tail)
+    out_ref[:, H_DEV * VD :] = tail.T.astype(BF)
 
 
 def merge(parts, tails):
@@ -173,15 +191,16 @@
 
 
 def project(in_ref, w_ref, out_ref):
+    groups = in_ref.shape[0] // 2
     data = [
-        jnp.concatenate(
-            [in_ref[x * 4 + z * 2 + c].astype(F32) for x in range(4) for c in range(2)], axis=0
-        )
+        jnp.concatenate([in_ref[2 * g + z].astype(F32) for g in range(groups)], axis=0)
         for z in range(2)
     ]
     nums, _, totals = merge([d[:, : H_DEV * VD] for d in data], [d[:, H_DEV * VD :] for d in data])
     value = jnp.concatenate([n / t for n, t in zip(nums, totals)], axis=1).astype(BF)
-    out_ref[...] = nt_dot(value, w_ref[...]).astype(BF)
+    res = nt_dot(value, w_ref[...])
+    order = [res[(c * 8 + xz) * 8 : (c * 8 + xz) * 8 + 8] for xz in range(8) for c in range(2)]
+    out_ref[...] = jnp.concatenate(order, axis=0).astype(BF)
 
 
 def call(kernel, out_shape, *args, scratch=(), spaces=None, limit=16):
@@ -196,10 +215,16 @@
     )(*args)
 
 
+def copies_to_all(copied):
+    got = lax.all_to_all(copied, "ctx", 0, 0, axis_index_groups=SAME_CORE)
+    return lax.all_gather(got, "ctx", axis=0, tiled=True, axis_index_groups=SAME_CHIP)
+
+
 def body(queries, w_uk, value_up_weight, w_out, kv_cache, blocks):
     n_ctx = lax.axis_size("ctx")
     n_blocks = kv_cache.shape[0]
-    q = lax.all_to_all(jnp.broadcast_to(queries[None], (n_ctx,) + queries.shape), "ctx", 0, 0)
+    own_rows = queries.shape[0]
+    q = copies_to_all(jnp.broadcast_to(queries[None], (n_ctx // 2,) + queries.shape))
     q = q.reshape(ROWS, -1)
 
     eye = jnp.broadcast_to(jnp.eye(ROPE, dtype=BF)[None], (H_DEV, ROPE, ROPE))
@@ -211,22 +236,24 @@
     second = jnp.concatenate([zero, both[:, 1]], axis=1)
     absorb = jnp.stack([first, second], axis=1).reshape(H_DEV, 256, WIDE)
 
-    offsets = blocks - lax.axis_index("ctx") * n_blocks
-    lane = jnp.arange(2 * n_blocks, dtype=jnp.int32) % n_blocks
-    present = jnp.any(offsets[:, :, None] == lane[None, None, :], axis=1)
+    picked = blocks.reshape(4, 2, 2, own_rows, -1).transpose(2, 0, 1, 3, 4).reshape(ROWS, -1)
+    offsets = picked - lax.axis_index("ctx") * n_blocks
+    key = jnp.arange(2 * n_blocks, dtype=jnp.int32) % n_blocks
+    present = jnp.any(offsets.T[None, :, :] == key[:, None, None], axis=1)
     bias = jnp.where(present, 0.0, NEG).astype(F32)
 
     keys = pltpu.with_memory_space_constraint(staged(kv_cache), pltpu.HBM)
+    width = H_DEV * ROWS
     parts = call(
         attend,
         jax.ShapeDtypeStruct((ROWS, WIDE), BF),
-        q, absorb, value_up_weight, bias, keys,
+        q, absorb.transpose(0, 2, 1), value_up_weight, bias, keys,
         scratch=[
-            pltpu.VMEM((H_DEV * ROWS, WIDE), BF),
-            pltpu.VMEM((H_DEV * ROWS, keys.shape[0]), F32),
-            pltpu.VMEM((H_DEV * ROWS, keys.shape[0]), BF),
+            pltpu.VMEM((WIDE, width), BF),
+            pltpu.VMEM((keys.shape[0], width), F32),
+            pltpu.VMEM((keys.shape[0], width), BF),
             pltpu.VMEM(keys.shape, BF),
-            pltpu.SemaphoreType.DMA((keys.shape[0] // CHUNK,)),
+            pltpu.SemaphoreType.DMA((len(PARTS),)),
         ],
         spaces=[pltpu.VMEM] * 4 + [pltpu.HBM],
         limit=40,
@@ -235,8 +262,8 @@
     parts = lax.all_to_all(
         parts.reshape(n_ctx // 2, own, WIDE), "ctx", 0, 0, axis_index_groups=SAME_HALF
     )
-    halves = call(merge_half, jax.ShapeDtypeStruct((n_ctx, own, WIDE), BF), parts)
-    halves = lax.all_to_all(halves, "ctx", 0, 0)
+    halves = call(merge_half, jax.ShapeDtypeStruct((n_ctx // 2, own, WIDE), BF), parts)
+    halves = copies_to_all(halves)
     partial = call(project, jax.ShapeDtypeStruct((ROWS, w_out.shape[1]), BF), halves, w_out.T)
     n_head = lax.axis_size("head")
     shares = lax.all_to_all(partial.reshape(n_head, ROWS // n_head, -1), "head", 0, 0)

time: 111 us -> 106 us (0.955)
  waiting for transfers between devices: 9.1 us -> 6 us
  local copies, waits for them, and re-layouts: 5.15 us -> 7.36 us
  blocking collectives: 63.5 us -> 61.6 us
  Pallas kernels: 12.5 us -> 10.8 us
    all_to_all x1, blocking collectives: 31.8 us -> 24.9 us  [body(): lax.all_to_all(partial.reshape(n_head, ROWS // n_head, -1), 'head', 0, 0)]
    all_gather x0 -> x2, blocking collectives: none -> 3.96 us  [copies_to_all(): lax.all_gather(got, 'ctx', axis=0, tiled=True, axis_index_groups=SAME_CHIP)]
    all_to_all x1, waiting for transfers between devices: 9.1 us -> 6 us  [copies_to_all(): got = lax.all_to_all(copied, 'ctx', 0, 0, axis_index_groups=SAME_CORE)]
    unnamed x10 -> x11, local copies, waits for them, and re-layouts: 3.4 us -> 5.42 us
    all_to_all x1, blocking collectives: 22.8 us -> 24.5 us  [copies_to_all(): got = lax.all_to_all(copied, 'ctx', 0, 0, axis_index_groups=SAME_CORE)]
    pallas_call x3, Pallas kernels: 10.8 us -> 9.24 us  [call(): pl.pallas_call(kernel, out_shape=out_shape, in_specs=[pl.BlockSpec(memory...]
  transfers between devices with their start and end apart: 1 -> 1, of which waited for: 1 -> 1; matrix products, arithmetic and copies ran while one was open for 2% -> 3% of each run, Pallas kernels for 1% -> 2%
where the time goes in v3:
time: 106 us
  blocking collectives  61.6 us (58%)
  starting transfers between devices  17.6 us (17%)
  Pallas kernels  10.8 us (10%)
  local copies, waits for them, and re-layouts  7.36 us (7%)
  waiting for transfers between devices  6 us (6%)
  other arithmetic  2.23 us (2%)
    all_to_all x1, blocking collectives, body(): lax.all_to_all(partial.reshape(n_head, ROWS // n_head, -1), 'head', 0, 0)  24.9 us
    all_to_all x1, blocking collectives, copies_to_all(): got = lax.all_to_all(copied, 'ctx', 0, 0, axis_index_groups=SAME_CORE)  24.5 us
    all_to_all x1, starting transfers between devices, copies_to_all(): got = lax.all_to_all(copied, 'ctx', 0, 0, axis_index_groups=SAME_CORE)  17.6 us
    pallas_call x3, Pallas kernels, call(): pl.pallas_call(kernel, out_shape=out_shape, in_specs=[pl.BlockSpec(memory...  9.24 us
    all_to_all x1, blocking collectives, body(): lax.all_to_all(parts.reshape(n_ctx // 2, own, WIDE), 'ctx', 0, 0, axis_in...  8.25 us
    all_to_all x1, waiting for transfers between devices, copies_to_all(): got = lax.all_to_all(copied, 'ctx', 0, 0, axis_index_groups=SAME_CORE)  6 us
    unnamed x11, local copies, waits for them, and re-layouts  5.42 us
    all_gather x2, blocking collectives, copies_to_all(): lax.all_gather(got, 'ctx', axis=0, tiled=True, axis_index_groups=SAME_CHIP)  3.96 us
  transfers between devices with their start and end apart: 1, of which 1 were waited for; matrix products, arithmetic and copies ran while one was open for 3% of the time, Pallas kernels for 2%

profile of v3, /device:TPU:8, one launch (start us, length us, event | category | flops | bytes accessed | tf_op | source)
XLA Modules:
  0.0 105.8 jit_solution(17313002871694695897)
XLA Ops:
  0.0 1.3 %broadcast_in_dim.10 = bf16[8,8,768]{2,1,0:T(8,128)(2,1)} broadcast(bf16[8,768]{1,0:T(8,128)(2,1)} %param.6), dimensions={1,2} | broadcast | bytes 110592 | tf_op jit(solution)/shard_map/broadcast_in_dim | solution.py:227
  1.3 17.6 %all-to-all-start = ((bf16[8,8,768]{2,1,0:T(8,128)(2,1)}), bf16[8,8,768]{2,1,0:T(8,128)(2,1)S(1)}, u32[]{:S(2)}, u32[]{:S(2)}) async-start(bf16[8,8,768]{2,1,0:T(8,128)(2,1)} %broadcast_in_dim.10), calls=%async_computation | async-start | bytes 196608 | tf_op jit(solution)/shard_map/all_to_all | solution.py:219
  18.9 0.8 copy.22
  19.8 0.1 copy.24
  19.9 1.1 %fusion.2 = bf16[4,192,640]{2,1,0:T(8,128)(2,1)S(1)} fusion(bf16[4,64,64]{2,1,0:T(8,128)(2,1)S(1)} %broadcast_in_dim.11, bf16[4,128,512]{2,1,0:T(8,128)(2,1)} %param.7), kind=kLoop, calls=%fused_computation.6 | loop fusion | flops 3932160 | bytes 1540096 | tf_op jit(solution)/shard_map/concatenate | solution.py:233
  21.0 0.1 fusion.4
  21.1 0.2 copy.25
  21.3 0.2 copy.26
  21.6 0.0 copy-start.1
  21.6 2.3 %copy-done.1 = bf16[64,36864]{1,0:T(8,128)(2,1)S(1)} copy-done((bf16[64,36864]{1,0:T(8,128)(2,1)S(1)}, bf16[64,36864]{1,0:T(8,128)(2,1)}, u32[]{:S(2)}) %copy-start.1) | copy-done | bytes 4718616
  23.9 1.6 %shard_map.64.k_hbm = bf16[4096,640]{1,0:T(8,128)(2,1)S(1)} custom-call(bf16[64,36864]{1,0:T(8,128)(2,1)S(1)} %copy-done.1), custom_call_target="tpu_custom_call" | custom-call | tf_op jit(solution)/shard_map/pallas_call | solution.py:80
  25.5 0.0 copy-start
  25.6 0.4 pad_bitcast_fusion
  25.9 0.0 copy-start.2
  25.9 0.1 pad_maximum_fusion
  26.1 1.8 %copy-done = bf16[4096,640]{1,0:T(8,128)(2,1)} copy-done((bf16[4096,640]{1,0:T(8,128)(2,1)}, bf16[4096,640]{1,0:T(8,128)(2,1)S(1)}, u32[]{:S(2)}) %copy-start) | copy-done | bytes 5242904
  27.8 0.3 compare_reduce_fusion
  28.1 6.0 %all-to-all-done = bf16[8,8,768]{2,1,0:T(8,128)(2,1)S(1)} async-done(((bf16[8,8,768]{2,1,0:T(8,128)(2,1)}), bf16[8,8,768]{2,1,0:T(8,128)(2,1)S(1)}, u32[]{:S(2)}, u32[]{:S(2)}) %all-to-all-start) | async-done | bytes 98336 | tf_op jit(solution)/shard_map/all_to_all | solution.py:219
  34.2 1.9 %all_gather.6 = bf16[16,8,768]{2,1,0:T(8,128)(2,1)S(1)} all-gather(bf16[8,8,768]{2,1,0:T(8,128)(2,1)S(1)} %all-to-all-done), channel_id=1, replica_groups={{0,32},{64,96},{128,160},{192,224},{256,288},{320,352},{384,416},{448,4..., dimensions={0}, use_global_device_ids=true | all-gather | bytes 294912 | tf_op jit(solution)/shard_map/all_gather | solution.py:220
  36.1 0.0 copy-done.2
  36.1 0.0 copy-start.3
  36.1 8.2 %shard_map.65 = bf16[128,640]{1,0:T(8,128)(2,1)S(1)} custom-call(bf16[128,768]{1,0:T(8,128)(2,1)S(1)} %bitcast.20, bf16[4,640,256]{2,1,0:T(8,128)(2,1)S(1)} %bitcast.19, bf16[4,512,128]{2,1,0:T(8,128)(2,1)S(1)} %copy-done.2, f32[128,128]{1,0:T(8,128)S(1)} %broadcast_select_fusion.bias_ref, bf16[4096,640]{1,0:T(8,128)(2,1)} %copy-done), custom_call_target="tpu_custom_call" | custom-call | tf_op jit(solution)/shard_map/pallas_call | solution.py:207
  44.3 8.3 %all_to_all.20.in_ref = bf16[8,16,640]{2,1,0:T(8,128)(2,1)S(1)} all-to-all(bf16[8,16,640]{2,1,0:T(8,128)(2,1)S(1)} %bitcast.21), channel_id=1, replica_groups={{0,128,256,384,32,160,288,416},{64,192,320,448,96,224,352,480},{1,129,2..., dimensions={0} | all-to-all | bytes 327680 | tf_op jit(solution)/shard_map/all_to_all | solution.py:262
  52.6 0.4 shard_map.66
  52.9 24.5 %all_to_all.21 = bf16[8,16,640]{2,1,0:T(8,128)(2,1)S(1)} all-to-all(bf16[8,16,640]{2,1,0:T(8,128)(2,1)S(1)} %shard_map.66), channel_id=1, replica_groups={{0,64,128,192,256,320,384,448},{32,96,160,224,288,352,416,480},{1,65,12..., dimensions={0} | all-to-all | bytes 327680 | tf_op jit(solution)/shard_map/all_to_all | solution.py:219
  77.5 2.0 %all_gather.7.in_ref = bf16[16,16,640]{2,1,0:T(8,128)(2,1)S(1)} all-gather(bf16[8,16,640]{2,1,0:T(8,128)(2,1)S(1)} %all_to_all.21), channel_id=1, replica_groups={{0,32},{64,96},{128,160},{192,224},{256,288},{320,352},{384,416},{448,4..., dimensions={0}, use_global_device_ids=true | all-gather | bytes 491520 | tf_op jit(solution)/shard_map/all_gather | solution.py:220
  79.5 0.0 copy-done.3
  79.5 0.7 shard_map.67
  80.2 0.1 reshape.44
  80.2 24.9 %all_to_all.22 = bf16[32,4,448]{2,1,0:T(4,128)(2,1)S(1)} all-to-all(bf16[32,4,448]{2,1,0:T(4,128)(2,1)S(1)} %reshape.44), channel_id=1, replica_groups=mesh['ctx'=16,'head'=32] {'head'}, dimensions={0} | all-to-all | bytes 229376 | tf_op jit(solution)/shard_map/all_to_all | solution.py:269
  105.1 0.7 reduce_sum.12
  (6 shorter events, 0.1 us)
Async XLA Ops:
  1.3 32.8 %all-to-all-start = ((bf16[8,8,768]{2,1,0:T(8,128)(2,1)}), bf16[8,8,768]{2,1,0:T(8,128)(2,1)S(1)}, u32[]{:S(2)}, u32[]{:S(2)}) async-start(bf16[8,8,768]{2,1,0:T(8,128)(2,1)} %broadcast_in_dim.10), calls=%async_computation | async-start | bytes 196608 | tf_op jit(solution)/shard_map/all_to_all | solution.py:219
  21.6 2.3 %copy-start.1 = (bf16[64,36864]{1,0:T(8,128)(2,1)S(1)}, bf16[64,36864]{1,0:T(8,128)(2,1)}, u32[]{:S(2)}) copy-start(bf16[64,36864]{1,0:T(8,128)(2,1)} %kv_ref.1) | copy-start | bytes 14155780
  25.5 2.3 %copy-start = (bf16[4096,640]{1,0:T(8,128)(2,1)}, bf16[4096,640]{1,0:T(8,128)(2,1)S(1)}, u32[]{:S(2)}) copy-start(bf16[4096,640]{1,0:T(8,128)(2,1)S(1)} %shard_map.64.k_hbm) | copy-start | bytes 15728644
  25.9 10.2 %copy-start.2 = (bf16[4,512,128]{2,1,0:T(8,128)(2,1)S(1)}, bf16[4,512,128]{2,1,0:T(8,128)(2,1)}, u32[]{:S(2)}) copy-start(bf16[4,512,128]{2,1,0:T(8,128)(2,1)} %vue_ref.1) | copy-start | bytes 1572868
  36.1 43.4 %copy-start.3 = (bf16[512,448]{0,1:T(8,128)(2,1)S(1)}, bf16[512,448]{0,1:T(8,128)(2,1)}, u32[]{:S(2)}) copy-start(bf16[512,448]{0,1:T(8,128)(2,1)} %param.9) | copy-start | bytes 1376260

commit v4 on v3

--- a/solution.py
+++ b/solution.py
@@ -67,28 +67,55 @@
     return top, t[:, 3:4] + t[:, 4:5]
 
 
-def stage(kv_ref, out_ref):
-    rows = kv_ref.shape[0]
+def in_hbm(x):
+    return pltpu.with_memory_space_constraint(x, pltpu.HBM)
+
+
+def stage(kv_ref, blocks_ref, shard_ref, out_ref, bias_ref):
+    count = kv_ref.shape[0]
     keys = [kv_ref[:, t * PAIR : (t + 1) * PAIR][:, o : o + KEY] for t in range(QUAD) for o in (0, KEY)]
-    pad = jnp.zeros((rows, WIDE - KEY), BF)
+    pad = jnp.zeros((count, WIDE - KEY), BF)
     out_ref[...] = jnp.concatenate([jnp.concatenate([k, pad], axis=1) for k in keys], axis=0)
 
-
-def staged(kv):
+    @pl.when(pl.program_id(0) == 0)
+    def _():
+        b = blocks_ref[...]
+        n = ROWS // 16
+        order = [xz * 2 + c for c in range(2) for xz in range(8)]
+        b = jnp.concatenate([b[:, k * n : (k + 1) * n] for k in order], axis=1)
+        b = b - shard_ref[0] * count
+        line = lax.broadcasted_iota(jnp.int32, (count, ROWS), 0)
+        bias = jnp.full((count, ROWS), NEG, F32)
+        for k in range(b.shape[0]):
+            bias = jnp.where(b[k : k + 1, :] == line, 0.0, bias)
+        bias_ref[...] = jnp.concatenate([bias, bias], axis=0)
+
+
+def staged(kv, blocks, shard):
     steps = kv.shape[1] // (PAIR * QUAD)
     chunk = kv.shape[0] * 2 * QUAD
     return pl.pallas_call(
         stage,
         grid=(steps,),
-        out_shape=jax.ShapeDtypeStruct((steps * chunk, WIDE), BF),
-        in_specs=[pl.BlockSpec((kv.shape[0], PAIR * QUAD), lambda i: (0, i))],
-        out_specs=pl.BlockSpec((chunk, WIDE), lambda i: (i, 0)),
+        out_shape=(
+            pltpu.HBM((steps * chunk, WIDE), BF),
+            jax.ShapeDtypeStruct((2 * kv.shape[0], ROWS), F32),
+        ),
+        in_specs=[
+            pl.BlockSpec((kv.shape[0], PAIR * QUAD), lambda i: (0, i)),
+            pl.BlockSpec(blocks.shape, lambda i: (0, 0)),
+            pl.BlockSpec(memory_space=pltpu.SMEM),
+        ],
+        out_specs=(
+            pl.BlockSpec((chunk, WIDE), lambda i: (i, 0)),
+            pl.BlockSpec((2 * kv.shape[0], ROWS), lambda i: (0, 0)),
+        ),
         compiler_params=pltpu.CompilerParams(vmem_limit_bytes=16 * 2**20),
         interpret=INTERPRET,
-    )(kv)
-
-
-def attend(q_ref, wt_ref, vue_ref, bias_ref, k_hbm, out_ref, qt, s_ref, p_ref, k_ref, sems):
+    )(in_hbm(kv), blocks, shard)
+
+
+def attend(q_ref, w_ref, vue_ref, bias_ref, k_hbm, out_ref, qt, s_ref, p_ref, k_ref, sems):
     width = qt.shape[1]
     rows = width // H_DEV
     bounds = [0]
@@ -100,10 +127,15 @@
         span = pl.ds(a, b - a)
         copies.append(pltpu.make_async_copy(k_hbm.at[span], k_ref.at[span], sems.at[n]))
         copies[-1].start()
-    for h in range(H_DEV):
-        start = (h // 2) * 384 + (h % 2) * 128
-        q = q_ref[:, start : start + 256]
-        qt[:, h * rows : (h + 1) * rows] = nt_dot(wt_ref[h], q).astype(BF)
+    qt[KEY:, :] = jnp.zeros((WIDE - KEY, width), BF)
+    for h in range(H_DEV):
+        own = slice(h * rows, (h + 1) * rows)
+        q = q_ref[:, h * (NOPE + ROPE) : (h + 1) * (NOPE + ROPE)]
+        absorbed = lax.dot_general(
+            w_ref[h], q[:, :NOPE], (((0,), (1,)), ((), ())), preferred_element_type=F32
+        )
+        qt[:KVR, own] = absorbed.astype(BF)
+        qt[KVR:KEY, own] = q[:, NOPE:].T
 
     def score(first, top):
         s = dot(k_ref[first : first + CHUNK, :], qt[...])
@@ -185,20 +217,19 @@
     n, rows, _ = in_ref.shape
     data = [in_ref[s].astype(F32) for s in range(n)]
     nums, tops, totals = merge([d[:, : H_DEV * VD] for d in data], [d[:, H_DEV * VD :] for d in data])
-    whole = jnp.concatenate(nums + [with_stats(tops, totals, rows)], axis=1).astype(BF)
-    for k in range(out_ref.shape[0]):
-        out_ref[k] = whole
-
-
-def project(in_ref, w_ref, out_ref):
-    groups = in_ref.shape[0] // 2
-    data = [
-        jnp.concatenate([in_ref[2 * g + z].astype(F32) for g in range(groups)], axis=0)
-        for z in range(2)
-    ]
+    out_ref[...] = jnp.concatenate(nums + [with_stats(tops, totals, rows)], axis=1).astype(BF)
+
+
+def merge_all(own_ref, other_ref, out_ref):
+    data = [own_ref[...].astype(F32), other_ref[...].astype(F32)]
     nums, _, totals = merge([d[:, : H_DEV * VD] for d in data], [d[:, H_DEV * VD :] for d in data])
     value = jnp.concatenate([n / t for n, t in zip(nums, totals)], axis=1).astype(BF)
-    res = nt_dot(value, w_ref[...])
+    for k in range(out_ref.shape[0]):
+        out_ref[k] = value
+
+
+def project(value_ref, w_ref, out_ref):
+    res = nt_dot(value_ref[...], w_ref[...])
     order = [res[(c * 8 + xz) * 8 : (c * 8 + xz) * 8 + 8] for xz in range(8) for c in range(2)]
     out_ref[...] = jnp.concatenate(order, axis=0).astype(BF)
 
@@ -215,39 +246,18 @@
     )(*args)
 
 
-def copies_to_all(copied):
-    got = lax.all_to_all(copied, "ctx", 0, 0, axis_index_groups=SAME_CORE)
-    return lax.all_gather(got, "ctx", axis=0, tiled=True, axis_index_groups=SAME_CHIP)
-
-
 def body(queries, w_uk, value_up_weight, w_out, kv_cache, blocks):
     n_ctx = lax.axis_size("ctx")
-    n_blocks = kv_cache.shape[0]
-    own_rows = queries.shape[0]
-    q = copies_to_all(jnp.broadcast_to(queries[None], (n_ctx // 2,) + queries.shape))
+    q = jnp.broadcast_to(queries[None], (n_ctx // 2,) + queries.shape)
+    q = lax.all_to_all(q, "ctx", 0, 0, axis_index_groups=SAME_CORE)
+    q = lax.all_gather(q, "ctx", axis=0, tiled=True, axis_index_groups=SAME_CHIP)
     q = q.reshape(ROWS, -1)
-
-    eye = jnp.broadcast_to(jnp.eye(ROPE, dtype=BF)[None], (H_DEV, ROPE, ROPE))
-    nope = jnp.pad(w_uk, ((0, 0), (0, 0), (0, WIDE - KVR)))
-    rope = jnp.pad(eye, ((0, 0), (0, 0), (KVR, WIDE - KVR - ROPE)))
-    both = jnp.concatenate([nope, rope], axis=1).reshape(H_DEV // 2, 2, NOPE + ROPE, WIDE)
-    zero = jnp.zeros_like(both[:, 0, :ROPE])
-    first = jnp.concatenate([both[:, 0], zero], axis=1)
-    second = jnp.concatenate([zero, both[:, 1]], axis=1)
-    absorb = jnp.stack([first, second], axis=1).reshape(H_DEV, 256, WIDE)
-
-    picked = blocks.reshape(4, 2, 2, own_rows, -1).transpose(2, 0, 1, 3, 4).reshape(ROWS, -1)
-    offsets = picked - lax.axis_index("ctx") * n_blocks
-    key = jnp.arange(2 * n_blocks, dtype=jnp.int32) % n_blocks
-    present = jnp.any(offsets.T[None, :, :] == key[:, None, None], axis=1)
-    bias = jnp.where(present, 0.0, NEG).astype(F32)
-
-    keys = pltpu.with_memory_space_constraint(staged(kv_cache), pltpu.HBM)
+    keys, bias = staged(kv_cache, blocks.T, lax.axis_index("ctx").reshape(1))
     width = H_DEV * ROWS
     parts = call(
         attend,
         jax.ShapeDtypeStruct((ROWS, WIDE), BF),
-        q, absorb.transpose(0, 2, 1), value_up_weight, bias, keys,
+        q, w_uk, value_up_weight, bias, in_hbm(keys),
         scratch=[
             pltpu.VMEM((WIDE, width), BF),
             pltpu.VMEM((keys.shape[0], width), F32),
@@ -262,9 +272,11 @@
     parts = lax.all_to_all(
         parts.reshape(n_ctx // 2, own, WIDE), "ctx", 0, 0, axis_index_groups=SAME_HALF
     )
-    halves = call(merge_half, jax.ShapeDtypeStruct((n_ctx // 2, own, WIDE), BF), parts)
-    halves = copies_to_all(halves)
-    partial = call(project, jax.ShapeDtypeStruct((ROWS, w_out.shape[1]), BF), halves, w_out.T)
+    half = call(merge_half, jax.ShapeDtypeStruct((own, WIDE), BF), parts)
+    other = lax.ppermute(half, "ctx", [(i, i ^ 2) for i in range(n_ctx)])
+    value = call(merge_all, jax.ShapeDtypeStruct((n_ctx // 2, own, H_DEV * VD), BF), half, other)
+    value = lax.all_to_all(value, "ctx", 0, 0, axis_index_groups=SAME_HALF).reshape(ROWS, -1)
+    partial = call(project, jax.ShapeDtypeStruct((ROWS, w_out.shape[1]), BF), value, w_out.T)
     n_head = lax.axis_size("head")
     shares = lax.all_to_all(partial.reshape(n_head, ROWS // n_head, -1), "head", 0, 0)
     return jnp.sum(shares.astype(F32), axis=0).astype(BF)

time: 106 us -> 99.5 us (0.939)
  the two profiles are of different devices: /device:TPU:8 before, /device:TPU:2 now
where the time goes in v4:
time: 99.5 us; the launch traced here: 99 us
  blocking collectives  41.5 us (42%)
  starting transfers between devices  25.5 us (26%)
  Pallas kernels  16.7 us (17%)
  waiting for transfers between devices  12.3 us (12%)
  local copies, waits for them, and re-layouts  2.2 us (2%)
    all_to_all x1, blocking collectives, body(): lax.all_to_all(partial.reshape(n_head, ROWS // n_head, -1), 'head', 0, 0)  22.4 us
    all_to_all x1, starting transfers between devices, body(): q = lax.all_to_all(q, 'ctx', 0, 0, axis_index_groups=SAME_CORE)  18.1 us
    pallas_call x4, Pallas kernels, call(): pl.pallas_call(kernel, out_shape=out_shape, in_specs=[pl.BlockSpec(memory...  9.09 us
    all_to_all x1, blocking collectives, body(): lax.all_to_all(parts.reshape(n_ctx // 2, own, WIDE), 'ctx', 0, 0, axis_in...  8.75 us
    all_to_all x1, blocking collectives, body(): lax.all_to_all(value, 'ctx', 0, 0, axis_index_groups=SAME_HALF)  8.4 us
    pallas_call x1, Pallas kernels, staged(): pl.pallas_call(stage, grid=(steps,), out_shape=(pltpu.HBM((steps * chunk,...  7.62 us
    ppermute x1, starting transfers between devices, body(): other = lax.ppermute(half, 'ctx', [(i, i ^ 2) for i in range(n_ctx)])  7.4 us
    ppermute x1, waiting for transfers between devices, body(): other = lax.ppermute(half, 'ctx', [(i, i ^ 2) for i in range(n_ctx)])  7 us
  transfers between devices with their start and end apart: 2, of which 2 were waited for; matrix products, arithmetic and copies ran while one was open for 0% of the time, Pallas kernels for 8%

profile of v4, /device:TPU:2, one launch (start us, length us, event | category | flops | bytes accessed | tf_op | source)
XLA Modules:
  0.0 99.0 jit_solution(7002280494340724351)
XLA Ops:
  0.0 0.0 copy-start.1
  0.0 0.0 copy-start
  0.0 1.4 %broadcast_in_dim.2 = bf16[8,8,768]{2,1,0:T(8,128)(2,1)} broadcast(bf16[8,768]{1,0:T(8,128)(2,1)} %param.6), dimensions={1,2} | broadcast | bytes 110592 | tf_op jit(solution)/shard_map/broadcast_in_dim | solution.py:251
  1.4 18.1 %all-to-all-start = ((bf16[8,8,768]{2,1,0:T(8,128)(2,1)}), bf16[8,8,768]{2,1,0:T(8,128)(2,1)S(1)}, u32[]{:S(2)}, u32[]{:S(2)}) async-start(bf16[8,8,768]{2,1,0:T(8,128)(2,1)} %broadcast_in_dim.2), calls=%async_computation | async-start | bytes 196608 | tf_op jit(solution)/shard_map/all_to_all | solution.py:252
  19.5 0.0 copy-start.3
  19.5 0.7 copy-done.3
  20.2 0.0 copy-start.2
  20.2 7.6 %shard_map.64 = (bf16[4096,640]{1,0:T(8,128)(2,1)}, f32[128,128]{1,0:T(8,128)S(1)}) custom-call(bf16[64,36864]{1,0:T(8,128)(2,1)} %kv_ref.1, s32[32,128]{1,0:T(8,128)S(1)} %bitcast.10, s32[1]{0:T(128)} %bitcast.2.shard_ref), custom_call_target="tpu_custom_call" | custom-call | tf_op jit(solution)/shard_map/pallas_call | solution.py:97
  27.9 5.4 %all-to-all-done = bf16[8,8,768]{2,1,0:T(8,128)(2,1)S(1)} async-done(((bf16[8,8,768]{2,1,0:T(8,128)(2,1)}), bf16[8,8,768]{2,1,0:T(8,128)(2,1)S(1)}, u32[]{:S(2)}, u32[]{:S(2)}) %all-to-all-start) | async-done | bytes 98336 | tf_op jit(solution)/shard_map/all_to_all | solution.py:252
  33.2 1.9 %all_gather.3 = bf16[16,8,768]{2,1,0:T(8,128)(2,1)S(1)} all-gather(bf16[8,8,768]{2,1,0:T(8,128)(2,1)S(1)} %all-to-all-done), channel_id=1, replica_groups={{0,32},{64,96},{128,160},{192,224},{256,288},{320,352},{384,416},{448,4..., dimensions={0}, use_global_device_ids=true | all-gather | bytes 294912 | tf_op jit(solution)/shard_map/all_gather | solution.py:253
  35.1 0.0 copy-done.1
  35.1 0.0 copy-done
  35.1 8.1 %shard_map.65 = bf16[128,640]{1,0:T(8,128)(2,1)S(1)} custom-call(bf16[128,768]{1,0:T(8,128)(2,1)S(1)} %bitcast.6, bf16[4,128,512]{2,1,0:T(8,128)(2,1)S(1)} %copy-done, bf16[4,512,128]{2,1,0:T(8,128)(2,1)S(1)} %copy-done.1, f32[128,128]{1,0:T(8,128)S(1)} %get-tuple-element.7.bias_ref, bf16[4096,640]{1,0:T(8,128)(2,1)} %get-tuple-element.8.k_hbm), custom_call_target="tpu_custom_call" | custom-call | tf_op jit(solution)/shard_map/pallas_call | solution.py:238
  43.3 8.8 %all_to_all.20.in_ref = bf16[8,16,640]{2,1,0:T(8,128)(2,1)S(1)} all-to-all(bf16[8,16,640]{2,1,0:T(8,128)(2,1)S(1)} %bitcast.7), channel_id=1, replica_groups={{0,128,256,384,32,160,288,416},{64,192,320,448,96,224,352,480},{1,129,2..., dimensions={0} | all-to-all | bytes 327680 | tf_op jit(solution)/shard_map/all_to_all | solution.py:272
  52.0 0.4 shard_map.66.own_ref
  52.4 7.4 %collective-permute-start = (bf16[16,640]{1,0:T(8,128)(2,1)S(1)}, bf16[16,640]{1,0:T(8,128)(2,1)S(1)}, u32[]{:S(2)}, u32[]{:S(2)}) collective-permute-start(bf16[16,640]{1,0:T(8,128)(2,1)S(1)} %shard_map.66.own_ref), channel_id=1, source_target_pairs={{0,64},{32,96},{64,0},{96,32},{128,192},{160,224},{192,128},{224,1... | collective-permute-start | bytes 61448 | tf_op jit(solution)/shard_map/ppermute | solution.py:276
  59.8 7.0 %collective-permute-done.other_ref = bf16[16,640]{1,0:T(8,128)(2,1)S(1)} collective-permute-done((bf16[16,640]{1,0:T(8,128)(2,1)S(1)}, bf16[16,640]{1,0:T(8,128)(2,1)S(1)}, u32[]{:S(2)}, u32[]{:S(2)}) %collective-permute-start) | collective-permute-done | bytes 20512 | tf_op jit(solution)/shard_map/ppermute | solution.py:276
  66.8 0.3 shard_map.67
  67.1 8.4 %all_to_all.21 = bf16[8,16,512]{2,1,0:T(8,128)(2,1)S(1)} all-to-all(bf16[8,16,512]{2,1,0:T(8,128)(2,1)S(1)} %shard_map.67), channel_id=1, replica_groups={{0,128,256,384,32,160,288,416},{64,192,320,448,96,224,352,480},{1,129,2..., dimensions={0} | all-to-all | bytes 262144 | tf_op jit(solution)/shard_map/all_to_all | solution.py:278
  75.5 0.0 copy-done.2
  75.5 0.3 shard_map.68
  75.9 22.4 %all_to_all.22 = bf16[32,4,448]{2,1,0:T(4,128)(2,1)S(1)} all-to-all(bf16[32,4,448]{2,1,0:T(4,128)(2,1)S(1)} %reshape.20), channel_id=1, replica_groups=mesh['ctx'=16,'head'=32] {'head'}, dimensions={0} | all-to-all | bytes 229376 | tf_op jit(solution)/shard_map/all_to_all | solution.py:281
  98.3 0.7 reduce_sum.12
  (1 shorter events, 0.0 us)
Async XLA Ops:
  0.0 35.1 %copy-start.1 = (bf16[4,512,128]{2,1,0:T(8,128)(2,1)S(1)}, bf16[4,512,128]{2,1,0:T(8,128)(2,1)}, u32[]{:S(2)}) copy-start(bf16[4,512,128]{2,1,0:T(8,128)(2,1)} %vue_ref.1) | copy-start | bytes 1572868
  0.0 35.1 %copy-start = (bf16[4,128,512]{2,1,0:T(8,128)(2,1)S(1)}, bf16[4,128,512]{2,1,0:T(8,128)(2,1)}, u32[]{:S(2)}) copy-start(bf16[4,128,512]{2,1,0:T(8,128)(2,1)} %w_ref.1) | copy-start | bytes 1572868
  1.4 31.8 %all-to-all-start = ((bf16[8,8,768]{2,1,0:T(8,128)(2,1)}), bf16[8,8,768]{2,1,0:T(8,128)(2,1)S(1)}, u32[]{:S(2)}, u32[]{:S(2)}) async-start(bf16[8,8,768]{2,1,0:T(8,128)(2,1)} %broadcast_in_dim.2), calls=%async_computation | async-start | bytes 196608 | tf_op jit(solution)/shard_map/all_to_all | solution.py:252
  19.5 0.7 copy-start.3
  20.2 55.3 %copy-start.2 = (bf16[512,448]{0,1:T(8,128)(2,1)S(1)}, bf16[512,448]{0,1:T(8,128)(2,1)}, u32[]{:S(2)}) copy-start(bf16[512,448]{0,1:T(8,128)(2,1)} %param.9) | copy-start | bytes 1376260
  52.4 14.4 %collective-permute-start = (bf16[16,640]{1,0:T(8,128)(2,1)S(1)}, bf16[16,640]{1,0:T(8,128)(2,1)S(1)}, u32[]{:S(2)}, u32[]{:S(2)}) collective-permute-start(bf16[16,640]{1,0:T(8,128)(2,1)S(1)} %shard_map.66.own_ref), channel_id=1, source_target_pairs={{0,64},{32,96},{64,0},{96,32},{128,192},{160,224},{192,128},{224,1... | collective-permute-start | bytes 61448 | tf_op jit(solution)/shard_map/ppermute | solution.py:276

commit v5 on v4

--- a/solution.py
+++ b/solution.py
@@ -18,9 +18,9 @@
 BLOCK = 64
 WIDE = 640
 PAIR = 1152
-PARTS = (0.25, 0.375, 0.375)
-CHUNK = 512
-QUAD = 4
+PARTS = (0.125, 0.25, 0.3125, 0.3125)
+CHUNK = 256
+STAGE_PAIRS = 4
 COEF = float((NOPE + ROPE) ** -0.5 * np.log2(np.e))
 INTERPRET = False
 KEY = KVR + ROPE
@@ -71,48 +71,68 @@
     return pltpu.with_memory_space_constraint(x, pltpu.HBM)
 
 
-def stage(kv_ref, blocks_ref, shard_ref, out_ref, bias_ref):
-    count = kv_ref.shape[0]
-    keys = [kv_ref[:, t * PAIR : (t + 1) * PAIR][:, o : o + KEY] for t in range(QUAD) for o in (0, KEY)]
+def stage(kv_hbm, blocks_hbm, shard_ref, out_hbm, bias_ref, kv_ref, blocks_ref, keys_ref, sems, sent):
+    count, lanes = kv_ref.shape
+    span = STAGE_PAIRS * PAIR
+    chunk = STAGE_PAIRS * 2 * count
+    steps = lanes // span
+    got = []
+    for i in range(steps):
+        at = pl.ds(i * span, span)
+        got.append(pltpu.make_async_copy(kv_hbm.at[:, at], kv_ref.at[:, at], sems.at[i]))
+        got[-1].start()
+    table = pltpu.make_async_copy(blocks_hbm, blocks_ref, sems.at[steps])
+    table.start()
     pad = jnp.zeros((count, WIDE - KEY), BF)
-    out_ref[...] = jnp.concatenate([jnp.concatenate([k, pad], axis=1) for k in keys], axis=0)
-
-    @pl.when(pl.program_id(0) == 0)
-    def _():
-        b = blocks_ref[...]
-        n = ROWS // 16
-        order = [xz * 2 + c for c in range(2) for xz in range(8)]
-        b = jnp.concatenate([b[:, k * n : (k + 1) * n] for k in order], axis=1)
-        b = b - shard_ref[0] * count
-        line = lax.broadcasted_iota(jnp.int32, (count, ROWS), 0)
-        bias = jnp.full((count, ROWS), NEG, F32)
-        for k in range(b.shape[0]):
-            bias = jnp.where(b[k : k + 1, :] == line, 0.0, bias)
-        bias_ref[...] = jnp.concatenate([bias, bias], axis=0)
+    put = []
+    for i in range(steps):
+        got[i].wait()
+        for t in range(STAGE_PAIRS):
+            pair = kv_ref[:, i * span + t * PAIR : i * span + (t + 1) * PAIR]
+            for o in range(2):
+                key = jnp.concatenate([pair[:, o * KEY : (o + 1) * KEY], pad], axis=1)
+                first = i * chunk + (2 * t + o) * count
+                keys_ref[first : first + count, :] = key
+        at = pl.ds(i * chunk, chunk)
+        put.append(pltpu.make_async_copy(keys_ref.at[at], out_hbm.at[at], sent.at[i]))
+        put[-1].start()
+    table.wait()
+    b = blocks_ref[...]
+    n = ROWS // 16
+    order = [xz * 2 + c for c in range(2) for xz in range(8)]
+    b = jnp.concatenate([b[:, k * n : (k + 1) * n] for k in order], axis=1)
+    b = b - shard_ref[0] * count
+    line = lax.broadcasted_iota(jnp.int32, (count, ROWS), 0)
+    bias = jnp.full((count, ROWS), NEG, F32)
+    for k in range(b.shape[0]):
+        bias = jnp.where(b[k : k + 1, :] == line, 0.0, bias)
+    bias_ref[...] = jnp.concatenate([bias, bias], axis=0)
+    for copy in put:
+        copy.wait()
 
 
 def staged(kv, blocks, shard):
-    steps = kv.shape[1] // (PAIR * QUAD)
-    chunk = kv.shape[0] * 2 * QUAD
+    steps = kv.shape[1] // (PAIR * STAGE_PAIRS)
+    keys = (kv.shape[0] * kv.shape[1] // KEY, WIDE)
     return pl.pallas_call(
         stage,
-        grid=(steps,),
-        out_shape=(
-            pltpu.HBM((steps * chunk, WIDE), BF),
-            jax.ShapeDtypeStruct((2 * kv.shape[0], ROWS), F32),
-        ),
+        out_shape=(pltpu.HBM(keys, BF), jax.ShapeDtypeStruct((2 * kv.shape[0], ROWS), F32)),
         in_specs=[
-            pl.BlockSpec((kv.shape[0], PAIR * QUAD), lambda i: (0, i)),
-            pl.BlockSpec(blocks.shape, lambda i: (0, 0)),
+            pl.BlockSpec(memory_space=pltpu.HBM),
+            pl.BlockSpec(memory_space=pltpu.HBM),
             pl.BlockSpec(memory_space=pltpu.SMEM),
         ],
-        out_specs=(
-            pl.BlockSpec((chunk, WIDE), lambda i: (i, 0)),
-            pl.BlockSpec((2 * kv.shape[0], ROWS), lambda i: (0, 0)),
-        ),
-        compiler_params=pltpu.CompilerParams(vmem_limit_bytes=16 * 2**20),
+        out_specs=(pl.BlockSpec(memory_space=pltpu.HBM), pl.BlockSpec(memory_space=pltpu.VMEM)),
+        scratch_shapes=[
+            pltpu.VMEM(kv.shape, BF),
+            pltpu.VMEM(blocks.shape, jnp.int32),
+            pltpu.VMEM(keys, BF),
+            pltpu.SemaphoreType.DMA((steps + 1,)),
+            pltpu.SemaphoreType.DMA((steps,)),
+        ],
+        compiler_params=pltpu.CompilerParams(vmem_limit_bytes=24 * 2**20),
         interpret=INTERPRET,
-    )(in_hbm(kv), blocks, shard)
+    )(in_hbm(kv), in_hbm(blocks), shard)
 
 
 def attend(q_ref, w_ref, vue_ref, bias_ref, k_hbm, out_ref, qt, s_ref, p_ref, k_ref, sems):

time: 99.5 us -> 99.4 us (level)
  waiting for transfers between devices: 12.3 us -> 21.1 us
  starting transfers between devices: 25.5 us -> 21.2 us
  Pallas kernels: 16.7 us -> 12.9 us
    ppermute x1, waiting for transfers between devices: 7 us -> 11.4 us  [body(): other = lax.ppermute(half, 'ctx', [(i, i ^ 2) for i in range(n_ctx)])]
    all_to_all x1, waiting for transfers between devices: 5.35 us -> 9.69 us  [body(): q = lax.all_to_all(q, 'ctx', 0, 0, axis_index_groups=SAME_CORE)]
    ppermute x1, starting transfers between devices: 7.4 us -> 3.07 us  [body(): other = lax.ppermute(half, 'ctx', [(i, i ^ 2) for i in range(n_ctx)])]
    pallas_call x1, Pallas kernels: 7.62 us -> 3.99 us  [staged(): pl.pallas_call(stage, out_shape=(pltpu.HBM(keys, BF), jax.ShapeDtypeStruc...]
  transfers between devices with their start and end apart: 2 -> 2, of which waited for: 2 -> 2; matrix products, arithmetic and copies ran while one was open for 0% -> 0% of each run, Pallas kernels for 8% -> 4%
where the time goes in v5:
time: 99.4 us; the launch traced here: 98.9 us
  blocking collectives  41.6 us (42%)
  starting transfers between devices  21.2 us (21%)
  waiting for transfers between devices  21.1 us (21%)
  Pallas kernels  12.9 us (13%)
  local copies, waits for them, and re-layouts  1.49 us (1%)
    all_to_all x1, blocking collectives, body(): lax.all_to_all(partial.reshape(n_head, ROWS // n_head, -1), 'head', 0, 0)  22.5 us
    all_to_all x1, starting transfers between devices, body(): q = lax.all_to_all(q, 'ctx', 0, 0, axis_index_groups=SAME_CORE)  18.1 us
    ppermute x1, waiting for transfers between devices, body(): other = lax.ppermute(half, 'ctx', [(i, i ^ 2) for i in range(n_ctx)])  11.4 us
    all_to_all x1, waiting for transfers between devices, body(): q = lax.all_to_all(q, 'ctx', 0, 0, axis_index_groups=SAME_CORE)  9.69 us
    pallas_call x4, Pallas kernels, call(): pl.pallas_call(kernel, out_shape=out_shape, in_specs=[pl.BlockSpec(memory...  8.96 us
    all_to_all x1, blocking collectives, body(): lax.all_to_all(parts.reshape(n_ctx // 2, own, WIDE), 'ctx', 0, 0, axis_in...  8.76 us
    all_to_all x1, blocking collectives, body(): lax.all_to_all(value, 'ctx', 0, 0, axis_index_groups=SAME_HALF)  8.35 us
    pallas_call x1, Pallas kernels, staged(): pl.pallas_call(stage, out_shape=(pltpu.HBM(keys, BF), jax.ShapeDtypeStruc...  3.99 us
  transfers between devices with their start and end apart: 2, of which 2 were waited for; matrix products, arithmetic and copies ran while one was open for 0% of the time, Pallas kernels for 4%

profile of v5, /device:TPU:2, one launch (start us, length us, event | category | flops | bytes accessed | tf_op | source)
XLA Modules:
  0.0 98.9 jit_solution(9785056372320968506)
XLA Ops:
  0.0 0.0 copy-start.1
  0.0 0.0 copy-start
  0.0 1.4 %broadcast_in_dim.2 = bf16[8,8,768]{2,1,0:T(8,128)(2,1)} broadcast(bf16[8,768]{1,0:T(8,128)(2,1)} %param.6), dimensions={1,2} | broadcast | bytes 110592 | tf_op jit(solution)/shard_map/broadcast_in_dim | solution.py:271
  1.4 18.1 %all-to-all-start = ((bf16[8,8,768]{2,1,0:T(8,128)(2,1)}), bf16[8,8,768]{2,1,0:T(8,128)(2,1)S(1)}, u32[]{:S(2)}, u32[]{:S(2)}) async-start(bf16[8,8,768]{2,1,0:T(8,128)(2,1)} %broadcast_in_dim.2), calls=%async_computation | async-start | bytes 196608 | tf_op jit(solution)/shard_map/all_to_all | solution.py:272
  19.5 0.0 copy-start.2
  19.5 4.0 %shard_map.64 = (bf16[4096,640]{1,0:T(8,128)(2,1)}, f32[128,128]{1,0:T(8,128)S(1)}) custom-call(bf16[64,36864]{1,0:T(8,128)(2,1)} %kv_hbm.1, s32[32,128]{1,0:T(8,128)} %bitcast.10, s32[1]{0:T(128)} %bitcast.2.shard_ref), custom_call_target="tpu_custom_call" | custom-call | tf_op jit(solution)/shard_map/pallas_call | solution.py:117
  23.5 9.7 %all-to-all-done = bf16[8,8,768]{2,1,0:T(8,128)(2,1)S(1)} async-done(((bf16[8,8,768]{2,1,0:T(8,128)(2,1)}), bf16[8,8,768]{2,1,0:T(8,128)(2,1)S(1)}, u32[]{:S(2)}, u32[]{:S(2)}) %all-to-all-start) | async-done | bytes 98336 | tf_op jit(solution)/shard_map/all_to_all | solution.py:272
  33.2 1.9 %all_gather.3 = bf16[16,8,768]{2,1,0:T(8,128)(2,1)S(1)} all-gather(bf16[8,8,768]{2,1,0:T(8,128)(2,1)S(1)} %all-to-all-done), channel_id=1, replica_groups={{0,32},{64,96},{128,160},{192,224},{256,288},{320,352},{384,416},{448,4..., dimensions={0}, use_global_device_ids=true | all-gather | bytes 294912 | tf_op jit(solution)/shard_map/all_gather | solution.py:273
  35.1 0.0 copy-done.1
  35.2 0.0 copy-done
  35.2 8.0 %shard_map.65 = bf16[128,640]{1,0:T(8,128)(2,1)S(1)} custom-call(bf16[128,768]{1,0:T(8,128)(2,1)S(1)} %bitcast.6, bf16[4,128,512]{2,1,0:T(8,128)(2,1)S(1)} %copy-done, bf16[4,512,128]{2,1,0:T(8,128)(2,1)S(1)} %copy-done.1, f32[128,128]{1,0:T(8,128)S(1)} %get-tuple-element.7.bias_ref, bf16[4096,640]{1,0:T(8,128)(2,1)} %get-tuple-element.8.k_hbm), custom_call_target="tpu_custom_call" | custom-call | tf_op jit(solution)/shard_map/pallas_call | solution.py:258
  43.2 8.8 %all_to_all.20.in_ref = bf16[8,16,640]{2,1,0:T(8,128)(2,1)S(1)} all-to-all(bf16[8,16,640]{2,1,0:T(8,128)(2,1)S(1)} %bitcast.7), channel_id=1, replica_groups={{0,128,256,384,32,160,288,416},{64,192,320,448,96,224,352,480},{1,129,2..., dimensions={0} | all-to-all | bytes 327680 | tf_op jit(solution)/shard_map/all_to_all | solution.py:292
  51.9 0.4 shard_map.66.own_ref
  52.3 3.1 %collective-permute-start = (bf16[16,640]{1,0:T(8,128)(2,1)S(1)}, bf16[16,640]{1,0:T(8,128)(2,1)S(1)}, u32[]{:S(2)}, u32[]{:S(2)}) collective-permute-start(bf16[16,640]{1,0:T(8,128)(2,1)S(1)} %shard_map.66.own_ref), channel_id=1, source_target_pairs={{0,64},{32,96},{64,0},{96,32},{128,192},{160,224},{192,128},{224,1... | collective-permute-start | bytes 61448 | tf_op jit(solution)/shard_map/ppermute | solution.py:296
  55.4 11.4 %collective-permute-done.other_ref = bf16[16,640]{1,0:T(8,128)(2,1)S(1)} collective-permute-done((bf16[16,640]{1,0:T(8,128)(2,1)S(1)}, bf16[16,640]{1,0:T(8,128)(2,1)S(1)}, u32[]{:S(2)}, u32[]{:S(2)}) %collective-permute-start) | collective-permute-done | bytes 20512 | tf_op jit(solution)/shard_map/ppermute | solution.py:296
  66.8 0.3 shard_map.67
  67.1 8.3 %all_to_all.21 = bf16[8,16,512]{2,1,0:T(8,128)(2,1)S(1)} all-to-all(bf16[8,16,512]{2,1,0:T(8,128)(2,1)S(1)} %shard_map.67), channel_id=1, replica_groups={{0,128,256,384,32,160,288,416},{64,192,320,448,96,224,352,480},{1,129,2..., dimensions={0} | all-to-all | bytes 262144 | tf_op jit(solution)/shard_map/all_to_all | solution.py:298
  75.4 0.0 copy-done.2
  75.4 0.3 shard_map.68
  75.8 22.5 %all_to_all.22 = bf16[32,4,448]{2,1,0:T(4,128)(2,1)S(1)} all-to-all(bf16[32,4,448]{2,1,0:T(4,128)(2,1)S(1)} %reshape.20), channel_id=1, replica_groups=mesh['ctx'=16,'head'=32] {'head'}, dimensions={0} | all-to-all | bytes 229376 | tf_op jit(solution)/shard_map/all_to_all | solution.py:301
  98.3 0.7 reduce_sum.12
  (1 shorter events, 0.0 us)
Async XLA Ops:
  0.0 35.1 %copy-start.1 = (bf16[4,512,128]{2,1,0:T(8,128)(2,1)S(1)}, bf16[4,512,128]{2,1,0:T(8,128)(2,1)}, u32[]{:S(2)}) copy-start(bf16[4,512,128]{2,1,0:T(8,128)(2,1)} %vue_ref.1) | copy-start | bytes 1572868
  0.0 35.2 %copy-start = (bf16[4,128,512]{2,1,0:T(8,128)(2,1)S(1)}, bf16[4,128,512]{2,1,0:T(8,128)(2,1)}, u32[]{:S(2)}) copy-start(bf16[4,128,512]{2,1,0:T(8,128)(2,1)} %w_ref.1) | copy-start | bytes 1572868
  1.4 31.8 %all-to-all-start = ((bf16[8,8,768]{2,1,0:T(8,128)(2,1)}), bf16[8,8,768]{2,1,0:T(8,128)(2,1)S(1)}, u32[]{:S(2)}, u32[]{:S(2)}) async-start(bf16[8,8,768]{2,1,0:T(8,128)(2,1)} %broadcast_in_dim.2), calls=%async_computation | async-start | bytes 196608 | tf_op jit(solution)/shard_map/all_to_all | solution.py:272
  19.5 55.9 %copy-start.2 = (bf16[512,448]{0,1:T(8,128)(2,1)S(1)}, bf16[512,448]{0,1:T(8,128)(2,1)}, u32[]{:S(2)}) copy-start(bf16[512,448]{0,1:T(8,128)(2,1)} %param.9) | copy-start | bytes 1376260
  52.3 14.5 %collective-permute-start = (bf16[16,640]{1,0:T(8,128)(2,1)S(1)}, bf16[16,640]{1,0:T(8,128)(2,1)S(1)}, u32[]{:S(2)}, u32[]{:S(2)}) collective-permute-start(bf16[16,640]{1,0:T(8,128)(2,1)S(1)} %shard_map.66.own_ref), channel_id=1, source_target_pairs={{0,64},{32,96},{64,0},{96,32},{128,192},{160,224},{192,128},{224,1... | collective-permute-start | bytes 61448 | tf_op jit(solution)/shard_map/ppermute | solution.py:296

commit v6 on v5

--- a/solution.py
+++ b/solution.py
@@ -25,9 +25,8 @@
 INTERPRET = False
 KEY = KVR + ROPE
 
-SAME_CORE = [[x * 4 + z * 2 + c for x in range(4) for z in range(2)] for c in range(2)]
-SAME_CHIP = [[x * 4 + z * 2 + c for c in range(2)] for x in range(4) for z in range(2)]
 SAME_HALF = [[x * 4 + z * 2 + c for c in range(2) for x in range(4)] for z in range(2)]
+OTHER_HALF = [(i, i ^ 2) for i in range(16)]
 
 
 def nt_dot(a, b):
@@ -71,7 +70,9 @@
     return pltpu.with_memory_space_constraint(x, pltpu.HBM)
 
 
-def stage(kv_hbm, blocks_hbm, shard_ref, out_hbm, bias_ref, kv_ref, blocks_ref, keys_ref, sems, sent):
+def stage(
+    kv_hbm, blocks_hbm, shard_ref, out_hbm, near_ref, far_ref, kv_ref, blocks_ref, keys_ref, sems, sent
+):
     count, lanes = kv_ref.shape
     span = STAGE_PAIRS * PAIR
     chunk = STAGE_PAIRS * 2 * count
@@ -99,14 +100,20 @@
     table.wait()
     b = blocks_ref[...]
     n = ROWS // 16
-    order = [xz * 2 + c for c in range(2) for xz in range(8)]
+    order = [x * 4 + z * 2 + c for z in range(2) for c in range(2) for x in range(4)]
     b = jnp.concatenate([b[:, k * n : (k + 1) * n] for k in order], axis=1)
     b = b - shard_ref[0] * count
     line = lax.broadcasted_iota(jnp.int32, (count, ROWS), 0)
     bias = jnp.full((count, ROWS), NEG, F32)
     for k in range(b.shape[0]):
         bias = jnp.where(b[k : k + 1, :] == line, 0.0, bias)
-    bias_ref[...] = jnp.concatenate([bias, bias], axis=0)
+    halves = [
+        jnp.concatenate([jnp.concatenate([part] * H_DEV, axis=1)] * 2, axis=0)
+        for part in (bias[:, : ROWS // 2], bias[:, ROWS // 2 :])
+    ]
+    lower = shard_ref[1] == 0
+    near_ref[...] = jnp.where(lower, halves[0], halves[1])
+    far_ref[...] = jnp.where(lower, halves[1], halves[0])
     for copy in put:
         copy.wait()
 
@@ -114,15 +121,20 @@
 def staged(kv, blocks, shard):
     steps = kv.shape[1] // (PAIR * STAGE_PAIRS)
     keys = (kv.shape[0] * kv.shape[1] // KEY, WIDE)
+    bias = jax.ShapeDtypeStruct((2 * kv.shape[0], H_DEV * ROWS // 2), F32)
     return pl.pallas_call(
         stage,
-        out_shape=(pltpu.HBM(keys, BF), jax.ShapeDtypeStruct((2 * kv.shape[0], ROWS), F32)),
+        out_shape=(pltpu.HBM(keys, BF), bias, bias),
         in_specs=[
             pl.BlockSpec(memory_space=pltpu.HBM),
             pl.BlockSpec(memory_space=pltpu.HBM),
             pl.BlockSpec(memory_space=pltpu.SMEM),
         ],
-        out_specs=(pl.BlockSpec(memory_space=pltpu.HBM), pl.BlockSpec(memory_space=pltpu.VMEM)),
+        out_specs=(
+            pl.BlockSpec(memory_space=pltpu.HBM),
+            pl.BlockSpec(memory_space=pltpu.VMEM),
+            pl.BlockSpec(memory_space=pltpu.VMEM),
+        ),
         scratch_shapes=[
             pltpu.VMEM(kv.shape, BF),
             pltpu.VMEM(blocks.shape, jnp.int32),
@@ -135,7 +147,19 @@
     )(in_hbm(kv), in_hbm(blocks), shard)
 
 
-def attend(q_ref, w_ref, vue_ref, bias_ref, k_hbm, out_ref, qt, s_ref, p_ref, k_ref, sems):
+def attend_near(q_ref, w_ref, vue_ref, bias_ref, k_hbm, out_ref, *scratch):
+    out_ref[...] = attend(q_ref, w_ref, vue_ref, bias_ref, k_hbm, *scratch).astype(BF)
+
+
+def attend_far(q_ref, w_ref, vue_ref, bias_ref, near_ref, k_hbm, out_ref, *scratch):
+    far = attend(q_ref, w_ref, vue_ref, bias_ref, k_hbm, *scratch)
+    near = near_ref[...].astype(F32)
+    for k in range(out_ref.shape[0]):
+        rows = slice(k * 8, (k + 1) * 8)
+        out_ref[k] = jnp.concatenate([near[rows], far[rows]], axis=0).astype(BF)
+
+
+def attend(q_ref, w_ref, vue_ref, bias_ref, k_hbm, qt, s_ref, p_ref, k_ref, sems):
     width = qt.shape[1]
     rows = width // H_DEV
     bounds = [0]
@@ -147,20 +171,21 @@
         span = pl.ds(a, b - a)
         copies.append(pltpu.make_async_copy(k_hbm.at[span], k_ref.at[span], sems.at[n]))
         copies[-1].start()
-    qt[KEY:, :] = jnp.zeros((WIDE - KEY, width), BF)
+    columns = []
     for h in range(H_DEV):
-        own = slice(h * rows, (h + 1) * rows)
         q = q_ref[:, h * (NOPE + ROPE) : (h + 1) * (NOPE + ROPE)]
         absorbed = lax.dot_general(
             w_ref[h], q[:, :NOPE], (((0,), (1,)), ((), ())), preferred_element_type=F32
         )
-        qt[:KVR, own] = absorbed.astype(BF)
-        qt[KVR:KEY, own] = q[:, NOPE:].T
+        columns.append((absorbed, q[:, NOPE:].astype(F32).T))
+    qt[:KVR, :] = jnp.concatenate([a for a, _ in columns], axis=1).astype(BF)
+    qt[KVR:KEY, :] = jnp.concatenate([r for _, r in columns], axis=1).astype(BF)
+    qt[KEY:, :] = jnp.zeros((WIDE - KEY, width), BF)
 
     def score(first, top):
         s = dot(k_ref[first : first + CHUNK, :], qt[...])
         for at in range(0, CHUNK, 128):
-            piece = s[at : at + 128, :] + jnp.concatenate([bias_ref[...]] * H_DEV, axis=1)
+            piece = s[at : at + 128, :] + bias_ref[...]
             top = jnp.maximum(top, jnp.max(piece.reshape(16, 8, width), axis=0))
             s_ref[first + at : first + at + 128, :] = piece
         return top
@@ -207,12 +232,13 @@
     acc = acc.astype(BF)
     line = lax.broadcasted_iota(jnp.int32, (128, rows), 0)
     tail = jnp.zeros((128, rows), F32)
+    values = []
     for h in range(H_DEV):
         own = slice(h * rows, (h + 1) * rows)
-        out_ref[:, h * VD : (h + 1) * VD] = dot(acc[own], vue_ref[h]).astype(BF)
+        values.append(dot(acc[own], vue_ref[h]))
         for k, row in enumerate(pieces(top[:, own], 3) + pieces(total[:, own], 2)):
             tail = jnp.where(line == 8 * h + k, row, tail)
-    out_ref[:, H_DEV * VD :] = tail.T.astype(BF)
+    return jnp.concatenate(values + [tail.T], axis=1)
 
 
 def merge(parts, tails):
@@ -240,10 +266,14 @@
     out_ref[...] = jnp.concatenate(nums + [with_stats(tops, totals, rows)], axis=1).astype(BF)
 
 
-def merge_all(own_ref, other_ref, out_ref):
-    data = [own_ref[...].astype(F32), other_ref[...].astype(F32)]
+def merge_all(own_ref, other_ref, shard_ref, out_ref):
+    n = own_ref.shape[0] // 2
+    other = other_ref[...].astype(F32)
+    data = [own_ref[...].astype(F32), jnp.concatenate([other[n:], other[:n]], axis=0)]
     nums, _, totals = merge([d[:, : H_DEV * VD] for d in data], [d[:, H_DEV * VD :] for d in data])
-    value = jnp.concatenate([n / t for n, t in zip(nums, totals)], axis=1).astype(BF)
+    value = jnp.concatenate([a / t for a, t in zip(nums, totals)], axis=1)
+    swapped = jnp.concatenate([value[n:], value[:n]], axis=0)
+    value = jnp.where(shard_ref[1] == 0, value, swapped).astype(BF)
     for k in range(out_ref.shape[0]):
         out_ref[k] = value
 
@@ -268,33 +298,50 @@
 
 def body(queries, w_uk, value_up_weight, w_out, kv_cache, blocks):
     n_ctx = lax.axis_size("ctx")
-    q = jnp.broadcast_to(queries[None], (n_ctx // 2,) + queries.shape)
-    q = lax.all_to_all(q, "ctx", 0, 0, axis_index_groups=SAME_CORE)
-    q = lax.all_gather(q, "ctx", axis=0, tiled=True, axis_index_groups=SAME_CHIP)
-    q = q.reshape(ROWS, -1)
-    keys, bias = staged(kv_cache, blocks.T, lax.axis_index("ctx").reshape(1))
-    width = H_DEV * ROWS
-    parts = call(
-        attend,
-        jax.ShapeDtypeStruct((ROWS, WIDE), BF),
-        q, w_uk, value_up_weight, bias, in_hbm(keys),
-        scratch=[
-            pltpu.VMEM((WIDE, width), BF),
-            pltpu.VMEM((keys.shape[0], width), F32),
-            pltpu.VMEM((keys.shape[0], width), BF),
-            pltpu.VMEM(keys.shape, BF),
-            pltpu.SemaphoreType.DMA((len(PARTS),)),
-        ],
+    n_half = n_ctx // 2
+    shard = lax.axis_index("ctx")
+    place = jnp.stack([shard, (shard // 2) % 2]).astype(jnp.int32)
+    near_q = jnp.broadcast_to(queries[None], (n_half,) + queries.shape)
+    near_q = lax.all_to_all(near_q, "ctx", 0, 0, axis_index_groups=SAME_HALF)
+    near_q = near_q.reshape(ROWS // 2, -1)
+    keys, near_bias, far_bias = staged(kv_cache, blocks.T, place)
+    near_q, near_bias = lax.optimization_barrier((near_q, near_bias))
+    far_q = lax.ppermute(near_q, "ctx", OTHER_HALF)
+    keys = in_hbm(keys)
+    width = H_DEV * ROWS // 2
+    scratch = [
+        pltpu.VMEM((WIDE, width), BF),
+        pltpu.VMEM((keys.shape[0], width), F32),
+        pltpu.VMEM((keys.shape[0], width), BF),
+        pltpu.VMEM(keys.shape, BF),
+        pltpu.SemaphoreType.DMA((len(PARTS),)),
+    ]
+    own = ROWS // n_half
+    near = call(
+        attend_near,
+        jax.ShapeDtypeStruct((ROWS // 2, WIDE), BF),
+        near_q, w_uk, value_up_weight, near_bias, keys,
+        scratch=scratch,
         spaces=[pltpu.VMEM] * 4 + [pltpu.HBM],
         limit=40,
     )
-    own = ROWS // (n_ctx // 2)
-    parts = lax.all_to_all(
-        parts.reshape(n_ctx // 2, own, WIDE), "ctx", 0, 0, axis_index_groups=SAME_HALF
+    parts = call(
+        attend_far,
+        jax.ShapeDtypeStruct((n_half, own, WIDE), BF),
+        far_q, w_uk, value_up_weight, far_bias, near, keys,
+        scratch=scratch,
+        spaces=[pltpu.VMEM] * 5 + [pltpu.HBM],
+        limit=40,
     )
+    parts = lax.all_to_all(parts, "ctx", 0, 0, axis_index_groups=SAME_HALF)
     half = call(merge_half, jax.ShapeDtypeStruct((own, WIDE), BF), parts)
-    other = lax.ppermute(half, "ctx", [(i, i ^ 2) for i in range(n_ctx)])
-    value = call(merge_all, jax.ShapeDtypeStruct((n_ctx // 2, own, H_DEV * VD), BF), half, other)
+    other = lax.ppermute(half, "ctx", OTHER_HALF)
+    value = call(
+        merge_all,
+        jax.ShapeDtypeStruct((n_half, own, H_DEV * VD), BF),
+        half, other, place,
+        spaces=[pltpu.VMEM] * 2 + [pltpu.SMEM],
+    )
     value = lax.all_to_all(value, "ctx", 0, 0, axis_index_groups=SAME_HALF).reshape(ROWS, -1)
     partial = call(project, jax.ShapeDtypeStruct((ROWS, w_out.shape[1]), BF), value, w_out.T)
     n_head = lax.axis_size("head")

time: 99.4 us -> 101 us (1.016)
  waiting for transfers between devices: 21.1 us -> 3.2 us
  starting transfers between devices: 21.2 us -> 31.7 us
  blocking collectives: 41.6 us -> 46.3 us
  Pallas kernels: 12.9 us -> 16.7 us
    ppermute x1 -> x2, starting transfers between devices: 3.07 us -> 22.6 us  [the longest x1 11.4 us: body(): far_q = lax.ppermute(near_q, 'ctx', OTHER_HALF)]
    all_to_all x1, waiting for transfers between devices: 9.69 us -> 0.01 us  [body(): near_q = lax.all_to_all(near_q, 'ctx', 0, 0, axis_index_groups=SAME_HALF)]
    all_to_all x1, starting transfers between devices: 18.1 us -> 9.17 us  [body(): near_q = lax.all_to_all(near_q, 'ctx', 0, 0, axis_index_groups=SAME_HALF)]
    ppermute x1 -> x2, waiting for transfers between devices: 11.4 us -> 3.2 us  [the longest x1 3.2 us: body(): other = lax.ppermute(half, 'ctx', OTHER_HALF)]
    all_to_all x1, blocking collectives: 22.5 us -> 28.4 us  [body(): lax.all_to_all(partial.reshape(n_head, ROWS // n_head, -1), 'head', 0, 0)]
    pallas_call x4 -> x5, Pallas kernels: 8.96 us -> 12.3 us  [call(): pl.pallas_call(kernel, out_shape=out_shape, in_specs=[pl.BlockSpec(memory...]
    all_gather x1 -> x0, blocking collectives: 1.93 us -> none  [body(): lax.all_gather(q, 'ctx', axis=0, tiled=True, axis_index_groups=SAME_CHIP)]
  transfers between devices with their start and end apart: 2 -> 3, of which waited for: 2 -> 1; matrix products, arithmetic and copies ran while one was open for 0% -> 0% of each run, Pallas kernels for 4% -> 10%
where the time goes in v6:
time: 101 us; the launch traced here: 100 us
  blocking collectives  46.3 us (46%)
  starting transfers between devices  31.7 us (31%)
  Pallas kernels  16.7 us (17%)
  waiting for transfers between devices  3.2 us (3%)
  local copies, waits for them, and re-layouts  1.48 us (1%)
    all_to_all x1, blocking collectives, body(): lax.all_to_all(partial.reshape(n_head, ROWS // n_head, -1), 'head', 0, 0)  28.4 us
    pallas_call x5, Pallas kernels, call(): pl.pallas_call(kernel, out_shape=out_shape, in_specs=[pl.BlockSpec(memory...  12.3 us
    ppermute x1, starting transfers between devices, body(): far_q = lax.ppermute(near_q, 'ctx', OTHER_HALF)  11.4 us
    ppermute x1, starting transfers between devices, body(): other = lax.ppermute(half, 'ctx', OTHER_HALF)  11.2 us
    all_to_all x1, blocking collectives, body(): parts = lax.all_to_all(parts, 'ctx', 0, 0, axis_index_groups=SAME_HALF)  9.41 us
    all_to_all x1, starting transfers between devices, body(): near_q = lax.all_to_all(near_q, 'ctx', 0, 0, axis_index_groups=SAME_HALF)  9.17 us
    all_to_all x1, blocking collectives, body(): lax.all_to_all(value, 'ctx', 0, 0, axis_index_groups=SAME_HALF)  8.42 us
    pallas_call x1, Pallas kernels, staged(): pl.pallas_call(stage, out_shape=(pltpu.HBM(keys, BF), bias, bias), in_spe...  4.47 us
  transfers between devices with their start and end apart: 3, of which 1 were waited for; matrix products, arithmetic and copies ran while one was open for 0% of the time, Pallas kernels for 10%

profile of v6, /device:TPU:2, one launch (start us, length us, event | category | flops | bytes accessed | tf_op | source)
XLA Modules:
  0.0 100.3 jit_solution(10181823365893216312)
XLA Ops:
  0.0 0.0 copy-start.1
  0.0 0.0 copy-start
  0.0 1.4 %broadcast_in_dim.2 = bf16[8,8,768]{2,1,0:T(8,128)(2,1)} broadcast(bf16[8,768]{1,0:T(8,128)(2,1)} %param.6), dimensions={1,2} | broadcast | bytes 110592 | tf_op jit(solution)/shard_map/broadcast_in_dim | solution.py:304
  1.4 9.2 %all-to-all-start = ((bf16[8,8,768]{2,1,0:T(8,128)(2,1)}), bf16[8,8,768]{2,1,0:T(8,128)(2,1)S(1)}, u32[]{:S(2)}, u32[]{:S(2)}) async-start(bf16[8,8,768]{2,1,0:T(8,128)(2,1)} %broadcast_in_dim.2), calls=%async_computation | async-start | bytes 196608 | tf_op jit(solution)/shard_map/all_to_all | solution.py:305
  10.6 0.1 pad_add_fusion.shard_ref
  10.7 4.5 %shard_map.64 = (bf16[4096,640]{1,0:T(8,128)(2,1)}, f32[128,256]{1,0:T(8,128)S(1)}, f32[128,256]{1,0:T(8,128)S(1)}) custom-call(bf16[64,36864]{1,0:T(8,128)(2,1)} %kv_hbm.1, s32[32,128]{1,0:T(8,128)} %bitcast.10, s32[2]{0:T(128)S(1)} %pad_add_fusion.shard_ref), custom_call_target="tpu_custom_call" | custom-call | tf_op jit(solution)/shard_map/pallas_call | solution.py:125
  15.2 0.0 all-to-all-done
  15.2 11.4 %collective-permute-start = (bf16[64,768]{1,0:T(8,128)(2,1)S(1)}, bf16[64,768]{1,0:T(8,128)(2,1)S(1)}, u32[]{:S(2)}, u32[]{:S(2)}) collective-permute-start(bf16[64,768]{1,0:T(8,128)(2,1)S(1)} %bitcast.8), channel_id=1, source_target_pairs={{0,64},{32,96},{64,0},{96,32},{128,192},{160,224},{192,128},{224,1... | collective-permute-start | bytes 294920 | tf_op jit(solution)/shard_map/ppermute | solution.py:309
  26.6 0.0 copy-done.1
  26.6 0.0 copy-done
  26.6 5.4 %shard_map.65.near_ref = bf16[64,640]{1,0:T(8,128)(2,1)S(1)} custom-call(bf16[64,768]{1,0:T(8,128)(2,1)S(1)} %bitcast.9, bf16[4,128,512]{2,1,0:T(8,128)(2,1)S(1)} %copy-done, bf16[4,512,128]{2,1,0:T(8,128)(2,1)S(1)} %copy-done.1, f32[128,256]{1,0:T(8,128)S(1)} %get-tuple-element.13.bias_ref, bf16[4096,640]{1,0:T(8,128)(2,1)} %get-tuple-element.14.k_hbm), custom_call_target="tpu_custom_call" | custom-call | tf_op jit(solution)/shard_map/pallas_call | solution.py:288
  32.0 0.0 copy-start.2
  32.0 0.0 collective-permute-done.q_ref
  32.0 5.4 %shard_map.66 = bf16[8,16,640]{2,1,0:T(8,128)(2,1)S(1)} custom-call(bf16[64,768]{1,0:T(8,128)(2,1)S(1)} %collective-permute-done.q_ref, bf16[4,128,512]{2,1,0:T(8,128)(2,1)S(1)} %copy-done, bf16[4,512,128]{2,1,0:T(8,128)(2,1)S(1)} %copy-done.1, f32[128,256]{1,0:T(8,128)S(1)} %get-tuple-element.12.bias_ref, bf16[64,640]{1,0:T(8,128)(2,1)S(1)} %shard_map.65.near_ref, ...), custom_call_target="tpu_custom_call" | custom-call | tf_op jit(solution)/shard_map/pallas_call | solution.py:288
  37.4 9.4 %all_to_all.20.in_ref = bf16[8,16,640]{2,1,0:T(8,128)(2,1)S(1)} all-to-all(bf16[8,16,640]{2,1,0:T(8,128)(2,1)S(1)} %shard_map.66), channel_id=1, replica_groups={{0,128,256,384,32,160,288,416},{64,192,320,448,96,224,352,480},{1,129,2..., dimensions={0} | all-to-all | bytes 327680 | tf_op jit(solution)/shard_map/all_to_all | solution.py:336
  46.8 0.4 shard_map.67.own_ref
  47.2 11.2 %collective-permute-start.1 = (bf16[16,640]{1,0:T(8,128)(2,1)S(1)}, bf16[16,640]{1,0:T(8,128)(2,1)S(1)}, u32[]{:S(2)}, u32[]{:S(2)}) collective-permute-start(bf16[16,640]{1,0:T(8,128)(2,1)S(1)} %shard_map.67.own_ref), channel_id=1, source_target_pairs={{0,64},{32,96},{64,0},{96,32},{128,192},{160,224},{192,128},{224,1... | collective-permute-start | bytes 61448 | tf_op jit(solution)/shard_map/ppermute | solution.py:338
  58.3 3.2 %collective-permute-done.1.other_ref = bf16[16,640]{1,0:T(8,128)(2,1)S(1)} collective-permute-done((bf16[16,640]{1,0:T(8,128)(2,1)S(1)}, bf16[16,640]{1,0:T(8,128)(2,1)S(1)}, u32[]{:S(2)}, u32[]{:S(2)}) %collective-permute-start.1) | collective-permute-done | bytes 20512 | tf_op jit(solution)/shard_map/ppermute | solution.py:338
  61.5 0.8 shard_map.68
  62.4 8.4 %all_to_all.21 = bf16[8,16,512]{2,1,0:T(8,128)(2,1)S(1)} all-to-all(bf16[8,16,512]{2,1,0:T(8,128)(2,1)S(1)} %shard_map.68), channel_id=1, replica_groups={{0,128,256,384,32,160,288,416},{64,192,320,448,96,224,352,480},{1,129,2..., dimensions={0} | all-to-all | bytes 262144 | tf_op jit(solution)/shard_map/all_to_all | solution.py:345
  70.8 0.0 copy-done.2
  70.8 0.3 shard_map.69
  71.2 28.4 %all_to_all.22 = bf16[32,4,448]{2,1,0:T(4,128)(2,1)S(1)} all-to-all(bf16[32,4,448]{2,1,0:T(4,128)(2,1)S(1)} %reshape.12), channel_id=1, replica_groups=mesh['ctx'=16,'head'=32] {'head'}, dimensions={0} | all-to-all | bytes 229376 | tf_op jit(solution)/shard_map/all_to_all | solution.py:348
  99.6 0.7 reduce_sum.12
  (1 shorter events, 0.0 us)
Async XLA Ops:
  0.0 26.6 %copy-start.1 = (bf16[4,512,128]{2,1,0:T(8,128)(2,1)S(1)}, bf16[4,512,128]{2,1,0:T(8,128)(2,1)}, u32[]{:S(2)}) copy-start(bf16[4,512,128]{2,1,0:T(8,128)(2,1)} %vue_ref.3) | copy-start | bytes 1572868
  0.0 26.6 %copy-start = (bf16[4,128,512]{2,1,0:T(8,128)(2,1)S(1)}, bf16[4,128,512]{2,1,0:T(8,128)(2,1)}, u32[]{:S(2)}) copy-start(bf16[4,128,512]{2,1,0:T(8,128)(2,1)} %w_ref.3) | copy-start | bytes 1572868
  1.4 13.7 %all-to-all-start = ((bf16[8,8,768]{2,1,0:T(8,128)(2,1)}), bf16[8,8,768]{2,1,0:T(8,128)(2,1)S(1)}, u32[]{:S(2)}, u32[]{:S(2)}) async-start(bf16[8,8,768]{2,1,0:T(8,128)(2,1)} %broadcast_in_dim.2), calls=%async_computation | async-start | bytes 196608 | tf_op jit(solution)/shard_map/all_to_all | solution.py:305
  15.2 16.8 %collective-permute-start = (bf16[64,768]{1,0:T(8,128)(2,1)S(1)}, bf16[64,768]{1,0:T(8,128)(2,1)S(1)}, u32[]{:S(2)}, u32[]{:S(2)}) collective-permute-start(bf16[64,768]{1,0:T(8,128)(2,1)S(1)} %bitcast.8), channel_id=1, source_target_pairs={{0,64},{32,96},{64,0},{96,32},{128,192},{160,224},{192,128},{224,1... | collective-permute-start | bytes 294920 | tf_op jit(solution)/shard_map/ppermute | solution.py:309
  32.0 38.9 %copy-start.2 = (bf16[512,448]{0,1:T(8,128)(2,1)S(1)}, bf16[512,448]{0,1:T(8,128)(2,1)}, u32[]{:S(2)}) copy-start(bf16[512,448]{0,1:T(8,128)(2,1)} %param.9) | copy-start | bytes 1376260
  47.2 14.4 %collective-permute-start.1 = (bf16[16,640]{1,0:T(8,128)(2,1)S(1)}, bf16[16,640]{1,0:T(8,128)(2,1)S(1)}, u32[]{:S(2)}, u32[]{:S(2)}) collective-permute-start(bf16[16,640]{1,0:T(8,128)(2,1)S(1)} %shard_map.67.own_ref), channel_id=1, source_target_pairs={{0,64},{32,96},{64,0},{96,32},{128,192},{160,224},{192,128},{224,1... | collective-permute-start | bytes 61448 | tf_op jit(solution)/shard_map/ppermute | solution.py:338

commit v7 on v5

--- a/solution.py
+++ b/solution.py
@@ -25,9 +25,8 @@
 INTERPRET = False
 KEY = KVR + ROPE
 
-SAME_CORE = [[x * 4 + z * 2 + c for x in range(4) for z in range(2)] for c in range(2)]
-SAME_CHIP = [[x * 4 + z * 2 + c for c in range(2)] for x in range(4) for z in range(2)]
 SAME_HALF = [[x * 4 + z * 2 + c for c in range(2) for x in range(4)] for z in range(2)]
+OTHER_HALF = [(i, i ^ 2) for i in range(16)]
 
 
 def nt_dot(a, b):
@@ -240,6 +239,15 @@
     out_ref[...] = jnp.concatenate(nums + [with_stats(tops, totals, rows)], axis=1).astype(BF)
 
 
+def copies_of_both(own_ref, other_ref, place_ref, out_ref):
+    own, other = own_ref[...].astype(F32), other_ref[...].astype(F32)
+    lower = place_ref[1] == 0
+    first, second = jnp.where(lower, own, other), jnp.where(lower, other, own)
+    both = jnp.concatenate([first, second], axis=0).astype(BF)
+    for k in range(out_ref.shape[0]):
+        out_ref[k] = both
+
+
 def merge_all(own_ref, other_ref, out_ref):
     data = [own_ref[...].astype(F32), other_ref[...].astype(F32)]
     nums, _, totals = merge([d[:, : H_DEV * VD] for d in data], [d[:, H_DEV * VD :] for d in data])
@@ -268,11 +276,19 @@
 
 def body(queries, w_uk, value_up_weight, w_out, kv_cache, blocks):
     n_ctx = lax.axis_size("ctx")
-    q = jnp.broadcast_to(queries[None], (n_ctx // 2,) + queries.shape)
-    q = lax.all_to_all(q, "ctx", 0, 0, axis_index_groups=SAME_CORE)
-    q = lax.all_gather(q, "ctx", axis=0, tiled=True, axis_index_groups=SAME_CHIP)
-    q = q.reshape(ROWS, -1)
-    keys, bias = staged(kv_cache, blocks.T, lax.axis_index("ctx").reshape(1))
+    n_half = n_ctx // 2
+    own = 2 * queries.shape[0]
+    shard = lax.axis_index("ctx")
+    place = jnp.stack([shard, (shard // 2) % 2]).astype(jnp.int32)
+    other = lax.ppermute(queries, "ctx", OTHER_HALF)
+    keys, bias = staged(kv_cache, blocks.T, place)
+    both = call(
+        copies_of_both,
+        jax.ShapeDtypeStruct((n_half, own, queries.shape[1]), BF),
+        queries, other, place,
+        spaces=[pltpu.VMEM] * 2 + [pltpu.SMEM],
+    )
+    q = lax.all_to_all(both, "ctx", 0, 0, axis_index_groups=SAME_HALF).reshape(ROWS, -1)
     width = H_DEV * ROWS
     parts = call(
         attend,
@@ -288,13 +304,12 @@
         spaces=[pltpu.VMEM] * 4 + [pltpu.HBM],
         limit=40,
     )
-    own = ROWS // (n_ctx // 2)
     parts = lax.all_to_all(
-        parts.reshape(n_ctx // 2, own, WIDE), "ctx", 0, 0, axis_index_groups=SAME_HALF
+        parts.reshape(n_half, own, WIDE), "ctx", 0, 0, axis_index_groups=SAME_HALF
     )
     half = call(merge_half, jax.ShapeDtypeStruct((own, WIDE), BF), parts)
-    other = lax.ppermute(half, "ctx", [(i, i ^ 2) for i in range(n_ctx)])
-    value = call(merge_all, jax.ShapeDtypeStruct((n_ctx // 2, own, H_DEV * VD), BF), half, other)
+    other = lax.ppermute(half, "ctx", OTHER_HALF)
+    value = call(merge_all, jax.ShapeDtypeStruct((n_half, own, H_DEV * VD), BF), half, other)
     value = lax.all_to_all(value, "ctx", 0, 0, axis_index_groups=SAME_HALF).reshape(ROWS, -1)
     partial = call(project, jax.ShapeDtypeStruct((ROWS, w_out.shape[1]), BF), value, w_out.T)
     n_head = lax.axis_size("head")

time: 99.4 us -> 98.2 us (0.988)
  waiting for transfers between devices: 21.1 us -> 5.46 us
  starting transfers between devices: 21.2 us -> 33.3 us
  Pallas kernels: 12.9 us -> 14.6 us
  blocking collectives: 41.6 us -> 42.7 us
    ppermute x1 -> x2, starting transfers between devices: 3.07 us -> 27.2 us  [the longest x1 15.8 us: body(): other = lax.ppermute(queries, 'ctx', OTHER_HALF)]
    all_to_all x1, starting transfers between devices: 18.1 us -> 6.11 us  [body(): lax.all_to_all(both, 'ctx', 0, 0, axis_index_groups=SAME_HALF)]
    all_to_all x1, waiting for transfers between devices: 9.69 us -> 0.66 us  [body(): lax.all_to_all(both, 'ctx', 0, 0, axis_index_groups=SAME_HALF)]
    ppermute x1 -> x2, waiting for transfers between devices: 11.4 us -> 4.8 us  [the longest x1 3.04 us: body(): other = lax.ppermute(half, 'ctx', OTHER_HALF)]
    all_to_all x1, blocking collectives: 22.5 us -> 25.5 us  [body(): lax.all_to_all(partial.reshape(n_head, ROWS // n_head, -1), 'head', 0, 0)]
    all_gather x1 -> x0, blocking collectives: 1.93 us -> none  [body(): lax.all_gather(q, 'ctx', axis=0, tiled=True, axis_index_groups=SAME_CHIP)]
    broadcast_in_dim x1 -> x0, local copies, waits for them, and re-layouts: 1.43 us -> none  [body(): q = jnp.broadcast_to(queries[None], (n_ctx // 2,) + queries.shape)]
    pallas_call x4 -> x5, Pallas kernels: 8.96 us -> 10.2 us  [call(): pl.pallas_call(kernel, out_shape=out_shape, in_specs=[pl.BlockSpec(memory...]
  transfers between devices with their start and end apart: 2 -> 3, of which waited for: 2 -> 3; matrix products, arithmetic and copies ran while one was open for 0% -> 0% of each run, Pallas kernels for 4% -> 5%
where the time goes in v7:
time: 98.2 us; the launch traced here: 97.8 us
  blocking collectives  42.7 us (43%)
  starting transfers between devices  33.3 us (34%)
  Pallas kernels  14.6 us (15%)
  waiting for transfers between devices  5.46 us (6%)
    all_to_all x1, blocking collectives, body(): lax.all_to_all(partial.reshape(n_head, ROWS // n_head, -1), 'head', 0, 0)  25.5 us
    ppermute x1, starting transfers between devices, body(): other = lax.ppermute(queries, 'ctx', OTHER_HALF)  15.8 us
    ppermute x1, starting transfers between devices, body(): other = lax.ppermute(half, 'ctx', OTHER_HALF)  11.3 us
    pallas_call x5, Pallas kernels, call(): pl.pallas_call(kernel, out_shape=out_shape, in_specs=[pl.BlockSpec(memory...  10.2 us
    all_to_all x1, blocking collectives, body(): lax.all_to_all(parts.reshape(n_half, own, WIDE), 'ctx', 0, 0, axis_index_...  8.79 us
    all_to_all x1, blocking collectives, body(): lax.all_to_all(value, 'ctx', 0, 0, axis_index_groups=SAME_HALF)  8.42 us
    all_to_all x1, starting transfers between devices, body(): lax.all_to_all(both, 'ctx', 0, 0, axis_index_groups=SAME_HALF)  6.11 us
    pallas_call x1, Pallas kernels, staged(): pl.pallas_call(stage, out_shape=(pltpu.HBM(keys, BF), jax.ShapeDtypeStruc...  4.47 us
  transfers between devices with their start and end apart: 3, of which 3 were waited for; matrix products, arithmetic and copies ran while one was open for 0% of the time, Pallas kernels for 5%

profile of v7, /device:TPU:2, one launch (start us, length us, event | category | flops | bytes accessed | tf_op | source)
XLA Modules:
  0.0 97.8 jit_solution(6298020915472214643)
XLA Ops:
  0.0 0.0 copy-start.1
  0.0 0.0 copy-start
  0.0 15.8 %collective-permute-start = (bf16[8,768]{1,0:T(8,128)(2,1)}, bf16[8,768]{1,0:T(8,128)(2,1)S(1)}, u32[]{:S(2)}, u32[]{:S(2)}) collective-permute-start(bf16[8,768]{1,0:T(8,128)(2,1)} %own_ref.1), channel_id=1, source_target_pairs={{0,64},{32,96},{64,0},{96,32},{128,192},{160,224},{192,128},{224,1... | collective-permute-start | bytes 36872 | tf_op jit(solution)/shard_map/ppermute | solution.py:283
  15.9 0.1 pad_add_fusion.place_ref.shard_ref
  16.0 1.8 %collective-permute-done.other_ref = bf16[8,768]{1,0:T(8,128)(2,1)S(1)} collective-permute-done((bf16[8,768]{1,0:T(8,128)(2,1)}, bf16[8,768]{1,0:T(8,128)(2,1)S(1)}, u32[]{:S(2)}, u32[]{:S(2)}) %collective-permute-start) | collective-permute-done | bytes 12320 | tf_op jit(solution)/shard_map/ppermute | solution.py:283
  17.7 0.0 copy-start.3
  17.7 0.7 copy-done.3
  18.4 1.2 %shard_map.64 = bf16[8,16,768]{2,1,0:T(8,128)(2,1)} custom-call(bf16[8,768]{1,0:T(8,128)(2,1)S(1)} %copy-done.3, bf16[8,768]{1,0:T(8,128)(2,1)S(1)} %collective-permute-done.other_ref, s32[2]{0:T(128)S(1)} %pad_add_fusion.place_ref.shard_ref), custom_call_target="tpu_custom_call" | custom-call | tf_op jit(solution)/shard_map/pallas_call | solution.py:266
  19.7 6.1 %all-to-all-start = ((bf16[8,16,768]{2,1,0:T(8,128)(2,1)}), bf16[8,16,768]{2,1,0:T(8,128)(2,1)S(1)}, u32[]{:S(2)}, u32[]{:S(2)}) async-start(bf16[8,16,768]{2,1,0:T(8,128)(2,1)} %shard_map.64), calls=%async_computation | async-start | bytes 393216 | tf_op jit(solution)/shard_map/all_to_all | solution.py:291
  25.8 0.0 copy-start.2
  25.8 4.5 %shard_map.65 = (bf16[4096,640]{1,0:T(8,128)(2,1)}, f32[128,128]{1,0:T(8,128)S(1)}) custom-call(bf16[64,36864]{1,0:T(8,128)(2,1)} %kv_hbm.1, s32[32,128]{1,0:T(8,128)} %bitcast.11, s32[2]{0:T(128)S(1)} %pad_add_fusion.place_ref.shard_ref), custom_call_target="tpu_custom_call" | custom-call | tf_op jit(solution)/shard_map/pallas_call | solution.py:116
  30.3 0.7 all-to-all-done
  30.9 0.0 copy-done.1
  30.9 0.0 copy-done
  30.9 8.0 %shard_map.66 = bf16[128,640]{1,0:T(8,128)(2,1)S(1)} custom-call(bf16[128,768]{1,0:T(8,128)(2,1)S(1)} %bitcast.7, bf16[4,128,512]{2,1,0:T(8,128)(2,1)S(1)} %copy-done, bf16[4,512,128]{2,1,0:T(8,128)(2,1)S(1)} %copy-done.1, f32[128,128]{1,0:T(8,128)S(1)} %get-tuple-element.7.bias_ref, bf16[4096,640]{1,0:T(8,128)(2,1)} %get-tuple-element.8.k_hbm), custom_call_target="tpu_custom_call" | custom-call | tf_op jit(solution)/shard_map/pallas_call | solution.py:266
  38.9 8.8 %all_to_all.20.in_ref = bf16[8,16,640]{2,1,0:T(8,128)(2,1)S(1)} all-to-all(bf16[8,16,640]{2,1,0:T(8,128)(2,1)S(1)} %bitcast.8), channel_id=1, replica_groups={{0,128,256,384,32,160,288,416},{64,192,320,448,96,224,352,480},{1,129,2..., dimensions={0} | all-to-all | bytes 327680 | tf_op jit(solution)/shard_map/all_to_all | solution.py:307
  47.7 0.4 shard_map.67.own_ref
  48.1 11.3 %collective-permute-start.1 = (bf16[16,640]{1,0:T(8,128)(2,1)S(1)}, bf16[16,640]{1,0:T(8,128)(2,1)S(1)}, u32[]{:S(2)}, u32[]{:S(2)}) collective-permute-start(bf16[16,640]{1,0:T(8,128)(2,1)S(1)} %shard_map.67.own_ref), channel_id=1, source_target_pairs={{0,64},{32,96},{64,0},{96,32},{128,192},{160,224},{192,128},{224,1... | collective-permute-start | bytes 61448 | tf_op jit(solution)/shard_map/ppermute | solution.py:311
  59.4 3.0 %collective-permute-done.1.other_ref = bf16[16,640]{1,0:T(8,128)(2,1)S(1)} collective-permute-done((bf16[16,640]{1,0:T(8,128)(2,1)S(1)}, bf16[16,640]{1,0:T(8,128)(2,1)S(1)}, u32[]{:S(2)}, u32[]{:S(2)}) %collective-permute-start.1) | collective-permute-done | bytes 20512 | tf_op jit(solution)/shard_map/ppermute | solution.py:311
  62.5 0.3 shard_map.68
  62.8 8.4 %all_to_all.21 = bf16[8,16,512]{2,1,0:T(8,128)(2,1)S(1)} all-to-all(bf16[8,16,512]{2,1,0:T(8,128)(2,1)S(1)} %shard_map.68), channel_id=1, replica_groups={{0,128,256,384,32,160,288,416},{64,192,320,448,96,224,352,480},{1,129,2..., dimensions={0} | all-to-all | bytes 262144 | tf_op jit(solution)/shard_map/all_to_all | solution.py:313
  71.2 0.0 copy-done.2
  71.2 0.3 shard_map.69
  71.5 25.5 %all_to_all.22 = bf16[32,4,448]{2,1,0:T(4,128)(2,1)S(1)} all-to-all(bf16[32,4,448]{2,1,0:T(4,128)(2,1)S(1)} %reshape.15), channel_id=1, replica_groups=mesh['ctx'=16,'head'=32] {'head'}, dimensions={0} | all-to-all | bytes 229376 | tf_op jit(solution)/shard_map/all_to_all | solution.py:316
  97.1 0.7 reduce_sum.12
  (1 shorter events, 0.0 us)
Async XLA Ops:
  0.0 30.9 %copy-start.1 = (bf16[4,512,128]{2,1,0:T(8,128)(2,1)S(1)}, bf16[4,512,128]{2,1,0:T(8,128)(2,1)}, u32[]{:S(2)}) copy-start(bf16[4,512,128]{2,1,0:T(8,128)(2,1)} %vue_ref.1) | copy-start | bytes 1572868
  0.0 30.9 %copy-start = (bf16[4,128,512]{2,1,0:T(8,128)(2,1)S(1)}, bf16[4,128,512]{2,1,0:T(8,128)(2,1)}, u32[]{:S(2)}) copy-start(bf16[4,128,512]{2,1,0:T(8,128)(2,1)} %w_ref.1) | copy-start | bytes 1572868
  0.0 17.7 %collective-permute-start = (bf16[8,768]{1,0:T(8,128)(2,1)}, bf16[8,768]{1,0:T(8,128)(2,1)S(1)}, u32[]{:S(2)}, u32[]{:S(2)}) collective-permute-start(bf16[8,768]{1,0:T(8,128)(2,1)} %own_ref.1), channel_id=1, source_target_pairs={{0,64},{32,96},{64,0},{96,32},{128,192},{160,224},{192,128},{224,1... | collective-permute-start | bytes 36872 | tf_op jit(solution)/shard_map/ppermute | solution.py:283
  17.7 0.7 copy-start.3
  19.7 11.3 %all-to-all-start = ((bf16[8,16,768]{2,1,0:T(8,128)(2,1)}), bf16[8,16,768]{2,1,0:T(8,128)(2,1)S(1)}, u32[]{:S(2)}, u32[]{:S(2)}) async-start(bf16[8,16,768]{2,1,0:T(8,128)(2,1)} %shard_map.64), calls=%async_computation | async-start | bytes 393216 | tf_op jit(solution)/shard_map/all_to_all | solution.py:291
  25.8 45.4 %copy-start.2 = (bf16[512,448]{0,1:T(8,128)(2,1)S(1)}, bf16[512,448]{0,1:T(8,128)(2,1)}, u32[]{:S(2)}) copy-start(bf16[512,448]{0,1:T(8,128)(2,1)} %param.9) | copy-start | bytes 1376260
  48.1 14.4 %collective-permute-start.1 = (bf16[16,640]{1,0:T(8,128)(2,1)S(1)}, bf16[16,640]{1,0:T(8,128)(2,1)S(1)}, u32[]{:S(2)}, u32[]{:S(2)}) collective-permute-start(bf16[16,640]{1,0:T(8,128)(2,1)S(1)} %shard_map.67.own_ref), channel_id=1, source_target_pairs={{0,64},{32,96},{64,0},{96,32},{128,192},{160,224},{192,128},{224,1... | collective-permute-start | bytes 61448 | tf_op jit(solution)/shard_map/ppermute | solution.py:311

commit v8 on v7

--- a/solution.py
+++ b/solution.py
@@ -70,7 +70,9 @@
     return pltpu.with_memory_space_constraint(x, pltpu.HBM)
 
 
-def stage(kv_hbm, blocks_hbm, shard_ref, out_hbm, bias_ref, kv_ref, blocks_ref, keys_ref, sems, sent):
+def stage(
+    kv_hbm, blocks_hbm, q_hbm, shard_ref, out_hbm, bias_ref, q_ref, kv_ref, blocks_ref, keys_ref, sems, sent
+):
     count, lanes = kv_ref.shape
     span = STAGE_PAIRS * PAIR
     chunk = STAGE_PAIRS * 2 * count
@@ -82,6 +84,8 @@
         got[-1].start()
     table = pltpu.make_async_copy(blocks_hbm, blocks_ref, sems.at[steps])
     table.start()
+    own = pltpu.make_async_copy(q_hbm, q_ref, sems.at[steps + 1])
+    own.start()
     pad = jnp.zeros((count, WIDE - KEY), BF)
     put = []
     for i in range(steps):
@@ -106,32 +110,42 @@
     for k in range(b.shape[0]):
         bias = jnp.where(b[k : k + 1, :] == line, 0.0, bias)
     bias_ref[...] = jnp.concatenate([bias, bias], axis=0)
+    own.wait()
     for copy in put:
         copy.wait()
 
 
-def staged(kv, blocks, shard):
+def staged(kv, blocks, queries, shard):
     steps = kv.shape[1] // (PAIR * STAGE_PAIRS)
     keys = (kv.shape[0] * kv.shape[1] // KEY, WIDE)
     return pl.pallas_call(
         stage,
-        out_shape=(pltpu.HBM(keys, BF), jax.ShapeDtypeStruct((2 * kv.shape[0], ROWS), F32)),
+        out_shape=(
+            pltpu.HBM(keys, BF),
+            jax.ShapeDtypeStruct((2 * kv.shape[0], ROWS), F32),
+            jax.ShapeDtypeStruct(queries.shape, BF),
+        ),
         in_specs=[
+            pl.BlockSpec(memory_space=pltpu.HBM),
             pl.BlockSpec(memory_space=pltpu.HBM),
             pl.BlockSpec(memory_space=pltpu.HBM),
             pl.BlockSpec(memory_space=pltpu.SMEM),
         ],
-        out_specs=(pl.BlockSpec(memory_space=pltpu.HBM), pl.BlockSpec(memory_space=pltpu.VMEM)),
+        out_specs=(
+            pl.BlockSpec(memory_space=pltpu.HBM),
+            pl.BlockSpec(memory_space=pltpu.VMEM),
+            pl.BlockSpec(memory_space=pltpu.VMEM),
+        ),
         scratch_shapes=[
             pltpu.VMEM(kv.shape, BF),
             pltpu.VMEM(blocks.shape, jnp.int32),
             pltpu.VMEM(keys, BF),
-            pltpu.SemaphoreType.DMA((steps + 1,)),
+            pltpu.SemaphoreType.DMA((steps + 2,)),
             pltpu.SemaphoreType.DMA((steps,)),
         ],
         compiler_params=pltpu.CompilerParams(vmem_limit_bytes=24 * 2**20),
         interpret=INTERPRET,
-    )(in_hbm(kv), in_hbm(blocks), shard)
+    )(in_hbm(kv), in_hbm(blocks), in_hbm(queries), shard)
 
 
 def attend(q_ref, w_ref, vue_ref, bias_ref, k_hbm, out_ref, qt, s_ref, p_ref, k_ref, sems):
@@ -281,7 +295,8 @@
     shard = lax.axis_index("ctx")
     place = jnp.stack([shard, (shard // 2) % 2]).astype(jnp.int32)
     other = lax.ppermute(queries, "ctx", OTHER_HALF)
-    keys, bias = staged(kv_cache, blocks.T, place)
+    keys, bias, queries = staged(kv_cache, blocks.T, queries, place)
+    other, bias = lax.optimization_barrier((other, bias))
     both = call(
         copies_of_both,
         jax.ShapeDtypeStruct((n_half, own, queries.shape[1]), BF),

time: 98.2 us -> 96.5 us (0.983)
  blocking collectives: 42.7 us -> 51 us
  starting transfers between devices: 33.3 us -> 25.7 us
    all_to_all x0 -> x1, blocking collectives: none -> 9.74 us  [body(): lax.all_to_all(both, 'ctx', 0, 0, axis_index_groups=SAME_HALF)]
    all_to_all x1 -> x0, starting transfers between devices: 6.11 us -> none  [body(): lax.all_to_all(both, 'ctx', 0, 0, axis_index_groups=SAME_HALF)]
    ppermute x1, waiting for transfers between devices: 1.77 us -> 0.01 us  [body(): other = lax.ppermute(queries, 'ctx', OTHER_HALF)]
    ppermute x1, waiting for transfers between devices: 3.04 us -> 4.51 us  [body(): other = lax.ppermute(half, 'ctx', OTHER_HALF)]
    ppermute x1, starting transfers between devices: 11.3 us -> 9.87 us  [body(): other = lax.ppermute(half, 'ctx', OTHER_HALF)]
    all_to_all x1, blocking collectives: 25.5 us -> 24.1 us  [body(): lax.all_to_all(partial.reshape(n_head, ROWS // n_head, -1), 'head', 0, 0)]
  transfers between devices with their start and end apart: 3 -> 2, of which waited for: 3 -> 1; matrix products, arithmetic and copies ran while one was open for 0% -> 0% of each run, Pallas kernels for 5% -> 5%
where the time goes in v8:
time: 96.5 us; the launch traced here: 96.2 us
  blocking collectives  51 us (53%)
  starting transfers between devices  25.7 us (27%)
  Pallas kernels  14 us (15%)
  waiting for transfers between devices  4.51 us (5%)
    all_to_all x1, blocking collectives, body(): lax.all_to_all(partial.reshape(n_head, ROWS // n_head, -1), 'head', 0, 0)  24.1 us
    ppermute x1, starting transfers between devices, body(): other = lax.ppermute(queries, 'ctx', OTHER_HALF)  15.8 us
    ppermute x1, starting transfers between devices, body(): other = lax.ppermute(half, 'ctx', OTHER_HALF)  9.87 us
    all_to_all x1, blocking collectives, body(): lax.all_to_all(both, 'ctx', 0, 0, axis_index_groups=SAME_HALF)  9.74 us
    pallas_call x5, Pallas kernels, call(): pl.pallas_call(kernel, out_shape=out_shape, in_specs=[pl.BlockSpec(memory...  9.52 us
    all_to_all x1, blocking collectives, body(): lax.all_to_all(parts.reshape(n_half, own, WIDE), 'ctx', 0, 0, axis_index_...  8.77 us
    all_to_all x1, blocking collectives, body(): lax.all_to_all(value, 'ctx', 0, 0, axis_index_groups=SAME_HALF)  8.42 us
    ppermute x1, waiting for transfers between devices, body(): other = lax.ppermute(half, 'ctx', OTHER_HALF)  4.51 us
  transfers between devices with their start and end apart: 2, of which 1 were waited for; matrix products, arithmetic and copies ran while one was open for 0% of the time, Pallas kernels for 5%

profile of v8, /device:TPU:2, one launch (start us, length us, event | category | flops | bytes accessed | tf_op | source)
XLA Modules:
  0.0 96.2 jit_solution(11691823383010758288)
XLA Ops:
  0.0 0.0 copy-start.1
  0.0 0.0 copy-start
  0.0 15.8 %collective-permute-start = (bf16[8,768]{1,0:T(8,128)(2,1)}, bf16[8,768]{1,0:T(8,128)(2,1)S(1)}, u32[]{:S(2)}, u32[]{:S(2)}) collective-permute-start(bf16[8,768]{1,0:T(8,128)(2,1)} %q_hbm.1), channel_id=1, source_target_pairs={{0,64},{32,96},{64,0},{96,32},{128,192},{160,224},{192,128},{224,1... | collective-permute-start | bytes 36872 | tf_op jit(solution)/shard_map/ppermute | solution.py:297
  15.9 0.1 pad_add_fusion.shard_ref.place_ref
  16.0 4.5 %shard_map.64 = (bf16[4096,640]{1,0:T(8,128)(2,1)}, f32[128,128]{1,0:T(8,128)S(1)}, bf16[8,768]{1,0:T(8,128)(2,1)S(1)}) custom-call(bf16[64,36864]{1,0:T(8,128)(2,1)} %kv_hbm.1, s32[32,128]{1,0:T(8,128)} %bitcast.11, bf16[8,768]{1,0:T(8,128)(2,1)} %q_hbm.1, s32[2]{0:T(128)S(1)} %pad_add_fusion.shard_ref.place_ref), custom_call_target="tpu_custom_call" | custom-call | tf_op jit(solution)/shard_map/pallas_call | solution.py:121
  20.5 0.0 copy-start.2
  20.5 0.0 collective-permute-done.other_ref
  20.5 0.6 shard_map.65
  21.0 9.7 %all_to_all.20 = bf16[8,16,768]{2,1,0:T(8,128)(2,1)S(1)} all-to-all(bf16[8,16,768]{2,1,0:T(8,128)(2,1)S(1)} %shard_map.65), channel_id=1, replica_groups={{0,128,256,384,32,160,288,416},{64,192,320,448,96,224,352,480},{1,129,2..., dimensions={0} | all-to-all | bytes 393216 | tf_op jit(solution)/shard_map/all_to_all | solution.py:306
  30.8 0.0 copy-done.1
  30.8 0.0 copy-done
  30.8 8.0 %shard_map.66 = bf16[128,640]{1,0:T(8,128)(2,1)S(1)} custom-call(bf16[128,768]{1,0:T(8,128)(2,1)S(1)} %bitcast.7, bf16[4,128,512]{2,1,0:T(8,128)(2,1)S(1)} %copy-done, bf16[4,512,128]{2,1,0:T(8,128)(2,1)S(1)} %copy-done.1, f32[128,128]{1,0:T(8,128)S(1)} %get-tuple-element.13.bias_ref, bf16[4096,640]{1,0:T(8,128)(2,1)} %get-tuple-element.14.k_hbm), custom_call_target="tpu_custom_call" | custom-call | tf_op jit(solution)/shard_map/pallas_call | solution.py:280
  38.8 8.8 %all_to_all.21.in_ref = bf16[8,16,640]{2,1,0:T(8,128)(2,1)S(1)} all-to-all(bf16[8,16,640]{2,1,0:T(8,128)(2,1)S(1)} %bitcast.8), channel_id=1, replica_groups={{0,128,256,384,32,160,288,416},{64,192,320,448,96,224,352,480},{1,129,2..., dimensions={0} | all-to-all | bytes 327680 | tf_op jit(solution)/shard_map/all_to_all | solution.py:322
  47.6 0.4 shard_map.67.own_ref
  48.0 9.9 %collective-permute-start.1 = (bf16[16,640]{1,0:T(8,128)(2,1)S(1)}, bf16[16,640]{1,0:T(8,128)(2,1)S(1)}, u32[]{:S(2)}, u32[]{:S(2)}) collective-permute-start(bf16[16,640]{1,0:T(8,128)(2,1)S(1)} %shard_map.67.own_ref), channel_id=1, source_target_pairs={{0,64},{32,96},{64,0},{96,32},{128,192},{160,224},{192,128},{224,1... | collective-permute-start | bytes 61448 | tf_op jit(solution)/shard_map/ppermute | solution.py:326
  57.8 4.5 %collective-permute-done.1.other_ref = bf16[16,640]{1,0:T(8,128)(2,1)S(1)} collective-permute-done((bf16[16,640]{1,0:T(8,128)(2,1)S(1)}, bf16[16,640]{1,0:T(8,128)(2,1)S(1)}, u32[]{:S(2)}, u32[]{:S(2)}) %collective-permute-start.1) | collective-permute-done | bytes 20512 | tf_op jit(solution)/shard_map/ppermute | solution.py:326
  62.3 0.3 shard_map.68
  62.7 8.4 %all_to_all.22 = bf16[8,16,512]{2,1,0:T(8,128)(2,1)S(1)} all-to-all(bf16[8,16,512]{2,1,0:T(8,128)(2,1)S(1)} %shard_map.68), channel_id=1, replica_groups={{0,128,256,384,32,160,288,416},{64,192,320,448,96,224,352,480},{1,129,2..., dimensions={0} | all-to-all | bytes 262144 | tf_op jit(solution)/shard_map/all_to_all | solution.py:328
  71.1 0.0 copy-done.2
  71.1 0.3 shard_map.69
  71.4 24.1 %all_to_all.23 = bf16[32,4,448]{2,1,0:T(4,128)(2,1)S(1)} all-to-all(bf16[32,4,448]{2,1,0:T(4,128)(2,1)S(1)} %reshape.15), channel_id=1, replica_groups=mesh['ctx'=16,'head'=32] {'head'}, dimensions={0} | all-to-all | bytes 229376 | tf_op jit(solution)/shard_map/all_to_all | solution.py:331
  95.5 0.7 reduce_sum.12
  (1 shorter events, 0.0 us)
Async XLA Ops:
  0.0 30.8 %copy-start.1 = (bf16[4,512,128]{2,1,0:T(8,128)(2,1)S(1)}, bf16[4,512,128]{2,1,0:T(8,128)(2,1)}, u32[]{:S(2)}) copy-start(bf16[4,512,128]{2,1,0:T(8,128)(2,1)} %vue_ref.1) | copy-start | bytes 1572868
  0.0 30.8 %copy-start = (bf16[4,128,512]{2,1,0:T(8,128)(2,1)S(1)}, bf16[4,128,512]{2,1,0:T(8,128)(2,1)}, u32[]{:S(2)}) copy-start(bf16[4,128,512]{2,1,0:T(8,128)(2,1)} %w_ref.1) | copy-start | bytes 1572868
  0.0 20.5 %collective-permute-start = (bf16[8,768]{1,0:T(8,128)(2,1)}, bf16[8,768]{1,0:T(8,128)(2,1)S(1)}, u32[]{:S(2)}, u32[]{:S(2)}) collective-permute-start(bf16[8,768]{1,0:T(8,128)(2,1)} %q_hbm.1), channel_id=1, source_target_pairs={{0,64},{32,96},{64,0},{96,32},{128,192},{160,224},{192,128},{224,1... | collective-permute-start | bytes 36872 | tf_op jit(solution)/shard_map/ppermute | solution.py:297
  20.5 50.6 %copy-start.2 = (bf16[512,448]{0,1:T(8,128)(2,1)S(1)}, bf16[512,448]{0,1:T(8,128)(2,1)}, u32[]{:S(2)}) copy-start(bf16[512,448]{0,1:T(8,128)(2,1)} %param.9) | copy-start | bytes 1376260
  48.0 14.4 %collective-permute-start.1 = (bf16[16,640]{1,0:T(8,128)(2,1)S(1)}, bf16[16,640]{1,0:T(8,128)(2,1)S(1)}, u32[]{:S(2)}, u32[]{:S(2)}) collective-permute-start(bf16[16,640]{1,0:T(8,128)(2,1)S(1)} %shard_map.67.own_ref), channel_id=1, source_target_pairs={{0,64},{32,96},{64,0},{96,32},{128,192},{160,224},{192,128},{224,1... | collective-permute-start | bytes 61448 | tf_op jit(solution)/shard_map/ppermute | solution.py:326

commit v9 on v8

--- a/solution.py
+++ b/solution.py
@@ -18,7 +18,7 @@
 BLOCK = 64
 WIDE = 640
 PAIR = 1152
-PARTS = (0.125, 0.25, 0.3125, 0.3125)
+PARTS = (0.25, 0.25, 0.25, 0.25)
 CHUNK = 256
 STAGE_PAIRS = 4
 COEF = float((NOPE + ROPE) ** -0.5 * np.log2(np.e))
@@ -71,7 +71,8 @@
 
 
 def stage(
-    kv_hbm, blocks_hbm, q_hbm, shard_ref, out_hbm, bias_ref, q_ref, kv_ref, blocks_ref, keys_ref, sems, sent
+    kv_hbm, blocks_hbm, q_hbm, shard_ref, out_hbm, bias_ref, q_ref, head_ref, kv_ref, blocks_ref, keys_ref,
+    sems, sent,
 ):
     count, lanes = kv_ref.shape
     span = STAGE_PAIRS * PAIR
@@ -96,6 +97,8 @@
                 key = jnp.concatenate([pair[:, o * KEY : (o + 1) * KEY], pad], axis=1)
                 first = i * chunk + (2 * t + o) * count
                 keys_ref[first : first + count, :] = key
+                if first < head_ref.shape[0]:
+                    head_ref[first : first + count, :] = key
         at = pl.ds(i * chunk, chunk)
         put.append(pltpu.make_async_copy(keys_ref.at[at], out_hbm.at[at], sent.at[i]))
         put[-1].start()
@@ -124,6 +127,7 @@
             pltpu.HBM(keys, BF),
             jax.ShapeDtypeStruct((2 * kv.shape[0], ROWS), F32),
             jax.ShapeDtypeStruct(queries.shape, BF),
+            jax.ShapeDtypeStruct((int(PARTS[0] * keys[0]), WIDE), BF),
         ),
         in_specs=[
             pl.BlockSpec(memory_space=pltpu.HBM),
@@ -133,6 +137,7 @@
         ],
         out_specs=(
             pl.BlockSpec(memory_space=pltpu.HBM),
+            pl.BlockSpec(memory_space=pltpu.VMEM),
             pl.BlockSpec(memory_space=pltpu.VMEM),
             pl.BlockSpec(memory_space=pltpu.VMEM),
         ),
@@ -148,15 +153,15 @@
     )(in_hbm(kv), in_hbm(blocks), in_hbm(queries), shard)
 
 
-def attend(q_ref, w_ref, vue_ref, bias_ref, k_hbm, out_ref, qt, s_ref, p_ref, k_ref, sems):
+def attend(q_ref, w_ref, vue_ref, bias_ref, head_ref, k_hbm, out_ref, qt, s_ref, p_ref, k_ref, sems):
     width = qt.shape[1]
     rows = width // H_DEV
     bounds = [0]
     for share in PARTS:
         bounds.append(bounds[-1] + int(share * k_ref.shape[0]))
     spans = list(zip(bounds, bounds[1:]))
-    copies = []
-    for n, (a, b) in enumerate(spans):
+    copies = [None]
+    for n, (a, b) in enumerate(spans[1:]):
         span = pl.ds(a, b - a)
         copies.append(pltpu.make_async_copy(k_hbm.at[span], k_ref.at[span], sems.at[n]))
         copies[-1].start()
@@ -170,8 +175,11 @@
         qt[:KVR, own] = absorbed.astype(BF)
         qt[KVR:KEY, own] = q[:, NOPE:].T
 
+    def keys(a, b, lanes=WIDE):
+        return (head_ref if b <= head_ref.shape[0] else k_ref)[a:b, :lanes]
+
     def score(first, top):
-        s = dot(k_ref[first : first + CHUNK, :], qt[...])
+        s = dot(keys(first, first + CHUNK), qt[...])
         for at in range(0, CHUNK, 128):
             piece = s[at : at + 128, :] + jnp.concatenate([bias_ref[...]] * H_DEV, axis=1)
             top = jnp.maximum(top, jnp.max(piece.reshape(16, 8, width), axis=0))
@@ -187,7 +195,6 @@
 
     lowest = jnp.full((8, width), NEG, F32)
     tops, totals, accs = [], [], []
-    copies[0].wait()
     top = lowest
     for first in range(spans[0][0], spans[0][1], CHUNK):
         top = score(first, top)
@@ -208,7 +215,7 @@
         if n + 1 < len(spans):
             tops.append(jnp.max(top, axis=0, keepdims=True))
         totals.append(jnp.sum(total, axis=0, keepdims=True))
-        accs.append(tn_dot(p_ref[a:b, :], k_ref[a:b, :KVR]))
+        accs.append(tn_dot(p_ref[a:b, :], keys(a, b, KVR)))
     top = tops[0]
     for t in tops[1:]:
         top = jnp.maximum(top, t)
@@ -295,7 +302,7 @@
     shard = lax.axis_index("ctx")
     place = jnp.stack([shard, (shard // 2) % 2]).astype(jnp.int32)
     other = lax.ppermute(queries, "ctx", OTHER_HALF)
-    keys, bias, queries = staged(kv_cache, blocks.T, queries, place)
+    keys, bias, queries, head = staged(kv_cache, blocks.T, queries, place)
     other, bias = lax.optimization_barrier((other, bias))
     both = call(
         copies_of_both,
@@ -308,15 +315,15 @@
     parts = call(
         attend,
         jax.ShapeDtypeStruct((ROWS, WIDE), BF),
-        q, w_uk, value_up_weight, bias, in_hbm(keys),
+        q, w_uk, value_up_weight, bias, head, in_hbm(keys),
         scratch=[
             pltpu.VMEM((WIDE, width), BF),
             pltpu.VMEM((keys.shape[0], width), F32),
             pltpu.VMEM((keys.shape[0], width), BF),
             pltpu.VMEM(keys.shape, BF),
-            pltpu.SemaphoreType.DMA((len(PARTS),)),
+            pltpu.SemaphoreType.DMA((len(PARTS) - 1,)),
         ],
-        spaces=[pltpu.VMEM] * 4 + [pltpu.HBM],
+        spaces=[pltpu.VMEM] * 5 + [pltpu.HBM],
         limit=40,
     )
     parts = lax.all_to_all(

time: 96.5 us -> 95.8 us (level)
  no operation moved by 1% of the time
where the time goes in v9:
time: 95.8 us; the launch traced here: 95.5 us
  blocking collectives  51.2 us (53%)
  starting transfers between devices  25.8 us (27%)
  Pallas kernels  13.1 us (14%)
  waiting for transfers between devices  4.47 us (5%)
    all_to_all x1, blocking collectives, body(): lax.all_to_all(partial.reshape(n_head, ROWS // n_head, -1), 'head', 0, 0)  24.1 us
    ppermute x1, starting transfers between devices, body(): other = lax.ppermute(queries, 'ctx', OTHER_HALF)  15.8 us
    ppermute x1, starting transfers between devices, body(): other = lax.ppermute(half, 'ctx', OTHER_HALF)  9.91 us
    all_to_all x1, blocking collectives, body(): lax.all_to_all(both, 'ctx', 0, 0, axis_index_groups=SAME_HALF)  9.87 us
    all_to_all x1, blocking collectives, body(): lax.all_to_all(parts.reshape(n_half, own, WIDE), 'ctx', 0, 0, axis_index_...  8.77 us
    pallas_call x5, Pallas kernels, call(): pl.pallas_call(kernel, out_shape=out_shape, in_specs=[pl.BlockSpec(memory...  8.67 us
    all_to_all x1, blocking collectives, body(): lax.all_to_all(value, 'ctx', 0, 0, axis_index_groups=SAME_HALF)  8.42 us
    ppermute x1, waiting for transfers between devices, body(): other = lax.ppermute(half, 'ctx', OTHER_HALF)  4.47 us
  transfers between devices with their start and end apart: 2, of which 1 were waited for; matrix products, arithmetic and copies ran while one was open for 0% of the time, Pallas kernels for 5%

profile of v9, /device:TPU:2, one launch (start us, length us, event | category | flops | bytes accessed | tf_op | source)
XLA Modules:
  0.0 95.5 jit_solution(9861745177491493695)
XLA Ops:
  0.0 0.0 copy-start.1
  0.0 0.0 copy-start
  0.0 15.8 %collective-permute-start = (bf16[8,768]{1,0:T(8,128)(2,1)}, bf16[8,768]{1,0:T(8,128)(2,1)S(1)}, u32[]{:S(2)}, u32[]{:S(2)}) collective-permute-start(bf16[8,768]{1,0:T(8,128)(2,1)} %q_hbm.1), channel_id=1, source_target_pairs={{0,64},{32,96},{64,0},{96,32},{128,192},{160,224},{192,128},{224,1... | collective-permute-start | bytes 36872 | tf_op jit(solution)/shard_map/ppermute | solution.py:304
  15.9 0.1 pad_add_fusion.shard_ref.place_ref
  16.0 4.5 %shard_map.64 = (bf16[4096,640]{1,0:T(8,128)(2,1)}, f32[128,128]{1,0:T(8,128)S(1)}, bf16[8,768]{1,0:T(8,128)(2,1)S(1)}, bf16[1024,640]{1,0:T(8,128)(2,1)S(1)}) custom-call(bf16[64,36864]{1,0:T(8,128)(2,1)} %kv_hbm.1, s32[32,128]{1,0:T(8,128)} %bitcast.11, bf16[8,768]{1,0:T(8,128)(2,1)} %q_hbm.1, s32[2]{0:T(128)S(1)} %pad_add_fusion.shard_ref.place_ref), custom_call_target="tpu_custom_call" | custom-call | tf_op jit(solution)/shard_map/pallas_call | solution.py:124
  20.4 0.0 collective-permute-done.other_ref
  20.4 0.6 shard_map.65
  21.0 0.0 copy-start.2
  21.0 9.9 %all_to_all.20 = bf16[8,16,768]{2,1,0:T(8,128)(2,1)S(1)} all-to-all(bf16[8,16,768]{2,1,0:T(8,128)(2,1)S(1)} %shard_map.65), channel_id=1, replica_groups={{0,128,256,384,32,160,288,416},{64,192,320,448,96,224,352,480},{1,129,2..., dimensions={0} | all-to-all | bytes 393216 | tf_op jit(solution)/shard_map/all_to_all | solution.py:313
  30.9 0.0 copy-done.1
  30.9 0.0 copy-done
  30.9 7.2 %shard_map.66 = bf16[128,640]{1,0:T(8,128)(2,1)S(1)} custom-call(bf16[128,768]{1,0:T(8,128)(2,1)S(1)} %bitcast.7, bf16[4,128,512]{2,1,0:T(8,128)(2,1)S(1)} %copy-done, bf16[4,512,128]{2,1,0:T(8,128)(2,1)S(1)} %copy-done.1, f32[128,128]{1,0:T(8,128)S(1)} %get-tuple-element.14.bias_ref, bf16[1024,640]{1,0:T(8,128)(2,1)S(1)} %get-tuple-element.15.head_ref, ...), custom_call_target="tpu_custom_call" | custom-call | tf_op jit(solution)/shard_map/pallas_call | solution.py:287
  38.1 8.8 %all_to_all.21.in_ref = bf16[8,16,640]{2,1,0:T(8,128)(2,1)S(1)} all-to-all(bf16[8,16,640]{2,1,0:T(8,128)(2,1)S(1)} %bitcast.8), channel_id=1, replica_groups={{0,128,256,384,32,160,288,416},{64,192,320,448,96,224,352,480},{1,129,2..., dimensions={0} | all-to-all | bytes 327680 | tf_op jit(solution)/shard_map/all_to_all | solution.py:329
  46.8 0.4 shard_map.67.own_ref
  47.2 9.9 %collective-permute-start.1 = (bf16[16,640]{1,0:T(8,128)(2,1)S(1)}, bf16[16,640]{1,0:T(8,128)(2,1)S(1)}, u32[]{:S(2)}, u32[]{:S(2)}) collective-permute-start(bf16[16,640]{1,0:T(8,128)(2,1)S(1)} %shard_map.67.own_ref), channel_id=1, source_target_pairs={{0,64},{32,96},{64,0},{96,32},{128,192},{160,224},{192,128},{224,1... | collective-permute-start | bytes 61448 | tf_op jit(solution)/shard_map/ppermute | solution.py:333
  57.1 4.5 %collective-permute-done.1.other_ref = bf16[16,640]{1,0:T(8,128)(2,1)S(1)} collective-permute-done((bf16[16,640]{1,0:T(8,128)(2,1)S(1)}, bf16[16,640]{1,0:T(8,128)(2,1)S(1)}, u32[]{:S(2)}, u32[]{:S(2)}) %collective-permute-start.1) | collective-permute-done | bytes 20512 | tf_op jit(solution)/shard_map/ppermute | solution.py:333
  61.6 0.3 shard_map.68
  61.9 8.4 %all_to_all.22 = bf16[8,16,512]{2,1,0:T(8,128)(2,1)S(1)} all-to-all(bf16[8,16,512]{2,1,0:T(8,128)(2,1)S(1)} %shard_map.68), channel_id=1, replica_groups={{0,128,256,384,32,160,288,416},{64,192,320,448,96,224,352,480},{1,129,2..., dimensions={0} | all-to-all | bytes 262144 | tf_op jit(solution)/shard_map/all_to_all | solution.py:335
  70.3 0.0 copy-done.2
  70.3 0.3 shard_map.69
  70.7 24.1 %all_to_all.23 = bf16[32,4,448]{2,1,0:T(4,128)(2,1)S(1)} all-to-all(bf16[32,4,448]{2,1,0:T(4,128)(2,1)S(1)} %reshape.15), channel_id=1, replica_groups=mesh['ctx'=16,'head'=32] {'head'}, dimensions={0} | all-to-all | bytes 229376 | tf_op jit(solution)/shard_map/all_to_all | solution.py:338
  94.8 0.7 reduce_sum.12
  (1 shorter events, 0.0 us)
Async XLA Ops:
  0.0 30.9 %copy-start.1 = (bf16[4,512,128]{2,1,0:T(8,128)(2,1)S(1)}, bf16[4,512,128]{2,1,0:T(8,128)(2,1)}, u32[]{:S(2)}) copy-start(bf16[4,512,128]{2,1,0:T(8,128)(2,1)} %vue_ref.1) | copy-start | bytes 1572868
  0.0 30.9 %copy-start = (bf16[4,128,512]{2,1,0:T(8,128)(2,1)S(1)}, bf16[4,128,512]{2,1,0:T(8,128)(2,1)}, u32[]{:S(2)}) copy-start(bf16[4,128,512]{2,1,0:T(8,128)(2,1)} %w_ref.1) | copy-start | bytes 1572868
  0.0 20.4 %collective-permute-start = (bf16[8,768]{1,0:T(8,128)(2,1)}, bf16[8,768]{1,0:T(8,128)(2,1)S(1)}, u32[]{:S(2)}, u32[]{:S(2)}) collective-permute-start(bf16[8,768]{1,0:T(8,128)(2,1)} %q_hbm.1), channel_id=1, source_target_pairs={{0,64},{32,96},{64,0},{96,32},{128,192},{160,224},{192,128},{224,1... | collective-permute-start | bytes 36872 | tf_op jit(solution)/shard_map/ppermute | solution.py:304
  21.0 49.3 %copy-start.2 = (bf16[512,448]{0,1:T(8,128)(2,1)S(1)}, bf16[512,448]{0,1:T(8,128)(2,1)}, u32[]{:S(2)}) copy-start(bf16[512,448]{0,1:T(8,128)(2,1)} %param.9) | copy-start | bytes 1376260
  47.2 14.4 %collective-permute-start.1 = (bf16[16,640]{1,0:T(8,128)(2,1)S(1)}, bf16[16,640]{1,0:T(8,128)(2,1)S(1)}, u32[]{:S(2)}, u32[]{:S(2)}) collective-permute-start(bf16[16,640]{1,0:T(8,128)(2,1)S(1)} %shard_map.67.own_ref), channel_id=1, source_target_pairs={{0,64},{32,96},{64,0},{96,32},{128,192},{160,224},{192,128},{224,1... | collective-permute-start | bytes 61448 | tf_op jit(solution)/shard_map/ppermute | solution.py:333

commit v10 on v9

--- a/solution.py
+++ b/solution.py
@@ -18,7 +18,7 @@
 BLOCK = 64
 WIDE = 640
 PAIR = 1152
-PARTS = (0.25, 0.25, 0.25, 0.25)
+PARTS = (0.375, 0.3125, 0.3125)
 CHUNK = 256
 STAGE_PAIRS = 4
 COEF = float((NOPE + ROPE) ** -0.5 * np.log2(np.e))

time: 95.8 us -> 95.2 us (level)
  no operation moved by 1% of the time
where the time goes in v10:
time: 95.2 us; the launch traced here: 94.9 us
  blocking collectives  51 us (54%)
  starting transfers between devices  25.8 us (27%)
  Pallas kernels  12.7 us (13%)
  waiting for transfers between devices  4.47 us (5%)
    all_to_all x1, blocking collectives, body(): lax.all_to_all(partial.reshape(n_head, ROWS // n_head, -1), 'head', 0, 0)  24.1 us
    ppermute x1, starting transfers between devices, body(): other = lax.ppermute(queries, 'ctx', OTHER_HALF)  15.8 us
    ppermute x1, starting transfers between devices, body(): other = lax.ppermute(half, 'ctx', OTHER_HALF)  9.92 us
    all_to_all x1, blocking collectives, body(): lax.all_to_all(both, 'ctx', 0, 0, axis_index_groups=SAME_HALF)  9.74 us
    all_to_all x1, blocking collectives, body(): lax.all_to_all(parts.reshape(n_half, own, WIDE), 'ctx', 0, 0, axis_index_...  8.77 us
    all_to_all x1, blocking collectives, body(): lax.all_to_all(value, 'ctx', 0, 0, axis_index_groups=SAME_HALF)  8.42 us
    pallas_call x5, Pallas kernels, call(): pl.pallas_call(kernel, out_shape=out_shape, in_specs=[pl.BlockSpec(memory...  8.25 us
    ppermute x1, waiting for transfers between devices, body(): other = lax.ppermute(half, 'ctx', OTHER_HALF)  4.47 us
  transfers between devices with their start and end apart: 2, of which 1 were waited for; matrix products, arithmetic and copies ran while one was open for 0% of the time, Pallas kernels for 5%

profile of v10, /device:TPU:2, one launch (start us, length us, event | category | flops | bytes accessed | tf_op | source)
XLA Modules:
  0.0 94.9 jit_solution(12540306376733669654)
XLA Ops:
  0.0 0.0 copy-start.1
  0.0 0.0 copy-start
  0.0 15.8 %collective-permute-start = (bf16[8,768]{1,0:T(8,128)(2,1)}, bf16[8,768]{1,0:T(8,128)(2,1)S(1)}, u32[]{:S(2)}, u32[]{:S(2)}) collective-permute-start(bf16[8,768]{1,0:T(8,128)(2,1)} %q_hbm.1), channel_id=1, source_target_pairs={{0,64},{32,96},{64,0},{96,32},{128,192},{160,224},{192,128},{224,1... | collective-permute-start | bytes 36872 | tf_op jit(solution)/shard_map/ppermute | solution.py:304
  15.9 0.1 pad_add_fusion.shard_ref.place_ref
  16.0 4.5 %shard_map.64 = (bf16[4096,640]{1,0:T(8,128)(2,1)}, f32[128,128]{1,0:T(8,128)S(1)}, bf16[8,768]{1,0:T(8,128)(2,1)S(1)}, bf16[1536,640]{1,0:T(8,128)(2,1)S(1)}) custom-call(bf16[64,36864]{1,0:T(8,128)(2,1)} %kv_hbm.1, s32[32,128]{1,0:T(8,128)} %bitcast.11, bf16[8,768]{1,0:T(8,128)(2,1)} %q_hbm.1, s32[2]{0:T(128)S(1)} %pad_add_fusion.shard_ref.place_ref), custom_call_target="tpu_custom_call" | custom-call | tf_op jit(solution)/shard_map/pallas_call | solution.py:124
  20.4 0.0 collective-permute-done.other_ref
  20.4 0.6 shard_map.65
  21.0 9.7 %all_to_all.20 = bf16[8,16,768]{2,1,0:T(8,128)(2,1)S(1)} all-to-all(bf16[8,16,768]{2,1,0:T(8,128)(2,1)S(1)} %shard_map.65), channel_id=1, replica_groups={{0,128,256,384,32,160,288,416},{64,192,320,448,96,224,352,480},{1,129,2..., dimensions={0} | all-to-all | bytes 393216 | tf_op jit(solution)/shard_map/all_to_all | solution.py:313
  30.8 0.0 copy-done.1
  30.8 0.0 copy-done
  30.8 0.0 copy-start.2
  30.8 6.7 %shard_map.66 = bf16[128,640]{1,0:T(8,128)(2,1)S(1)} custom-call(bf16[128,768]{1,0:T(8,128)(2,1)S(1)} %bitcast.7, bf16[4,128,512]{2,1,0:T(8,128)(2,1)S(1)} %copy-done, bf16[4,512,128]{2,1,0:T(8,128)(2,1)S(1)} %copy-done.1, f32[128,128]{1,0:T(8,128)S(1)} %get-tuple-element.14.bias_ref, bf16[1536,640]{1,0:T(8,128)(2,1)S(1)} %get-tuple-element.15.head_ref, ...), custom_call_target="tpu_custom_call" | custom-call | tf_op jit(solution)/shard_map/pallas_call | solution.py:287
  37.5 8.8 %all_to_all.21.in_ref = bf16[8,16,640]{2,1,0:T(8,128)(2,1)S(1)} all-to-all(bf16[8,16,640]{2,1,0:T(8,128)(2,1)S(1)} %bitcast.8), channel_id=1, replica_groups={{0,128,256,384,32,160,288,416},{64,192,320,448,96,224,352,480},{1,129,2..., dimensions={0} | all-to-all | bytes 327680 | tf_op jit(solution)/shard_map/all_to_all | solution.py:329
  46.3 0.4 shard_map.67.own_ref
  46.6 9.9 %collective-permute-start.1 = (bf16[16,640]{1,0:T(8,128)(2,1)S(1)}, bf16[16,640]{1,0:T(8,128)(2,1)S(1)}, u32[]{:S(2)}, u32[]{:S(2)}) collective-permute-start(bf16[16,640]{1,0:T(8,128)(2,1)S(1)} %shard_map.67.own_ref), channel_id=1, source_target_pairs={{0,64},{32,96},{64,0},{96,32},{128,192},{160,224},{192,128},{224,1... | collective-permute-start | bytes 61448 | tf_op jit(solution)/shard_map/ppermute | solution.py:333
  56.6 4.5 %collective-permute-done.1.other_ref = bf16[16,640]{1,0:T(8,128)(2,1)S(1)} collective-permute-done((bf16[16,640]{1,0:T(8,128)(2,1)S(1)}, bf16[16,640]{1,0:T(8,128)(2,1)S(1)}, u32[]{:S(2)}, u32[]{:S(2)}) %collective-permute-start.1) | collective-permute-done | bytes 20512 | tf_op jit(solution)/shard_map/ppermute | solution.py:333
  61.0 0.3 shard_map.68
  61.4 8.4 %all_to_all.22 = bf16[8,16,512]{2,1,0:T(8,128)(2,1)S(1)} all-to-all(bf16[8,16,512]{2,1,0:T(8,128)(2,1)S(1)} %shard_map.68), channel_id=1, replica_groups={{0,128,256,384,32,160,288,416},{64,192,320,448,96,224,352,480},{1,129,2..., dimensions={0} | all-to-all | bytes 262144 | tf_op jit(solution)/shard_map/all_to_all | solution.py:335
  69.8 0.0 copy-done.2
  69.8 0.3 shard_map.69
  70.1 24.1 %all_to_all.23 = bf16[32,4,448]{2,1,0:T(4,128)(2,1)S(1)} all-to-all(bf16[32,4,448]{2,1,0:T(4,128)(2,1)S(1)} %reshape.15), channel_id=1, replica_groups=mesh['ctx'=16,'head'=32] {'head'}, dimensions={0} | all-to-all | bytes 229376 | tf_op jit(solution)/shard_map/all_to_all | solution.py:338
  94.2 0.7 reduce_sum.12
  (1 shorter events, 0.0 us)
Async XLA Ops:
  0.0 30.8 %copy-start.1 = (bf16[4,512,128]{2,1,0:T(8,128)(2,1)S(1)}, bf16[4,512,128]{2,1,0:T(8,128)(2,1)}, u32[]{:S(2)}) copy-start(bf16[4,512,128]{2,1,0:T(8,128)(2,1)} %vue_ref.1) | copy-start | bytes 1572868
  0.0 30.8 %copy-start = (bf16[4,128,512]{2,1,0:T(8,128)(2,1)S(1)}, bf16[4,128,512]{2,1,0:T(8,128)(2,1)}, u32[]{:S(2)}) copy-start(bf16[4,128,512]{2,1,0:T(8,128)(2,1)} %w_ref.1) | copy-start | bytes 1572868
  0.0 20.4 %collective-permute-start = (bf16[8,768]{1,0:T(8,128)(2,1)}, bf16[8,768]{1,0:T(8,128)(2,1)S(1)}, u32[]{:S(2)}, u32[]{:S(2)}) collective-permute-start(bf16[8,768]{1,0:T(8,128)(2,1)} %q_hbm.1), channel_id=1, source_target_pairs={{0,64},{32,96},{64,0},{96,32},{128,192},{160,224},{192,128},{224,1... | collective-permute-start | bytes 36872 | tf_op jit(solution)/shard_map/ppermute | solution.py:304
  30.8 39.0 %copy-start.2 = (bf16[512,448]{0,1:T(8,128)(2,1)S(1)}, bf16[512,448]{0,1:T(8,128)(2,1)}, u32[]{:S(2)}) copy-start(bf16[512,448]{0,1:T(8,128)(2,1)} %param.9) | copy-start | bytes 1376260
  46.6 14.4 %collective-permute-start.1 = (bf16[16,640]{1,0:T(8,128)(2,1)S(1)}, bf16[16,640]{1,0:T(8,128)(2,1)S(1)}, u32[]{:S(2)}, u32[]{:S(2)}) collective-permute-start(bf16[16,640]{1,0:T(8,128)(2,1)S(1)} %shard_map.67.own_ref), channel_id=1, source_target_pairs={{0,64},{32,96},{64,0},{96,32},{128,192},{160,224},{192,128},{224,1... | collective-permute-start | bytes 61448 | tf_op jit(solution)/shard_map/ppermute | solution.py:333

commit v11 on v10

--- a/solution.py
+++ b/solution.py
@@ -18,7 +18,7 @@
 BLOCK = 64
 WIDE = 640
 PAIR = 1152
-PARTS = (0.375, 0.3125, 0.3125)
+PARTS = (0.5, 0.25, 0.25)
 CHUNK = 256
 STAGE_PAIRS = 4
 COEF = float((NOPE + ROPE) ** -0.5 * np.log2(np.e))

time: 95.2 us -> 95.5 us (level)
  no operation moved by 1% of the time
where the time goes in v11:
time: 95.5 us; the launch traced here: 95.2 us
  blocking collectives  51 us (53%)
  starting transfers between devices  25.8 us (27%)
  Pallas kernels  13 us (14%)
  waiting for transfers between devices  4.47 us (5%)
    all_to_all x1, blocking collectives, body(): lax.all_to_all(partial.reshape(n_head, ROWS // n_head, -1), 'head', 0, 0)  24.1 us
    ppermute x1, starting transfers between devices, body(): other = lax.ppermute(queries, 'ctx', OTHER_HALF)  15.8 us
    ppermute x1, starting transfers between devices, body(): other = lax.ppermute(half, 'ctx', OTHER_HALF)  9.91 us
    all_to_all x1, blocking collectives, body(): lax.all_to_all(both, 'ctx', 0, 0, axis_index_groups=SAME_HALF)  9.74 us
    all_to_all x1, blocking collectives, body(): lax.all_to_all(parts.reshape(n_half, own, WIDE), 'ctx', 0, 0, axis_index_...  8.77 us
    pallas_call x5, Pallas kernels, call(): pl.pallas_call(kernel, out_shape=out_shape, in_specs=[pl.BlockSpec(memory...  8.51 us
    all_to_all x1, blocking collectives, body(): lax.all_to_all(value, 'ctx', 0, 0, axis_index_groups=SAME_HALF)  8.42 us
    ppermute x1, waiting for transfers between devices, body(): other = lax.ppermute(half, 'ctx', OTHER_HALF)  4.47 us
  transfers between devices with their start and end apart: 2, of which 1 were waited for; matrix products, arithmetic and copies ran while one was open for 0% of the time, Pallas kernels for 5%

profile of v11, /device:TPU:2, one launch (start us, length us, event | category | flops | bytes accessed | tf_op | source)
XLA Modules:
  0.0 95.2 jit_solution(15483536612040862805)
XLA Ops:
  0.0 0.0 copy-start.1
  0.0 0.0 copy-start
  0.0 15.8 %collective-permute-start = (bf16[8,768]{1,0:T(8,128)(2,1)}, bf16[8,768]{1,0:T(8,128)(2,1)S(1)}, u32[]{:S(2)}, u32[]{:S(2)}) collective-permute-start(bf16[8,768]{1,0:T(8,128)(2,1)} %q_hbm.1), channel_id=1, source_target_pairs={{0,64},{32,96},{64,0},{96,32},{128,192},{160,224},{192,128},{224,1... | collective-permute-start | bytes 36872 | tf_op jit(solution)/shard_map/ppermute | solution.py:304
  15.9 0.1 pad_add_fusion.shard_ref.place_ref
  16.0 4.5 %shard_map.64 = (bf16[4096,640]{1,0:T(8,128)(2,1)}, f32[128,128]{1,0:T(8,128)S(1)}, bf16[8,768]{1,0:T(8,128)(2,1)S(1)}, bf16[2048,640]{1,0:T(8,128)(2,1)S(1)}) custom-call(bf16[64,36864]{1,0:T(8,128)(2,1)} %kv_hbm.1, s32[32,128]{1,0:T(8,128)} %bitcast.11, bf16[8,768]{1,0:T(8,128)(2,1)} %q_hbm.1, s32[2]{0:T(128)S(1)} %pad_add_fusion.shard_ref.place_ref), custom_call_target="tpu_custom_call" | custom-call | tf_op jit(solution)/shard_map/pallas_call | solution.py:124
  20.4 0.0 collective-permute-done.other_ref
  20.4 0.6 shard_map.65
  21.0 9.7 %all_to_all.20 = bf16[8,16,768]{2,1,0:T(8,128)(2,1)S(1)} all-to-all(bf16[8,16,768]{2,1,0:T(8,128)(2,1)S(1)} %shard_map.65), channel_id=1, replica_groups={{0,128,256,384,32,160,288,416},{64,192,320,448,96,224,352,480},{1,129,2..., dimensions={0} | all-to-all | bytes 393216 | tf_op jit(solution)/shard_map/all_to_all | solution.py:313
  30.8 0.0 copy-done.1
  30.8 0.0 copy-done
  30.8 0.0 copy-start.2
  30.8 7.0 %shard_map.66 = bf16[128,640]{1,0:T(8,128)(2,1)S(1)} custom-call(bf16[128,768]{1,0:T(8,128)(2,1)S(1)} %bitcast.7, bf16[4,128,512]{2,1,0:T(8,128)(2,1)S(1)} %copy-done, bf16[4,512,128]{2,1,0:T(8,128)(2,1)S(1)} %copy-done.1, f32[128,128]{1,0:T(8,128)S(1)} %get-tuple-element.14.bias_ref, bf16[2048,640]{1,0:T(8,128)(2,1)S(1)} %get-tuple-element.15.head_ref, ...), custom_call_target="tpu_custom_call" | custom-call | tf_op jit(solution)/shard_map/pallas_call | solution.py:287
  37.8 8.8 %all_to_all.21.in_ref = bf16[8,16,640]{2,1,0:T(8,128)(2,1)S(1)} all-to-all(bf16[8,16,640]{2,1,0:T(8,128)(2,1)S(1)} %bitcast.8), channel_id=1, replica_groups={{0,128,256,384,32,160,288,416},{64,192,320,448,96,224,352,480},{1,129,2..., dimensions={0} | all-to-all | bytes 327680 | tf_op jit(solution)/shard_map/all_to_all | solution.py:329
  46.5 0.4 shard_map.67.own_ref
  46.9 9.9 %collective-permute-start.1 = (bf16[16,640]{1,0:T(8,128)(2,1)S(1)}, bf16[16,640]{1,0:T(8,128)(2,1)S(1)}, u32[]{:S(2)}, u32[]{:S(2)}) collective-permute-start(bf16[16,640]{1,0:T(8,128)(2,1)S(1)} %shard_map.67.own_ref), channel_id=1, source_target_pairs={{0,64},{32,96},{64,0},{96,32},{128,192},{160,224},{192,128},{224,1... | collective-permute-start | bytes 61448 | tf_op jit(solution)/shard_map/ppermute | solution.py:333
  56.8 4.5 %collective-permute-done.1.other_ref = bf16[16,640]{1,0:T(8,128)(2,1)S(1)} collective-permute-done((bf16[16,640]{1,0:T(8,128)(2,1)S(1)}, bf16[16,640]{1,0:T(8,128)(2,1)S(1)}, u32[]{:S(2)}, u32[]{:S(2)}) %collective-permute-start.1) | collective-permute-done | bytes 20512 | tf_op jit(solution)/shard_map/ppermute | solution.py:333
  61.3 0.3 shard_map.68
  61.6 8.4 %all_to_all.22 = bf16[8,16,512]{2,1,0:T(8,128)(2,1)S(1)} all-to-all(bf16[8,16,512]{2,1,0:T(8,128)(2,1)S(1)} %shard_map.68), channel_id=1, replica_groups={{0,128,256,384,32,160,288,416},{64,192,320,448,96,224,352,480},{1,129,2..., dimensions={0} | all-to-all | bytes 262144 | tf_op jit(solution)/shard_map/all_to_all | solution.py:335
  70.0 0.0 copy-done.2
  70.0 0.3 shard_map.69
  70.4 24.1 %all_to_all.23 = bf16[32,4,448]{2,1,0:T(4,128)(2,1)S(1)} all-to-all(bf16[32,4,448]{2,1,0:T(4,128)(2,1)S(1)} %reshape.15), channel_id=1, replica_groups=mesh['ctx'=16,'head'=32] {'head'}, dimensions={0} | all-to-all | bytes 229376 | tf_op jit(solution)/shard_map/all_to_all | solution.py:338
  94.5 0.7 reduce_sum.12
  (1 shorter events, 0.0 us)
Async XLA Ops:
  0.0 30.8 %copy-start.1 = (bf16[4,512,128]{2,1,0:T(8,128)(2,1)S(1)}, bf16[4,512,128]{2,1,0:T(8,128)(2,1)}, u32[]{:S(2)}) copy-start(bf16[4,512,128]{2,1,0:T(8,128)(2,1)} %vue_ref.1) | copy-start | bytes 1572868
  0.0 30.8 %copy-start = (bf16[4,128,512]{2,1,0:T(8,128)(2,1)S(1)}, bf16[4,128,512]{2,1,0:T(8,128)(2,1)}, u32[]{:S(2)}) copy-start(bf16[4,128,512]{2,1,0:T(8,128)(2,1)} %w_ref.1) | copy-start | bytes 1572868
  0.0 20.4 %collective-permute-start = (bf16[8,768]{1,0:T(8,128)(2,1)}, bf16[8,768]{1,0:T(8,128)(2,1)S(1)}, u32[]{:S(2)}, u32[]{:S(2)}) collective-permute-start(bf16[8,768]{1,0:T(8,128)(2,1)} %q_hbm.1), channel_id=1, source_target_pairs={{0,64},{32,96},{64,0},{96,32},{128,192},{160,224},{192,128},{224,1... | collective-permute-start | bytes 36872 | tf_op jit(solution)/shard_map/ppermute | solution.py:304
  30.8 39.3 %copy-start.2 = (bf16[512,448]{0,1:T(8,128)(2,1)S(1)}, bf16[512,448]{0,1:T(8,128)(2,1)}, u32[]{:S(2)}) copy-start(bf16[512,448]{0,1:T(8,128)(2,1)} %param.9) | copy-start | bytes 1376260
  46.9 14.4 %collective-permute-start.1 = (bf16[16,640]{1,0:T(8,128)(2,1)S(1)}, bf16[16,640]{1,0:T(8,128)(2,1)S(1)}, u32[]{:S(2)}, u32[]{:S(2)}) collective-permute-start(bf16[16,640]{1,0:T(8,128)(2,1)S(1)} %shard_map.67.own_ref), channel_id=1, source_target_pairs={{0,64},{32,96},{64,0},{96,32},{128,192},{160,224},{192,128},{224,1... | collective-permute-start | bytes 61448 | tf_op jit(solution)/shard_map/ppermute | solution.py:333
